TPU v7x, 512 devices: a whole 4x8x8 slice. The times are simulated.
512 devices in a mesh: layer: 8 (over x, y_lo), latent: 64 (over z, y_hi, core).
Axes of the slice: x: 4, y: 8 (y_hi: 4, y_lo: 2; y = y_hi * 2 + y_lo), z: 8, core: 2. Of those that a mesh axis runs over, the one named last changes fastest.
Arguments:
- residual: bfloat16 [512, 4608], P('latent', 'layer'), may hold values from -6 to 6
- w_enc: bfloat16 [4608, 65536], P('layer', 'latent'), may hold values from -0.09375 to 0.09375
- b_enc: float32 [65536], P('latent'), may hold values from -1 to 0.5
- w_dec: bfloat16 [65536, 4608], P('latent', 'layer'), may hold values from -0.0234375 to 0.0234375
- b_dec: float32 [4608], P('layer'), may hold values from -3 to 3
Outputs:
- grad_enc: bfloat16 [4608, 65536], P('layer', 'latent')
- grad_benc: bfloat16 [65536], P('latent')
- grad_dec: bfloat16 [65536, 4608], P('latent', 'layer')
- grad_bdec: bfloat16 [4608], P('layer')
- loss: float32 [], replicated
All inputs are finite; a program needn't handle non-finite values.
Results may differ from a plain program's by a relative error of at most 0.02.
Values may be sent and summed in bfloat16 or wider, within the bound.
No kernel may reach another device: no remote copies, remote signals or barrier semaphores. Data moves between devices by JAX's collectives and lax.ppermute only.
A program may use at most 64 MiB of HBM per device.

v0:
```python
import jax
import jax.numpy as jnp
from jax import lax
from jax.sharding import PartitionSpec as P

D = 4608


penalty_weight = 0.5


def local(residual, w_enc, b_enc, w_dec, b_dec):
    rows_all = lax.all_gather(residual, "latent", axis=0, tiled=True)
    wide = w_dec.astype(jnp.float32)
    squares = jnp.sum(wide * wide, axis=1)
    partial_value = jnp.dot(rows_all, w_enc, preferred_element_type=jnp.float32)
    pre_sum, square_sum = lax.psum((partial_value, squares), "layer")
    acts = jnp.maximum(pre_sum + b_enc, 0.0).astype(jnp.bfloat16)
    norms = jnp.sqrt(square_sum + 1e-06)
    acts_wide = acts.astype(jnp.float32)
    penalty_part = penalty_weight * jnp.sum(acts_wide * norms[None, :])
    first_layer = (lax.axis_index("layer") == 0).astype(jnp.float32)
    recon_part = jnp.dot(acts, w_dec, preferred_element_type=jnp.float32)
    recon = lax.psum(recon_part, "latent") + b_dec
    err = recon - rows_all.astype(jnp.float32)
    d_recon = (err / 8.0).astype(jnp.bfloat16)
    grad_bdec = jnp.sum(d_recon.astype(jnp.float32), axis=0).astype(jnp.bfloat16)
    first_latent = (lax.axis_index("latent") == 0).astype(jnp.float32)
    total = lax.psum(
        jnp.sum(err * err) * first_latent + penalty_part * first_layer, ("layer", "latent")
    )
    loss = total / (rows_all.shape[0] * D)
    col_sum = jnp.sum(acts_wide, axis=0)
    outer = lax.dot_general(
        acts, d_recon, (((0,), (0,)), ((), ())), preferred_element_type=jnp.float32
    )
    grad_dec = (outer + penalty_weight / 16.0 * col_sum[:, None] * wide / norms[:, None]).astype(
        jnp.bfloat16
    )
    act_part = lax.dot_general(
        d_recon, w_dec, (((1,), (1,)), ((), ())), preferred_element_type=jnp.float32
    )
    d_acts = lax.psum(act_part, "layer") + penalty_weight / 16.0 * norms[None, :]
    d_pre = jnp.where(acts > 0, d_acts, 0.0).astype(jnp.bfloat16)
    grad_enc = lax.dot_general(
        rows_all, d_pre, (((0,), (0,)), ((), ())), preferred_element_type=jnp.float32
    ).astype(jnp.bfloat16)
    grad_benc = jnp.sum(d_pre.astype(jnp.float32), axis=0).astype(jnp.bfloat16)
    return (grad_enc, grad_benc, grad_dec, grad_bdec, loss)


def solution(mesh):
    placed = (
        P("latent", "layer"),
        P("layer", "latent"),
        P("latent"),
        P("latent", "layer"),
        P("layer"),
    )
    return jax.shard_map(
        local,
        mesh=mesh,
        in_specs=placed,
        out_specs=(P("layer", "latent"), P("latent"), P("latent", "layer"), P("layer"), P()),
        check_vma=False,
    )
```

profile of v0, /device:TPU:1, one launch (start us, length us, event | category | flops | bytes accessed | tf_op | source)
XLA Modules:
  0.0 881.6 jit_solution(15861054209048879506)
XLA Ops:
  7.2 0.0 copy-start
  7.2 0.0 all-reduce.4.cloned.1.call-start
  7.2 92.3 %all_gather.3 = bf16[512,576]{1,0:T(8,128)(2,1)S(1)} all-gather(bf16[8,576]{1,0:T(8,128)(2,1)} %param.5), channel_id=1, replica_groups=mesh['layer'=8,'latent'=64] {'latent'}, dimensions={0}, use_global_device_ids=true | all-gather | bytes 599040 | tf_op jit(solution)/shard_map/all_gather | solution.py:13
  99.5 0.0 copy-done
  99.6 0.0 copy-start.4
  99.6 2.3 fusion.8
  101.8 0.0 copy-start.9
  101.8 0.0 all-reduce.4.cloned.1.call-update
  101.9 0.0 all-reduce.6.cloned.1.call-start
  101.9 1.5 fusion
  103.5 16.6 %psum.38 = f32[1024]{0:T(1024)S(1)} all-reduce(f32[1024]{0:T(1024)S(1)} %fusion), channel_id=1, replica_groups=mesh['layer'=8,'latent'=64] {'layer'}, use_global_device_ids=true, to_apply=%region_4.0 | all-reduce | flops 1024 | bytes 8192 | tf_op jit(solution)/shard_map/psum | solution.py:17
  120.1 87.5 %all-reduce.4.cloned.1.call-done = f32[512,1024]{1,0:T(8,128)} async-done(((f32[512,1024]{1,0:T(8,128)}), f32[512,1024]{1,0:T(8,128)}) %all-reduce.4.cloned.1.call-update) | async-done | bytes 2097168 | tf_op jit(solution)/shard_map/psum | solution.py:17
  207.6 0.0 copy-done.9
  207.6 0.0 copy-start.6
  207.6 2.8 fusion.4
  210.5 0.0 copy-start.2
  210.5 1.0 copy-done.2
  211.4 0.0 copy-done.6
  211.4 1.8 fusion.9
  213.3 0.0 copy-start.8
  213.3 0.0 all-reduce.6.cloned.1.call-update
  213.3 0.0 all-reduce.8.cloned.1.call-start
  213.3 0.0 copy-done.4
  213.3 0.2 copy.11
  213.6 0.0 copy-start.7
  213.6 537.4 %all-reduce.6.cloned.1.call-done = f32[512,576]{0,1:T(8,128)} async-done(((f32[512,576]{0,1:T(8,128)}), f32[512,576]{0,1:T(8,128)}) %all-reduce.6.cloned.1.call-update) | async-done | bytes 1179664 | tf_op jit(solution)/shard_map/psum | solution.py:24
  751.0 0.0 copy-done.8
  751.0 2.3 fusion.6
  753.2 0.0 copy-done.7
  753.2 2.3 fusion.10
  755.5 0.0 copy-start.1
  755.5 0.0 all-reduce.8.cloned.1.call-update
  756.3 0.5 copy-done.1
  756.8 1.0 multiply_reduce_fusion
  758.5 100.2 %psum.39 = f32[]{:T(128)} all-reduce(f32[]{:T(128)S(6)} %add.55), channel_id=1, replica_groups=mesh['layer'=8,'latent'=64] {'layer','latent'}, use_global_device_ids=true, to_apply=%region_10.11 | all-reduce | flops 1 | bytes 8 | tf_op jit(solution)/shard_map/psum | solution.py:29
  859.3 0.0 copy-start.3
  859.3 3.5 fusion.3
  862.8 6.6 all-reduce.8.cloned.1.call-done
  869.4 0.0 copy-done.3
  869.4 0.0 copy-start.5
  869.4 2.7 fusion.7
  872.1 0.0 copy-done.5
  872.1 1.8 fusion.5
  (2 shorter events, 0.0 us)
Async XLA Ops:
  7.2 92.4 %copy-start = (bf16[576,1024]{1,0:T(8,128)(2,1)S(1)}, bf16[576,1024]{1,0:T(8,128)(2,1)}, u32[]{:S(2)}) copy-start(bf16[576,1024]{1,0:T(8,128)(2,1)} %param.6) | copy-start | bytes 3538948
  7.2 200.4 %all-reduce.4.cloned.1.call-start = ((), (), s32[]{:S(2)}) async-start(), calls=%async_computation | async-start | bytes 4194304 | tf_op jit(solution)/shard_map/psum | solution.py:17
  99.6 113.8 %copy-start.4 = (bf16[512,576]{1,0:T(8,128)(2,1)}, bf16[512,576]{1,0:T(8,128)(2,1)S(1)}, u32[]{:S(2)}) copy-start(bf16[512,576]{1,0:T(8,128)(2,1)S(1)} %all_gather.3) | copy-start | bytes 1769476
  101.8 105.8 %copy-start.9 = (f32[1024]{0:T(1024)S(1)}, f32[1024]{0:T(1024)}, u32[]{:S(2)}) copy-start(f32[1024]{0:T(1024)} %param.7) | copy-start | bytes 12292
  101.9 649.1 %all-reduce.6.cloned.1.call-start = ((), (), s32[]{:S(2)}) async-start(), calls=%async_computation.1 | async-start | bytes 2359296 | tf_op jit(solution)/shard_map/psum | solution.py:24
  207.6 3.8 copy-start.6
  210.5 1.0 copy-start.2
  213.3 537.7 %copy-start.8 = (f32[576]{0:T(1024)S(1)}, f32[576]{0:T(1024)}, u32[]{:S(2)}) copy-start(f32[576]{0:T(1024)} %param.9) | copy-start | bytes 6916
  213.3 656.2 %all-reduce.8.cloned.1.call-start = ((), (), s32[]{:S(2)}) async-start(), calls=%async_computation.2 | async-start | bytes 4194304 | tf_op jit(solution)/shard_map/psum | solution.py:43
  213.6 539.6 %copy-start.7 = (bf16[1024,576]{0,1:T(8,128)(2,1)S(1)}, bf16[1024,576]{0,1:T(8,128)(2,1)}, u32[]{:S(2)}) copy-start(bf16[1024,576]{0,1:T(8,128)(2,1)} %param.8) | copy-start | bytes 3538948
  755.5 1.3 copy-start.1
  859.3 10.1 %copy-start.3 = (bf16[512,1024]{1,0:T(8,128)(2,1)S(1)}, bf16[512,1024]{1,0:T(8,128)(2,1)}, u32[]{:S(2)}) copy-start(bf16[512,1024]{1,0:T(8,128)(2,1)} %copy-done.2) | copy-start | bytes 3145732
  869.4 2.7 copy-start.5
Sparse Core Ops, SparseCore 0:
  102.0 105.5 all-reduce.3
  213.4 537.4 all-reduce.5
  755.6 113.7 all-reduce.7
where the time goes:
time: 882 us
  waiting for transfers between devices  632 us (72%)
  blocking collectives  209 us (24%)
  between operations  17 us (2%)
  matrix products  11.7 us (1%)
  other arithmetic  10.3 us (1%)
    psum x1, waiting for transfers between devices, local(): recon = lax.psum(recon_part, 'latent') + b_dec  537 us
    psum x1, blocking collectives, local(): lax.psum(jnp.sum(err * err) * first_latent + penalty_part * first_layer,...  100 us
    all_gather x1, blocking collectives, local(): rows_all = lax.all_gather(residual, 'latent', axis=0, tiled=True)  92.3 us
    psum x1, waiting for transfers between devices, local(): pre_sum, square_sum = lax.psum((partial_value, squares), 'layer')  87.5 us
  transfers between devices with their start and end apart: 3, of which 3 were waited for; matrix products, arithmetic and copies ran while one was open for 1% of the time, Pallas kernels for 0%

commit v1 on v0

v1 whole, which is shorter than its diff:
```python
import jax
import jax.numpy as jnp
from jax import lax
from jax.sharding import Mesh, PartitionSpec as P

D = 4608
ROWS = 512
LAYER = ("x", "yl")
CHIPS = ("z", "yh")
LATENT = ("z", "yh", "c")
f32, bf16 = jnp.float32, jnp.bfloat16

penalty_weight = 0.5


def exchange(blocks, axes):
    return lax.all_to_all(blocks, axes, 0, 0, tiled=True)


def spread(block, axes, count):
    return exchange(jnp.broadcast_to(block[None], (count,) + block.shape), axes)


def split(value):
    high = lax.reduce_precision(value, exponent_bits=8, mantissa_bits=7)
    return high.astype(bf16), (value - high).astype(bf16)


def chunked(value):
    return value.reshape(8, 64, 8, 128).transpose(0, 2, 1, 3).reshape(8, 512, 128)


def whole(value):
    return value.reshape(8, 8, 64, 128).transpose(0, 2, 1, 3).reshape(512, 1024)


def local(residual, w_enc, b_enc, w_dec, b_dec):
    core = lax.axis_index("c")
    near = spread(residual, CHIPS, 32).reshape(256, 576)
    rows_all = lax.all_gather(near, "c", axis=0, tiled=True)
    wide = w_dec.astype(f32)
    squares = jnp.stack(split(jnp.sum(wide * wide, axis=1).reshape(8, 128))).reshape(1, 16, 128)

    part = chunked(jnp.dot(rows_all, w_enc, preferred_element_type=f32))
    sent = jnp.concatenate([part.astype(bf16), jnp.broadcast_to(squares, (8, 16, 128))], axis=1)
    got = jnp.sum(exchange(sent, LAYER).astype(f32), axis=0)
    bias = b_enc.reshape(8, 1, 128)
    norms = jnp.sqrt(got[512:520] + got[520:528] + 1e-06)
    acts_own = jnp.maximum(got[:512].reshape(8, 64, 128) + bias, 0.0).astype(bf16)
    penalty_part = penalty_weight * jnp.sum(acts_own.astype(f32) * norms[:, None, :])
    acts = whole(spread(acts_own.reshape(512, 128), LAYER, 8))
    exact = lax.psum_scatter(part, LAYER, scatter_dimension=0, tiled=True)
    active = exact.reshape(8, 64, 128) + bias > 0

    recon_part = jnp.dot(acts, w_dec, preferred_element_type=f32).reshape(2, 256, 576)
    other = lax.dynamic_index_in_dim(recon_part, 1 - core, 0, keepdims=False).astype(bf16)
    mine = lax.dynamic_index_in_dim(recon_part, core, 0, keepdims=False)
    pair = mine + lax.ppermute(other, "c", [(0, 1), (1, 0)]).astype(f32)
    recon = jnp.sum(exchange(pair.astype(bf16).reshape(32, 8, 576), CHIPS).astype(f32), axis=0) + b_dec
    err = recon - residual.astype(f32)
    high, low = split(jnp.sum(err * err) + penalty_part)
    column = lax.broadcasted_iota(jnp.int32, (8, 64), 1)
    row = lax.broadcasted_iota(jnp.int32, (8, 64), 0)
    tail = jnp.where((row == 0) & (column == 0), high, jnp.where((row == 0) & (column == 1), low, jnp.zeros((), bf16)))
    packed = jnp.concatenate([(err / 8.0).astype(bf16), tail], axis=1)
    packed = spread(packed, CHIPS, 32).reshape(256, 640)
    packed = lax.all_gather(packed, "c", axis=0, tiled=True)
    d_recon = packed[:, :576]
    total = jnp.sum(packed[:, 576:].astype(f32))
    high, low = split(total)
    at = lax.broadcasted_iota(jnp.int32, (16, 128), 1)
    up = lax.broadcasted_iota(jnp.int32, (16, 128), 0)
    tail = jnp.where((up == 0) & (at == 0), high, jnp.where((up == 0) & (at == 1), low, jnp.zeros((), bf16)))

    act_part = lax.dot_general(d_recon, w_dec, (((1,), (1,)), ((), ())), preferred_element_type=f32)
    sent = jnp.concatenate([chunked(act_part).astype(bf16), jnp.broadcast_to(tail[None], (8, 16, 128))], axis=1)
    got = jnp.sum(exchange(sent, LAYER).astype(f32), axis=0)
    loss = jnp.sum(got[512:]) / (ROWS * D)
    d_acts = got[:512].reshape(8, 64, 128) + penalty_weight / 16.0 * norms[:, None, :]
    d_pre_own = jnp.where(active, d_acts, 0.0).astype(bf16).reshape(512, 128)

    grad_bdec = jnp.sum(d_recon.astype(f32), axis=0).astype(bf16)
    col_sum = jnp.sum(acts.astype(f32), axis=0)
    outer = lax.dot_general(acts, d_recon, (((0,), (0,)), ((), ())), preferred_element_type=f32)
    scale = penalty_weight / 16.0 * col_sum / norms.reshape(1024)
    grad_dec = (outer + scale[:, None] * wide).astype(bf16)

    d_pre = whole(spread(d_pre_own, LAYER, 8))
    grad_enc = lax.dot_general(rows_all, d_pre, (((0,), (0,)), ((), ())), preferred_element_type=f32).astype(bf16)
    grad_benc = jnp.sum(d_pre.astype(f32), axis=0).astype(bf16)
    return (grad_enc, grad_benc, grad_dec, grad_bdec, loss)


def solution(mesh):
    fine = Mesh(mesh.devices.reshape(4, 2, 8, 4, 2), ("x", "yl", "z", "yh", "c"))
    placed = (P(LATENT, LAYER), P(LAYER, LATENT), P(LATENT), P(LATENT, LAYER), P(LAYER))
    return jax.shard_map(
        local,
        mesh=fine,
        in_specs=placed,
        out_specs=(P(LAYER, LATENT), P(LATENT), P(LATENT, LAYER), P(LAYER), P()),
        check_vma=False,
    )
```

time: 882 us -> 220 us (0.25)
  waiting for transfers between devices: 632 us -> 83.6 us
  blocking collectives: 209 us -> 28.6 us
  starting transfers between devices: 0.12 us -> 43.6 us
  local copies, waits for them, and re-layouts: 1.76 us -> 14.1 us
    psum x3 -> x0, waiting for transfers between devices: 632 us -> none  [the longest x1 537 us: local(): recon = lax.psum(recon_part, 'latent') + b_dec]
    psum x2 -> x0, blocking collectives: 117 us -> none  [the longest x1 100 us: local(): lax.psum(jnp.sum(err * err) * first_latent + penalty_part * first_layer,...]
    all_gather x1 -> x2, blocking collectives: 92.3 us -> 9.16 us  [the longest x1 4.67 us: local(): rows_all = lax.all_gather(near, 'c', axis=0, tiled=True)]
    all_to_all x0 -> x6, waiting for transfers between devices: none -> 81.4 us  [exchange(): return lax.all_to_all(blocks, axes, 0, 0, tiled=True)]
    all_to_all x0 -> x6, starting transfers between devices: none -> 39 us  [exchange(): return lax.all_to_all(blocks, axes, 0, 0, tiled=True)]
    all_to_all x0 -> x1, blocking collectives: none -> 19.4 us  [exchange(): return lax.all_to_all(blocks, axes, 0, 0, tiled=True)]
  transfers between devices with their start and end apart: 3 -> 8, of which waited for: 3 -> 7; matrix products, arithmetic and copies ran while one was open for 1% -> 8% of each run, Pallas kernels for 0% -> 0%
where the time goes in v1:
time: 220 us; the launch traced here: 219 us
  waiting for transfers between devices  83.6 us (38%)
  starting transfers between devices  43.6 us (20%)
  blocking collectives  28.6 us (13%)
  between operations  22.3 us (10%)
  other arithmetic  14.9 us (7%)
  local copies, waits for them, and re-layouts  14.1 us (6%)
  matrix products  11.8 us (5%)
    all_to_all x6, waiting for transfers between devices, exchange(): return lax.all_to_all(blocks, axes, 0, 0, tiled=True)  81.4 us
    all_to_all x6, starting transfers between devices, exchange(): return lax.all_to_all(blocks, axes, 0, 0, tiled=True)  39 us
    all_to_all x1, blocking collectives, exchange(): return lax.all_to_all(blocks, axes, 0, 0, tiled=True)  19.4 us
    all_gather x1, blocking collectives, local(): rows_all = lax.all_gather(near, 'c', axis=0, tiled=True)  4.67 us
    ppermute x1, starting transfers between devices, local(): pair = mine + lax.ppermute(other, 'c', [(0, 1), (1, 0)]).astype(f32)  4.54 us
    broadcast_in_dim x4, local copies, waits for them, and re-layouts, spread(): return exchange(jnp.broadcast_to(block[None], (count,) + block.shape), axes)  4.51 us
    all_gather x1, blocking collectives, local(): packed = lax.all_gather(packed, 'c', axis=0, tiled=True)  4.49 us
  transfers between devices with their start and end apart: 8, of which 7 were waited for; matrix products, arithmetic and copies ran while one was open for 8% of the time, Pallas kernels for 0%

profile of v1, /device:TPU:1, one launch (start us, length us, event | category | flops | bytes accessed | tf_op | source)
XLA Modules:
  0.0 219.0 jit_solution(5335199204518925962)
XLA Ops:
  7.2 0.0 copy-start
  7.2 1.5 broadcast_in_dim.67
  8.7 16.5 %all-to-all-start = ((bf16[32,8,576]{2,1,0:T(8,128)(2,1)}), bf16[32,8,576]{2,1,0:T(8,128)(2,1)S(1)}, u32[]{:S(2)}, u32[]{:S(2)}) async-start(bf16[32,8,576]{2,1,0:T(8,128)(2,1)} %broadcast_in_dim.67), calls=%async_computation | async-start | bytes 655360 | tf_op jit(solution)/shard_map/all_to_all | solution.py:17
  25.3 1.5 fusion
  26.8 12.0 %all-to-all-done = bf16[32,8,576]{2,1,0:T(8,128)(2,1)S(1)} async-done(((bf16[32,8,576]{2,1,0:T(8,128)(2,1)}), bf16[32,8,576]{2,1,0:T(8,128)(2,1)S(1)}, u32[]{:S(2)}, u32[]{:S(2)}) %all-to-all-start) | async-done | bytes 294944 | tf_op jit(solution)/shard_map/all_to_all | solution.py:17
  38.9 4.7 %all_gather.6 = bf16[512,576]{1,0:T(8,128)(2,1)S(1)} all-gather(bf16[256,576]{1,0:T(8,128)(2,1)S(1)} %bitcast.94), channel_id=1, replica_groups=mesh['x'=4,'yl'=2,'z'=8,'yh'=4,'c'=2] {'c'}, dimensions={0}, use_global_device_ids=true | all-gather | bytes 884736 | tf_op jit(solution)/shard_map/all_gather | solution.py:40
  43.5 1.0 convolution_bitcast_fusion
  44.5 0.5 copy.42
  45.0 0.4 copy.35
  45.4 0.1 bitcast_convert_fusion
  45.6 1.2 copy-done.1
  46.8 0.1 pad_maximum_fusion
  46.8 19.4 %all_to_all.35 = bf16[8,528,128]{2,1,0:T(8,128)(2,1)S(1)} all-to-all(bf16[8,528,128]{2,1,0:T(8,128)(2,1)S(1)} %pad_maximum_fusion), channel_id=1, replica_groups=mesh['x'=4,'yl'=2,'z'=8,'yh'=4,'c'=2] {'x','yl'}, dimensions={0} | all-to-all | bytes 2162688 | tf_op jit(solution)/shard_map/all_to_all | solution.py:17
  66.3 0.1 convert_reduce_fusion.1
  66.4 0.5 copy-done.7
  67.0 1.1 broadcast_in_dim.70
  68.1 3.6 %all-to-all-start.2 = ((bf16[8,512,128]{2,1,0:T(8,128)(2,1)}), bf16[8,512,128]{2,1,0:T(8,128)(2,1)S(1)}, u32[]{:S(2)}, u32[]{:S(2)}) async-start(bf16[8,512,128]{2,1,0:T(8,128)(2,1)} %broadcast_in_dim.70), calls=%async_computation.3 | async-start | bytes 2097152 | tf_op jit(solution)/shard_map/all_to_all | solution.py:17
  71.7 13.9 %all-to-all-done.2 = bf16[8,512,128]{2,1,0:T(8,128)(2,1)S(1)} async-done(((bf16[8,512,128]{2,1,0:T(8,128)(2,1)}), bf16[8,512,128]{2,1,0:T(8,128)(2,1)S(1)}, u32[]{:S(2)}, u32[]{:S(2)}) %all-to-all-start.2) | async-done | bytes 1048608 | tf_op jit(solution)/shard_map/all_to_all | solution.py:17
  85.6 0.7 copy.36
  86.3 1.3 dot_general.18
  87.6 2.4 %fusion.5 = f32[2,256,576]{1,2,0:T(8,128)S(1)} fusion(bf16[2,256,1024]{2,1,0:T(8,128)(2,1)} %dot_general.18, bf16[1024,576]{0,1:T(8,128)(2,1)} %param.8), kind=kOutput, calls=%fused_computation.13 | convolution fusion | flops 603979776 | bytes 3407872 | tf_op jit(solution)/shard_map/dot_general | solution.py:55
  90.0 1.0 copy-done.4
  91.0 0.7 fusion.14
  91.7 4.5 %collective-permute-start = (bf16[256,576]{0,1:T(8,128)(2,1)}, bf16[256,576]{0,1:T(8,128)(2,1)}, u32[]{:S(2)}, u32[]{:S(2)}) collective-permute-start(bf16[256,576]{0,1:T(8,128)(2,1)} %fusion.14), channel_id=1, source_target_pairs={{0,1},{1,0},{2,3},{3,2},{4,5},{5,4},{6,7},{7,6},{8,9},{9,8},{10,11... | collective-permute-start | bytes 884744 | tf_op jit(solution)/shard_map/ppermute | solution.py:58
  96.3 1.5 collective-permute-done
  97.8 1.9 fusion.11
  99.7 1.9 copy.37
  101.6 4.9 %all-to-all-start.3 = ((bf16[32,8,576]{2,1,0:T(8,128)(2,1)}), bf16[32,8,576]{2,1,0:T(8,128)(2,1)}, u32[]{:S(2)}, u32[]{:S(2)}) async-start(bf16[32,8,576]{2,1,0:T(8,128)(2,1)} %bitcast.92), calls=%async_computation.4 | async-start | bytes 655360 | tf_op jit(solution)/shard_map/all_to_all | solution.py:17
  106.5 0.0 reduce-scatter.2.cloned.1.call-start
  106.6 0.7 reduce-scatter.2.cloned.1.call-update
  107.3 0.0 copy-start.6
  107.3 0.0 copy-start.8
  107.3 0.2 convert_reduce_fusion.2
  107.5 0.7 divide_bitcast_fusion
  108.2 0.7 fusion.20
  109.5 10.0 %all-to-all-done.3 = bf16[32,8,576]{2,1,0:T(8,128)(2,1)} async-done(((bf16[32,8,576]{2,1,0:T(8,128)(2,1)}), bf16[32,8,576]{2,1,0:T(8,128)(2,1)}, u32[]{:S(2)}, u32[]{:S(2)}) %all-to-all-start.3) | async-done | bytes 294944 | tf_op jit(solution)/shard_map/all_to_all | solution.py:17
  119.5 1.0 convert_reduce_fusion.3
  120.6 0.6 multiply_convert_fusion
  123.6 0.1 and_select_fusion.3
  123.7 0.1 pad_maximum_fusion.2
  123.8 0.8 broadcast_in_dim.74
  124.6 6.9 %all-to-all-start.4 = ((bf16[32,8,640]{2,1,0:T(8,128)(2,1)}), bf16[32,8,640]{2,1,0:T(8,128)(2,1)S(1)}, u32[]{:S(2)}, u32[]{:S(2)}) async-start(bf16[32,8,640]{2,1,0:T(8,128)(2,1)} %broadcast_in_dim.74), calls=%async_computation.5 | async-start | bytes 655360 | tf_op jit(solution)/shard_map/all_to_all | solution.py:17
  131.5 18.1 %all-to-all-done.4 = bf16[32,8,640]{2,1,0:T(8,128)(2,1)S(1)} async-done(((bf16[32,8,640]{2,1,0:T(8,128)(2,1)}), bf16[32,8,640]{2,1,0:T(8,128)(2,1)S(1)}, u32[]{:S(2)}, u32[]{:S(2)}) %all-to-all-start.4) | async-done | bytes 327712 | tf_op jit(solution)/shard_map/all_to_all | solution.py:17
  149.6 0.2 copy.38
  149.8 4.5 %all_gather.7 = bf16[512,640]{0,1:T(8,128)(2,1)S(1)} all-gather(bf16[256,640]{0,1:T(8,128)(2,1)S(1)} %copy.38), channel_id=1, replica_groups=mesh['x'=4,'yl'=2,'z'=8,'yh'=4,'c'=2] {'c'}, dimensions={0}, use_global_device_ids=true | all-gather | bytes 983040 | tf_op jit(solution)/shard_map/all_gather | solution.py:67
  154.2 0.7 convert_reduce_fusion.4
  158.1 2.3 %fusion.4 = bf16[64,8,8,128]{3,1,2,0:T(8,128)(2,1)S(1)} fusion(bf16[1024,576]{0,1:T(8,128)(2,1)} %param.8, bf16[512,640]{0,1:T(8,128)(2,1)S(1)} %all_gather.7), kind=kOutput, calls=%fused_computation.12 | convolution fusion | flops 604504064 | bytes 2818048 | tf_op jit(solution)/shard_map/dot_general | solution.py:75
  160.4 0.3 copy.43
  160.7 0.3 copy.39
  160.9 0.1 and_select_fusion.1
  161.0 1.1 pad_maximum_fusion.1
  162.1 3.6 %all-to-all-start.5 = ((bf16[8,528,128]{2,1,0:T(8,128)(2,1)}), bf16[8,528,128]{2,1,0:T(8,128)(2,1)S(1)}, u32[]{:S(2)}, u32[]{:S(2)}) async-start(bf16[8,528,128]{2,1,0:T(8,128)(2,1)} %pad_maximum_fusion.1), calls=%async_computation.6 | async-start | bytes 2162688 | tf_op jit(solution)/shard_map/all_to_all | solution.py:17
  165.7 19.2 %all-to-all-done.5 = bf16[8,528,128]{2,1,0:T(8,128)(2,1)S(1)} async-done(((bf16[8,528,128]{2,1,0:T(8,128)(2,1)}), bf16[8,528,128]{2,1,0:T(8,128)(2,1)S(1)}, u32[]{:S(2)}, u32[]{:S(2)}) %all-to-all-start.5) | async-done | bytes 1081376 | tf_op jit(solution)/shard_map/all_to_all | solution.py:17
  184.8 0.8 convert_reduce_fusion
  185.7 1.1 fusion.17
  186.8 1.1 broadcast_in_dim.80
  187.9 3.6 %all-to-all-start.6 = ((bf16[8,512,128]{2,1,0:T(8,128)(2,1)}), bf16[8,512,128]{2,1,0:T(8,128)(2,1)S(1)}, u32[]{:S(2)}, u32[]{:S(2)}) async-start(bf16[8,512,128]{2,1,0:T(8,128)(2,1)} %broadcast_in_dim.80), calls=%async_computation.7 | async-start | bytes 2097152 | tf_op jit(solution)/shard_map/all_to_all | solution.py:17
  191.5 1.8 slice_reduce_fusion
  193.3 3.3 %fusion.2 = bf16[1024,576]{0,1:T(8,128)(2,1)} fusion(bf16[1024,576]{0,1:T(8,128)(2,1)} %param.8, f32[1024]{0:T(1024)S(1)} %get-tuple-element.5, bf16[64,8,8,128]{3,2,1,0:T(8,128)(2,1)S(1)} %bitcast.89, bf16[512,640]{0,1:T(8,128)(2,1)} %copy-done.2), kind=kOutput, calls=%fused_computation.4 | convolution fusion | flops 606339072 | bytes 4001792 | tf_op jit(solution)/shard_map/dot_general | solution.py:84
  196.6 1.3 slice_reduce_fusion.1
  198.5 8.1 %all-to-all-done.6 = bf16[8,512,128]{2,1,0:T(8,128)(2,1)S(1)} async-done(((bf16[8,512,128]{2,1,0:T(8,128)(2,1)}), bf16[8,512,128]{2,1,0:T(8,128)(2,1)S(1)}, u32[]{:S(2)}, u32[]{:S(2)}) %all-to-all-start.6) | async-done | bytes 1048608 | tf_op jit(solution)/shard_map/all_to_all | solution.py:17
  206.6 0.7 copy.40
  207.3 0.8 reduce_sum.114
  208.1 2.9 %fusion.3 = bf16[576,1024]{1,0:T(8,128)(2,1)} fusion(bf16[512,576]{1,0:T(8,128)(2,1)} %copy-done.5, bf16[64,8,8,128]{3,2,1,0:T(8,128)(2,1)S(1)} %bitcast.96), kind=kOutput, calls=%fused_computation.11 | convolution fusion | flops 604569600 | bytes 2818048 | tf_op jit(solution)/shard_map/dot_general | solution.py:89
  (24 shorter events, 0.1 us)
Async XLA Ops:
  7.2 36.4 %copy-start = (bf16[576,1024]{1,0:T(8,128)(2,1)S(1)}, bf16[576,1024]{1,0:T(8,128)(2,1)}, u32[]{:S(2)}) copy-start(bf16[576,1024]{1,0:T(8,128)(2,1)} %param.6) | copy-start | bytes 3538948
  8.7 30.1 %all-to-all-start = ((bf16[32,8,576]{2,1,0:T(8,128)(2,1)}), bf16[32,8,576]{2,1,0:T(8,128)(2,1)S(1)}, u32[]{:S(2)}, u32[]{:S(2)}) async-start(bf16[32,8,576]{2,1,0:T(8,128)(2,1)} %broadcast_in_dim.67), calls=%async_computation | async-start | bytes 655360 | tf_op jit(solution)/shard_map/all_to_all | solution.py:17
  43.5 1.0 copy-start.5
  45.4 1.4 copy-start.1
  66.3 0.7 copy-start.7
  66.4 1.7 copy-start.3
  68.1 17.5 %all-to-all-start.2 = ((bf16[8,512,128]{2,1,0:T(8,128)(2,1)}), bf16[8,512,128]{2,1,0:T(8,128)(2,1)S(1)}, u32[]{:S(2)}, u32[]{:S(2)}) async-start(bf16[8,512,128]{2,1,0:T(8,128)(2,1)} %broadcast_in_dim.70), calls=%async_computation.3 | async-start | bytes 2097152 | tf_op jit(solution)/shard_map/all_to_all | solution.py:17
  90.0 1.0 copy-start.4
  91.7 6.1 %collective-permute-start = (bf16[256,576]{0,1:T(8,128)(2,1)}, bf16[256,576]{0,1:T(8,128)(2,1)}, u32[]{:S(2)}, u32[]{:S(2)}) collective-permute-start(bf16[256,576]{0,1:T(8,128)(2,1)} %fusion.14), channel_id=1, source_target_pairs={{0,1},{1,0},{2,3},{3,2},{4,5},{5,4},{6,7},{7,6},{8,9},{9,8},{10,11... | collective-permute-start | bytes 884744 | tf_op jit(solution)/shard_map/ppermute | solution.py:58
  101.6 17.9 %all-to-all-start.3 = ((bf16[32,8,576]{2,1,0:T(8,128)(2,1)}), bf16[32,8,576]{2,1,0:T(8,128)(2,1)}, u32[]{:S(2)}, u32[]{:S(2)}) async-start(bf16[32,8,576]{2,1,0:T(8,128)(2,1)} %bitcast.92), calls=%async_computation.4 | async-start | bytes 655360 | tf_op jit(solution)/shard_map/all_to_all | solution.py:17
  106.5 79.2 %reduce-scatter.2.cloned.1.call-start = ((), (), s32[]{:S(2)}) async-start(), calls=%async_computation.8 | async-start | bytes 2359296 | tf_op jit(solution)/shard_map/reduce_scatter | solution.py:52
  107.3 13.3 %copy-start.6 = (bf16[8,576]{1,0:T(8,128)(2,1)S(1)}, bf16[8,576]{1,0:T(8,128)(2,1)}, u32[]{:S(2)}) copy-start(bf16[8,576]{1,0:T(8,128)(2,1)} %param.5) | copy-start | bytes 27652
  107.3 13.3 %copy-start.8 = (f32[576]{0:T(1024)S(1)}, f32[576]{0:T(1024)}, u32[]{:S(2)}) copy-start(f32[576]{0:T(1024)} %param.9) | copy-start | bytes 6916
  124.6 25.0 %all-to-all-start.4 = ((bf16[32,8,640]{2,1,0:T(8,128)(2,1)}), bf16[32,8,640]{2,1,0:T(8,128)(2,1)S(1)}, u32[]{:S(2)}, u32[]{:S(2)}) async-start(bf16[32,8,640]{2,1,0:T(8,128)(2,1)} %broadcast_in_dim.74), calls=%async_computation.5 | async-start | bytes 655360 | tf_op jit(solution)/shard_map/all_to_all | solution.py:17
  154.2 6.1 %copy-start.2 = (bf16[512,640]{0,1:T(8,128)(2,1)}, bf16[512,640]{0,1:T(8,128)(2,1)S(1)}, u32[]{:S(2)}) copy-start(bf16[512,640]{0,1:T(8,128)(2,1)S(1)} %all_gather.7) | copy-start | bytes 1966084
  162.1 22.8 %all-to-all-start.5 = ((bf16[8,528,128]{2,1,0:T(8,128)(2,1)}), bf16[8,528,128]{2,1,0:T(8,128)(2,1)S(1)}, u32[]{:S(2)}, u32[]{:S(2)}) async-start(bf16[8,528,128]{2,1,0:T(8,128)(2,1)} %pad_maximum_fusion.1), calls=%async_computation.6 | async-start | bytes 2162688 | tf_op jit(solution)/shard_map/all_to_all | solution.py:17
  187.9 18.7 %all-to-all-start.6 = ((bf16[8,512,128]{2,1,0:T(8,128)(2,1)}), bf16[8,512,128]{2,1,0:T(8,128)(2,1)S(1)}, u32[]{:S(2)}, u32[]{:S(2)}) async-start(bf16[8,512,128]{2,1,0:T(8,128)(2,1)} %broadcast_in_dim.80), calls=%async_computation.7 | async-start | bytes 2097152 | tf_op jit(solution)/shard_map/all_to_all | solution.py:17
Sparse Core Ops, SparseCore 0:
  110.2 64.7 reduce-scatter.1

commit v2 on v1

--- a/solution.py
+++ b/solution.py
@@ -26,6 +26,22 @@
     return high.astype(bf16), (value - high).astype(bf16)
 
 
+def forward(block, by):
+    pairs = [(x * 2 + y, (x + by[0]) % 4 * 2 + (y + by[1]) % 2) for x in range(4) for y in range(2)]
+    return lax.ppermute(block, LAYER, pairs)
+
+
+def remainders(low, steps):
+    at_x, at_y = lax.axis_index("x"), lax.axis_index("yl")
+    total = None
+    for by in steps:
+        to = (at_x + by[0]) % 4 * 2 + (at_y + by[1]) % 2
+        block = lax.dynamic_index_in_dim(low, to, 0, keepdims=False)
+        block = (block if by == (0, 0) else forward(block, by)).astype(f32)
+        total = block if total is None else total + block
+    return total
+
+
 def chunked(value):
     return value.reshape(8, 64, 8, 128).transpose(0, 2, 1, 3).reshape(8, 512, 128)
 
@@ -43,27 +59,32 @@
 
     part = chunked(jnp.dot(rows_all, w_enc, preferred_element_type=f32))
     sent = jnp.concatenate([part.astype(bf16), jnp.broadcast_to(squares, (8, 16, 128))], axis=1)
-    got = jnp.sum(exchange(sent, LAYER).astype(f32), axis=0)
+    pre = jnp.sum(exchange(sent, LAYER).astype(f32), axis=0)
     bias = b_enc.reshape(8, 1, 128)
-    norms = jnp.sqrt(got[512:520] + got[520:528] + 1e-06)
-    acts_own = jnp.maximum(got[:512].reshape(8, 64, 128) + bias, 0.0).astype(bf16)
+    norms = jnp.sqrt(pre[512:520] + pre[520:528] + 1e-06)
+    acts_own = jnp.maximum(pre[:512].reshape(8, 64, 128) + bias, 0.0).astype(bf16)
     penalty_part = penalty_weight * jnp.sum(acts_own.astype(f32) * norms[:, None, :])
     acts = whole(spread(acts_own.reshape(512, 128), LAYER, 8))
-    exact = lax.psum_scatter(part, LAYER, scatter_dimension=0, tiled=True)
-    active = exact.reshape(8, 64, 128) + bias > 0
+    _, low_part = split(part)
 
     recon_part = jnp.dot(acts, w_dec, preferred_element_type=f32).reshape(2, 256, 576)
     other = lax.dynamic_index_in_dim(recon_part, 1 - core, 0, keepdims=False).astype(bf16)
     mine = lax.dynamic_index_in_dim(recon_part, core, 0, keepdims=False)
     pair = mine + lax.ppermute(other, "c", [(0, 1), (1, 0)]).astype(f32)
-    recon = jnp.sum(exchange(pair.astype(bf16).reshape(32, 8, 576), CHIPS).astype(f32), axis=0) + b_dec
+    pair, low_part = lax.optimization_barrier((pair, low_part))
+    fine = remainders(low_part, [(0, 0), (0, 1), (1, 0), (1, 1)])
+    recon, fine = lax.optimization_barrier((exchange(pair.astype(bf16).reshape(32, 8, 576), CHIPS), fine))
+    recon = jnp.sum(recon.astype(f32), axis=0) + b_dec
     err = recon - residual.astype(f32)
     high, low = split(jnp.sum(err * err) + penalty_part)
     column = lax.broadcasted_iota(jnp.int32, (8, 64), 1)
     row = lax.broadcasted_iota(jnp.int32, (8, 64), 0)
     tail = jnp.where((row == 0) & (column == 0), high, jnp.where((row == 0) & (column == 1), low, jnp.zeros((), bf16)))
     packed = jnp.concatenate([(err / 8.0).astype(bf16), tail], axis=1)
-    packed = spread(packed, CHIPS, 32).reshape(256, 640)
+    packed, low_part = lax.optimization_barrier((packed, low_part))
+    fine = fine + remainders(low_part, [(2, 0), (2, 1), (3, 0), (3, 1)])
+    packed, fine = lax.optimization_barrier((spread(packed, CHIPS, 32), fine))
+    packed = packed.reshape(256, 640)
     packed = lax.all_gather(packed, "c", axis=0, tiled=True)
     d_recon = packed[:, :576]
     total = jnp.sum(packed[:, 576:].astype(f32))
@@ -77,6 +98,7 @@
     got = jnp.sum(exchange(sent, LAYER).astype(f32), axis=0)
     loss = jnp.sum(got[512:]) / (ROWS * D)
     d_acts = got[:512].reshape(8, 64, 128) + penalty_weight / 16.0 * norms[:, None, :]
+    active = (pre[:512] + fine).reshape(8, 64, 128) + bias > 0
     d_pre_own = jnp.where(active, d_acts, 0.0).astype(bf16).reshape(512, 128)
 
     grad_bdec = jnp.sum(d_recon.astype(f32), axis=0).astype(bf16)

time: 220 us -> 212 us (0.964)
  starting transfers between devices: 43.6 us -> 68.6 us
  waiting for transfers between devices: 83.6 us -> 58.8 us
  between operations: 22.3 us -> 9.14 us
  local copies, waits for them, and re-layouts: 14.1 us -> 16.8 us
    all_to_all x6, waiting for transfers between devices: 81.4 us -> 47.7 us  [exchange(): return lax.all_to_all(blocks, axes, 0, 0, tiled=True)]
    ppermute x0 -> x7, starting transfers between devices: none -> 19.5 us  [forward(): return lax.ppermute(block, LAYER, pairs)]
    ppermute x0 -> x7, waiting for transfers between devices: none -> 11.1 us  [forward(): return lax.ppermute(block, LAYER, pairs)]
    all_to_all x6, starting transfers between devices: 39 us -> 44.6 us  [exchange(): return lax.all_to_all(blocks, axes, 0, 0, tiled=True)]
  transfers between devices with their start and end apart: 8 -> 14, of which waited for: 7 -> 8; matrix products, arithmetic and copies ran while one was open for 8% -> 7% of each run, Pallas kernels for 0% -> 0%
where the time goes in v2:
time: 212 us; the launch traced here: 210 us
  starting transfers between devices  68.6 us (32%)
  waiting for transfers between devices  58.8 us (28%)
  blocking collectives  29.2 us (14%)
  local copies, waits for them, and re-layouts  16.8 us (8%)
  other arithmetic  15.9 us (8%)
  matrix products  11.8 us (6%)
  between operations  9.14 us (4%)
    all_to_all x6, waiting for transfers between devices, exchange(): return lax.all_to_all(blocks, axes, 0, 0, tiled=True)  47.7 us
    all_to_all x6, starting transfers between devices, exchange(): return lax.all_to_all(blocks, axes, 0, 0, tiled=True)  44.6 us
    ppermute x7, starting transfers between devices, forward(): return lax.ppermute(block, LAYER, pairs)  19.5 us
    all_to_all x1, blocking collectives, exchange(): return lax.all_to_all(blocks, axes, 0, 0, tiled=True)  19.4 us
    ppermute x7, waiting for transfers between devices, forward(): return lax.ppermute(block, LAYER, pairs)  11.1 us
    all_gather x1, blocking collectives, local(): packed = lax.all_gather(packed, 'c', axis=0, tiled=True)  5.07 us
    all_gather x1, blocking collectives, local(): rows_all = lax.all_gather(near, 'c', axis=0, tiled=True)  4.67 us
    ppermute x1, starting transfers between devices, local(): pair = mine + lax.ppermute(other, 'c', [(0, 1), (1, 0)]).astype(f32)  4.55 us
  transfers between devices with their start and end apart: 14, of which 8 were waited for; matrix products, arithmetic and copies ran while one was open for 7% of the time, Pallas kernels for 0%

profile of v2, /device:TPU:1, one launch (start us, length us, event | category | flops | bytes accessed | tf_op | source)
XLA Modules:
  0.0 210.1 jit_solution(2599563028317778386)
XLA Ops:
  0.6 1.5 broadcast_in_dim.65
  2.2 16.5 %all-to-all-start = ((bf16[32,8,576]{2,1,0:T(8,128)(2,1)}), bf16[32,8,576]{2,1,0:T(8,128)(2,1)S(1)}, u32[]{:S(2)}, u32[]{:S(2)}) async-start(bf16[32,8,576]{2,1,0:T(8,128)(2,1)} %broadcast_in_dim.65), calls=%async_computation | async-start | bytes 655360 | tf_op jit(solution)/shard_map/all_to_all | solution.py:17
  18.7 1.5 fusion
  20.3 12.0 %all-to-all-done = bf16[32,8,576]{2,1,0:T(8,128)(2,1)S(1)} async-done(((bf16[32,8,576]{2,1,0:T(8,128)(2,1)}), bf16[32,8,576]{2,1,0:T(8,128)(2,1)S(1)}, u32[]{:S(2)}, u32[]{:S(2)}) %all-to-all-start) | async-done | bytes 294944 | tf_op jit(solution)/shard_map/all_to_all | solution.py:17
  32.3 4.7 %all_gather.6 = bf16[512,576]{1,0:T(8,128)(2,1)S(1)} all-gather(bf16[256,576]{1,0:T(8,128)(2,1)S(1)} %bitcast.101), channel_id=1, replica_groups=mesh['x'=4,'yl'=2,'z'=8,'yh'=4,'c'=2] {'c'}, dimensions={0}, use_global_device_ids=true | all-gather | bytes 884736 | tf_op jit(solution)/shard_map/all_gather | solution.py:56
  37.0 0.9 copy-done.7
  37.9 1.0 convolution_bitcast_fusion
  38.9 0.5 copy.42
  39.3 0.4 copy.35
  40.0 19.4 %all_to_all.35 = bf16[8,528,128]{2,1,0:T(8,128)(2,1)S(1)} all-to-all(bf16[8,528,128]{2,1,0:T(8,128)(2,1)S(1)} %pad_maximum_fusion), channel_id=1, replica_groups=mesh['x'=4,'yl'=2,'z'=8,'yh'=4,'c'=2] {'x','yl'}, dimensions={0} | all-to-all | bytes 2162688 | tf_op jit(solution)/shard_map/all_to_all | solution.py:17
  59.5 0.5 copy-done.9
  60.1 0.7 copy-done.4
  60.8 1.1 broadcast_in_dim.68
  61.9 4.2 %all-to-all-start.2 = ((bf16[8,512,128]{2,1,0:T(8,128)(2,1)}), bf16[8,512,128]{2,1,0:T(8,128)(2,1)}, u32[]{:S(2)}, u32[]{:S(2)}) async-start(bf16[8,512,128]{2,1,0:T(8,128)(2,1)} %broadcast_in_dim.68), calls=%async_computation.2 | async-start | bytes 2097152 | tf_op jit(solution)/shard_map/all_to_all | solution.py:17
  66.2 0.5 iota_compare_fusion.5
  66.7 0.5 iota_compare_fusion.3
  67.2 12.9 %all-to-all-done.2 = bf16[8,512,128]{2,1,0:T(8,128)(2,1)} async-done(((bf16[8,512,128]{2,1,0:T(8,128)(2,1)}), bf16[8,512,128]{2,1,0:T(8,128)(2,1)}, u32[]{:S(2)}, u32[]{:S(2)}) %all-to-all-start.2) | async-done | bytes 1048608 | tf_op jit(solution)/shard_map/all_to_all | solution.py:17
  80.2 2.9 %copy.36 = bf16[8,64,8,128]{3,2,1,0:T(8,128)(2,1)} copy(bf16[8,64,8,128]{3,1,2,0:T(8,128)(2,1)} %bitcast.8) | data formatting | bytes 2097152 | tf_op jit(solution)/shard_map/transpose | solution.py:50
  83.0 2.3 %dot_general.18 = bf16[2,256,1024]{2,1,0:T(8,128)(2,1)} reshape(bf16[8,64,8,128]{3,2,1,0:T(8,128)(2,1)} %copy.36) | data formatting | bytes 2097152 | tf_op jit(solution)/shard_map/dot_general | solution.py:70
  85.3 2.4 %fusion.6 = f32[2,256,576]{1,2,0:T(8,128)S(1)} fusion(bf16[2,256,1024]{2,1,0:T(8,128)(2,1)} %dot_general.18, bf16[1024,576]{0,1:T(8,128)(2,1)} %param.8), kind=kOutput, calls=%fused_computation.16 | convolution fusion | flops 603979776 | bytes 3407872 | tf_op jit(solution)/shard_map/dot_general | solution.py:70
  87.8 4.6 %collective-permute-start = (bf16[256,576]{0,1:T(8,128)(2,1)S(1)}, bf16[256,576]{0,1:T(8,128)(2,1)S(1)}, u32[]{:S(2)}, u32[]{:S(2)}) collective-permute-start(bf16[256,576]{0,1:T(8,128)(2,1)S(1)} %fusion.14), channel_id=1, source_target_pairs={{0,1},{1,0},{2,3},{3,2},{4,5},{5,4},{6,7},{7,6},{8,9},{9,8},{10,11... | collective-permute-start | bytes 884744 | tf_op jit(solution)/shard_map/ppermute | solution.py:73
  92.3 1.2 fusion.3
  93.5 1.4 convert_reduce_fusion.2
  95.1 0.9 copy.37
  96.0 4.8 %all-to-all-start.3 = ((bf16[32,8,576]{2,1,0:T(8,128)(2,1)}), bf16[32,8,576]{2,1,0:T(8,128)(2,1)S(1)}, u32[]{:S(2)}, u32[]{:S(2)}) async-start(bf16[32,8,576]{2,1,0:T(8,128)(2,1)} %bitcast.13), calls=%async_computation.3 | async-start | bytes 655360 | tf_op jit(solution)/shard_map/all_to_all | solution.py:17
  100.8 0.7 dynamic-slice_bitcast_fusion.6
  101.5 2.5 %collective-permute-start.1 = (bf16[512,128]{1,0:T(8,128)(2,1)}, bf16[512,128]{1,0:T(8,128)(2,1)S(1)}, u32[]{:S(2)}, u32[]{:S(2)}) collective-permute-start(bf16[512,128]{1,0:T(8,128)(2,1)} %get-tuple-element.27), channel_id=1, source_target_pairs={{0,64},{64,0},{128,192},{192,128},{256,320},{320,256},{384,448},{4... | collective-permute-start | bytes 393224 | tf_op jit(solution)/shard_map/ppermute | solution.py:31
  104.0 2.2 %collective-permute-start.3 = (bf16[512,128]{1,0:T(8,128)(2,1)S(1)}, bf16[512,128]{1,0:T(8,128)(2,1)S(1)}, u32[]{:S(2)}, u32[]{:S(2)}) collective-permute-start(bf16[512,128]{1,0:T(8,128)(2,1)S(1)} %get-tuple-element.28), channel_id=1, source_target_pairs={{0,192},{64,128},{128,320},{192,256},{256,448},{320,384},{384,64},... | collective-permute-start | bytes 393224 | tf_op jit(solution)/shard_map/ppermute | solution.py:31
  106.2 2.5 %collective-permute-start.2 = (bf16[512,128]{1,0:T(8,128)(2,1)S(1)}, bf16[512,128]{1,0:T(8,128)(2,1)}, u32[]{:S(2)}, u32[]{:S(2)}) collective-permute-start(bf16[512,128]{1,0:T(8,128)(2,1)S(1)} %get-tuple-element.29), channel_id=1, source_target_pairs={{0,128},{64,192},{128,256},{192,320},{256,384},{320,448},{384,0},{... | collective-permute-start | bytes 393224 | tf_op jit(solution)/shard_map/ppermute | solution.py:31
  108.7 0.6 divide_bitcast_fusion
  109.3 0.7 fusion.22
  110.6 1.4 collective-permute-done.1
  112.0 3.4 %collective-permute-done.3 = bf16[512,128]{1,0:T(8,128)(2,1)S(1)} collective-permute-done((bf16[512,128]{1,0:T(8,128)(2,1)S(1)}, bf16[512,128]{1,0:T(8,128)(2,1)S(1)}, u32[]{:S(2)}, u32[]{:S(2)}) %collective-permute-start.3) | collective-permute-done | bytes 131104 | tf_op jit(solution)/shard_map/ppermute | solution.py:31
  115.5 2.0 collective-permute-done.2
  117.4 1.0 fusion.21
  118.5 0.6 multiply_convert_fusion
  121.8 0.8 broadcast_in_dim.72
  122.5 11.6 %all-to-all-start.4 = ((bf16[32,8,640]{2,1,0:T(8,128)(2,1)}), bf16[32,8,640]{2,1,0:T(8,128)(2,1)S(1)}, u32[]{:S(2)}, u32[]{:S(2)}) async-start(bf16[32,8,640]{2,1,0:T(8,128)(2,1)} %broadcast_in_dim.72), calls=%async_computation.4 | async-start | bytes 655360 | tf_op jit(solution)/shard_map/all_to_all | solution.py:17
  134.2 2.5 %collective-permute-start.4 = (bf16[512,128]{1,0:T(8,128)(2,1)S(1)}, bf16[512,128]{1,0:T(8,128)(2,1)S(1)}, u32[]{:S(2)}, u32[]{:S(2)}) collective-permute-start(bf16[512,128]{1,0:T(8,128)(2,1)S(1)} %get-tuple-element.23), channel_id=1, source_target_pairs={{0,256},{64,320},{128,384},{192,448},{256,0},{320,64},{384,128},{4... | collective-permute-start | bytes 393224 | tf_op jit(solution)/shard_map/ppermute | solution.py:31
  136.7 2.4 %collective-permute-start.7 = (bf16[512,128]{1,0:T(8,128)(2,1)S(1)}, bf16[512,128]{1,0:T(8,128)(2,1)S(1)}, u32[]{:S(2)}, u32[]{:S(2)}) collective-permute-start(bf16[512,128]{1,0:T(8,128)(2,1)S(1)} %get-tuple-element.24), channel_id=1, source_target_pairs={{0,448},{64,384},{128,64},{192,0},{256,192},{320,128},{384,320},{4... | collective-permute-start | bytes 393224 | tf_op jit(solution)/shard_map/ppermute | solution.py:31
  139.1 4.7 %collective-permute-start.6 = (bf16[512,128]{1,0:T(8,128)(2,1)S(1)}, bf16[512,128]{1,0:T(8,128)(2,1)S(1)}, u32[]{:S(2)}, u32[]{:S(2)}) collective-permute-start(bf16[512,128]{1,0:T(8,128)(2,1)S(1)} %get-tuple-element.25), channel_id=1, source_target_pairs={{0,384},{64,448},{128,0},{192,64},{256,128},{320,192},{384,256},{4... | collective-permute-start | bytes 393224 | tf_op jit(solution)/shard_map/ppermute | solution.py:31
  143.8 2.8 %collective-permute-start.5 = (bf16[512,128]{1,0:T(8,128)(2,1)S(1)}, bf16[512,128]{1,0:T(8,128)(2,1)S(1)}, u32[]{:S(2)}, u32[]{:S(2)}) collective-permute-start(bf16[512,128]{1,0:T(8,128)(2,1)S(1)} %get-tuple-element.26), channel_id=1, source_target_pairs={{0,320},{64,256},{128,448},{192,384},{256,64},{320,0},{384,192},{4... | collective-permute-start | bytes 393224 | tf_op jit(solution)/shard_map/ppermute | solution.py:31
  146.6 0.5 iota_compare_fusion.2
  147.1 0.5 iota_compare_fusion
  147.7 4.2 %collective-permute-done.5 = bf16[512,128]{1,0:T(8,128)(2,1)S(1)} collective-permute-done((bf16[512,128]{1,0:T(8,128)(2,1)S(1)}, bf16[512,128]{1,0:T(8,128)(2,1)S(1)}, u32[]{:S(2)}, u32[]{:S(2)}) %collective-permute-start.5) | collective-permute-done | bytes 131104 | tf_op jit(solution)/shard_map/ppermute | solution.py:31
  152.2 5.1 %all_gather.7 = bf16[512,640]{0,1:T(8,128)(2,1)S(1)} all-gather(bf16[256,640]{0,1:T(8,128)(2,1)S(1)} %copy.38), channel_id=1, replica_groups=mesh['x'=4,'yl'=2,'z'=8,'yh'=4,'c'=2] {'c'}, dimensions={0}, use_global_device_ids=true | all-gather | bytes 983040 | tf_op jit(solution)/shard_map/all_gather | solution.py:88
  157.2 0.7 convert_reduce_fusion.4
  161.0 2.3 %fusion.5 = bf16[64,8,8,128]{3,1,2,0:T(8,128)(2,1)S(1)} fusion(bf16[1024,576]{0,1:T(8,128)(2,1)} %param.8, bf16[512,640]{0,1:T(8,128)(2,1)S(1)} %all_gather.7), kind=kOutput, calls=%fused_computation.15 | convolution fusion | flops 604504064 | bytes 2818048 | tf_op jit(solution)/shard_map/dot_general | solution.py:96
  163.3 0.3 copy.43
  163.6 0.3 copy.39
  163.9 0.4 copy-done.15
  164.4 1.1 pad_maximum_fusion.1
  165.4 3.6 %all-to-all-start.5 = ((bf16[8,528,128]{2,1,0:T(8,128)(2,1)}), bf16[8,528,128]{2,1,0:T(8,128)(2,1)S(1)}, u32[]{:S(2)}, u32[]{:S(2)}) async-start(bf16[8,528,128]{2,1,0:T(8,128)(2,1)} %pad_maximum_fusion.1), calls=%async_computation.5 | async-start | bytes 2162688 | tf_op jit(solution)/shard_map/all_to_all | solution.py:17
  169.0 15.8 %all-to-all-done.5 = bf16[8,528,128]{2,1,0:T(8,128)(2,1)S(1)} async-done(((bf16[8,528,128]{2,1,0:T(8,128)(2,1)}), bf16[8,528,128]{2,1,0:T(8,128)(2,1)S(1)}, u32[]{:S(2)}, u32[]{:S(2)}) %all-to-all-start.5) | async-done | bytes 1081376 | tf_op jit(solution)/shard_map/all_to_all | solution.py:17
  185.0 0.6 copy-done.6
  185.6 1.1 broadcast_in_dim.77
  186.8 3.9 %all-to-all-start.6 = ((bf16[8,512,128]{2,1,0:T(8,128)(2,1)}), bf16[8,512,128]{2,1,0:T(8,128)(2,1)S(1)}, u32[]{:S(2)}, u32[]{:S(2)}) async-start(bf16[8,512,128]{2,1,0:T(8,128)(2,1)} %broadcast_in_dim.77), calls=%async_computation.6 | async-start | bytes 2097152 | tf_op jit(solution)/shard_map/all_to_all | solution.py:17
  190.6 1.8 slice_reduce_fusion
  192.5 3.3 %fusion.2 = bf16[1024,576]{0,1:T(8,128)(2,1)} fusion(bf16[1024,576]{0,1:T(8,128)(2,1)} %param.8, f32[1024]{0:T(1024)S(1)} %copy-done.11, bf16[64,8,8,128]{3,2,1,0:T(8,128)(2,1)S(1)} %bitcast.97, bf16[512,640]{0,1:T(8,128)(2,1)} %copy-done.3), kind=kOutput, calls=%fused_computation.5 | convolution fusion | flops 606339072 | bytes 4001792 | tf_op jit(solution)/shard_map/dot_general | solution.py:106
  195.7 1.3 slice_reduce_fusion.1
  197.7 6.9 %all-to-all-done.6 = bf16[8,512,128]{2,1,0:T(8,128)(2,1)S(1)} async-done(((bf16[8,512,128]{2,1,0:T(8,128)(2,1)}), bf16[8,512,128]{2,1,0:T(8,128)(2,1)S(1)}, u32[]{:S(2)}, u32[]{:S(2)}) %all-to-all-start.6) | async-done | bytes 1048608 | tf_op jit(solution)/shard_map/all_to_all | solution.py:17
  204.6 0.7 copy.40
  205.3 0.8 reduce_sum.114
  206.1 2.9 %fusion.4 = bf16[576,1024]{1,0:T(8,128)(2,1)} fusion(bf16[512,576]{1,0:T(8,128)(2,1)} %copy-done.7, bf16[64,8,8,128]{3,2,1,0:T(8,128)(2,1)S(1)} %bitcast.102), kind=kOutput, calls=%fused_computation.14 | convolution fusion | flops 604569600 | bytes 2818048 | tf_op jit(solution)/shard_map/dot_general | solution.py:111
  (57 shorter events, 1.5 us)
Async XLA Ops:
  0.6 37.2 %copy-start = (bf16[576,1024]{1,0:T(8,128)(2,1)S(1)}, bf16[576,1024]{1,0:T(8,128)(2,1)}, u32[]{:S(2)}) copy-start(bf16[576,1024]{1,0:T(8,128)(2,1)} %param.6) | copy-start | bytes 3538948
  2.2 30.1 %all-to-all-start = ((bf16[32,8,576]{2,1,0:T(8,128)(2,1)}), bf16[32,8,576]{2,1,0:T(8,128)(2,1)S(1)}, u32[]{:S(2)}, u32[]{:S(2)}) async-start(bf16[32,8,576]{2,1,0:T(8,128)(2,1)} %broadcast_in_dim.65), calls=%async_computation | async-start | bytes 655360 | tf_op jit(solution)/shard_map/all_to_all | solution.py:17
  37.0 0.9 copy-start.7
  59.4 0.7 copy-start.9
  60.1 0.7 copy-start.4
  61.9 18.3 %all-to-all-start.2 = ((bf16[8,512,128]{2,1,0:T(8,128)(2,1)}), bf16[8,512,128]{2,1,0:T(8,128)(2,1)}, u32[]{:S(2)}, u32[]{:S(2)}) async-start(bf16[8,512,128]{2,1,0:T(8,128)(2,1)} %broadcast_in_dim.68), calls=%async_computation.2 | async-start | bytes 2097152 | tf_op jit(solution)/shard_map/all_to_all | solution.py:17
  87.8 7.2 %collective-permute-start = (bf16[256,576]{0,1:T(8,128)(2,1)S(1)}, bf16[256,576]{0,1:T(8,128)(2,1)S(1)}, u32[]{:S(2)}, u32[]{:S(2)}) collective-permute-start(bf16[256,576]{0,1:T(8,128)(2,1)S(1)} %fusion.14), channel_id=1, source_target_pairs={{0,1},{1,0},{2,3},{3,2},{4,5},{5,4},{6,7},{7,6},{8,9},{9,8},{10,11... | collective-permute-start | bytes 884744 | tf_op jit(solution)/shard_map/ppermute | solution.py:73
  94.9 5.8 %copy-start.1 = (bf16[8,512,128]{2,1,0:T(8,128)(2,1)S(1)}, bf16[8,512,128]{2,1,0:T(8,128)(2,1)}, u32[]{:S(2)}) copy-start(bf16[8,512,128]{2,1,0:T(8,128)(2,1)} %fusion.3) | copy-start | bytes 3145732
  95.0 14.2 %copy-start.5 = (bf16[512,128]{1,0:T(8,128)(2,1)S(1)}, bf16[512,128]{1,0:T(8,128)(2,1)}, u32[]{:S(2)}) copy-start(bf16[512,128]{1,0:T(8,128)(2,1)} %copy-done.4) | copy-start | bytes 393220
  96.0 22.5 %all-to-all-start.3 = ((bf16[32,8,576]{2,1,0:T(8,128)(2,1)}), bf16[32,8,576]{2,1,0:T(8,128)(2,1)S(1)}, u32[]{:S(2)}, u32[]{:S(2)}) async-start(bf16[32,8,576]{2,1,0:T(8,128)(2,1)} %bitcast.13), calls=%async_computation.3 | async-start | bytes 655360 | tf_op jit(solution)/shard_map/all_to_all | solution.py:17
  100.8 17.7 %copy-start.8 = (bf16[8,576]{1,0:T(8,128)(2,1)S(1)}, bf16[8,576]{1,0:T(8,128)(2,1)}, u32[]{:S(2)}) copy-start(bf16[8,576]{1,0:T(8,128)(2,1)} %param.5) | copy-start | bytes 27652
  100.8 17.7 %copy-start.10 = (f32[576]{0:T(1024)S(1)}, f32[576]{0:T(1024)}, u32[]{:S(2)}) copy-start(f32[576]{0:T(1024)} %param.9) | copy-start | bytes 6916
  100.8 20.8 %copy-start.12 = (pred[8]{0:T(512)(128)(4,1)S(1)}, pred[8]{0:T(512)(128)(4,1)}, u32[]{:S(2)}) copy-start(pred[8]{0:T(512)(128)(4,1)} %iota_compare_fusion.5) | copy-start | bytes 28
  100.8 20.8 %copy-start.13 = (pred[64]{0:T(512)(128)(4,1)S(1)}, pred[64]{0:T(512)(128)(4,1)}, u32[]{:S(2)}) copy-start(pred[64]{0:T(512)(128)(4,1)} %get-tuple-element.34) | copy-start | bytes 196
  100.8 20.8 %copy-start.14 = (pred[64]{0:T(512)(128)(4,1)S(1)}, pred[64]{0:T(512)(128)(4,1)}, u32[]{:S(2)}) copy-start(pred[64]{0:T(512)(128)(4,1)} %get-tuple-element.35) | copy-start | bytes 196
  101.5 10.5 %collective-permute-start.1 = (bf16[512,128]{1,0:T(8,128)(2,1)}, bf16[512,128]{1,0:T(8,128)(2,1)S(1)}, u32[]{:S(2)}, u32[]{:S(2)}) collective-permute-start(bf16[512,128]{1,0:T(8,128)(2,1)} %get-tuple-element.27), channel_id=1, source_target_pairs={{0,64},{64,0},{128,192},{192,128},{256,320},{320,256},{384,448},{4... | collective-permute-start | bytes 393224 | tf_op jit(solution)/shard_map/ppermute | solution.py:31
  104.0 11.5 %collective-permute-start.3 = (bf16[512,128]{1,0:T(8,128)(2,1)S(1)}, bf16[512,128]{1,0:T(8,128)(2,1)S(1)}, u32[]{:S(2)}, u32[]{:S(2)}) collective-permute-start(bf16[512,128]{1,0:T(8,128)(2,1)S(1)} %get-tuple-element.28), channel_id=1, source_target_pairs={{0,192},{64,128},{128,320},{192,256},{256,448},{320,384},{384,64},... | collective-permute-start | bytes 393224 | tf_op jit(solution)/shard_map/ppermute | solution.py:31
  106.2 11.2 %collective-permute-start.2 = (bf16[512,128]{1,0:T(8,128)(2,1)S(1)}, bf16[512,128]{1,0:T(8,128)(2,1)}, u32[]{:S(2)}, u32[]{:S(2)}) collective-permute-start(bf16[512,128]{1,0:T(8,128)(2,1)S(1)} %get-tuple-element.29), channel_id=1, source_target_pairs={{0,128},{64,192},{128,256},{192,320},{256,384},{320,448},{384,0},{... | collective-permute-start | bytes 393224 | tf_op jit(solution)/shard_map/ppermute | solution.py:31
  122.5 29.5 %all-to-all-start.4 = ((bf16[32,8,640]{2,1,0:T(8,128)(2,1)}), bf16[32,8,640]{2,1,0:T(8,128)(2,1)S(1)}, u32[]{:S(2)}, u32[]{:S(2)}) async-start(bf16[32,8,640]{2,1,0:T(8,128)(2,1)} %broadcast_in_dim.72), calls=%async_computation.4 | async-start | bytes 655360 | tf_op jit(solution)/shard_map/all_to_all | solution.py:17
  134.2 13.4 %collective-permute-start.4 = (bf16[512,128]{1,0:T(8,128)(2,1)S(1)}, bf16[512,128]{1,0:T(8,128)(2,1)S(1)}, u32[]{:S(2)}, u32[]{:S(2)}) collective-permute-start(bf16[512,128]{1,0:T(8,128)(2,1)S(1)} %get-tuple-element.23), channel_id=1, source_target_pairs={{0,256},{64,320},{128,384},{192,448},{256,0},{320,64},{384,128},{4... | collective-permute-start | bytes 393224 | tf_op jit(solution)/shard_map/ppermute | solution.py:31
  136.7 10.9 %collective-permute-start.7 = (bf16[512,128]{1,0:T(8,128)(2,1)S(1)}, bf16[512,128]{1,0:T(8,128)(2,1)S(1)}, u32[]{:S(2)}, u32[]{:S(2)}) collective-permute-start(bf16[512,128]{1,0:T(8,128)(2,1)S(1)} %get-tuple-element.24), channel_id=1, source_target_pairs={{0,448},{64,384},{128,64},{192,0},{256,192},{320,128},{384,320},{4... | collective-permute-start | bytes 393224 | tf_op jit(solution)/shard_map/ppermute | solution.py:31
  139.1 8.6 %collective-permute-start.6 = (bf16[512,128]{1,0:T(8,128)(2,1)S(1)}, bf16[512,128]{1,0:T(8,128)(2,1)S(1)}, u32[]{:S(2)}, u32[]{:S(2)}) collective-permute-start(bf16[512,128]{1,0:T(8,128)(2,1)S(1)} %get-tuple-element.25), channel_id=1, source_target_pairs={{0,384},{64,448},{128,0},{192,64},{256,128},{320,192},{384,256},{4... | collective-permute-start | bytes 393224 | tf_op jit(solution)/shard_map/ppermute | solution.py:31
  143.8 8.1 %collective-permute-start.5 = (bf16[512,128]{1,0:T(8,128)(2,1)S(1)}, bf16[512,128]{1,0:T(8,128)(2,1)S(1)}, u32[]{:S(2)}, u32[]{:S(2)}) collective-permute-start(bf16[512,128]{1,0:T(8,128)(2,1)S(1)} %get-tuple-element.26), channel_id=1, source_target_pairs={{0,320},{64,256},{128,448},{192,384},{256,64},{320,0},{384,192},{4... | collective-permute-start | bytes 393224 | tf_op jit(solution)/shard_map/ppermute | solution.py:31
  157.2 6.1 %copy-start.3 = (bf16[512,640]{0,1:T(8,128)(2,1)}, bf16[512,640]{0,1:T(8,128)(2,1)S(1)}, u32[]{:S(2)}) copy-start(bf16[512,640]{0,1:T(8,128)(2,1)S(1)} %all_gather.7) | copy-start | bytes 1966084
  163.6 0.7 copy-start.15
  163.6 0.7 copy-start.16
  163.6 0.7 copy-start.17
  165.4 19.4 %all-to-all-start.5 = ((bf16[8,528,128]{2,1,0:T(8,128)(2,1)}), bf16[8,528,128]{2,1,0:T(8,128)(2,1)S(1)}, u32[]{:S(2)}, u32[]{:S(2)}) async-start(bf16[8,528,128]{2,1,0:T(8,128)(2,1)} %pad_maximum_fusion.1), calls=%async_computation.5 | async-start | bytes 2162688 | tf_op jit(solution)/shard_map/all_to_all | solution.py:17
  184.9 0.7 copy-start.6
  186.8 5.7 %copy-start.2 = (bf16[8,64,8,128]{3,2,1,0:T(8,128)(2,1)S(1)}, bf16[8,64,8,128]{3,2,1,0:T(8,128)(2,1)}, u32[]{:S(2)}) copy-start(bf16[8,64,8,128]{3,2,1,0:T(8,128)(2,1)} %copy.36) | copy-start | bytes 3145732
  186.8 5.7 %copy-start.11 = (f32[1024]{0:T(1024)S(1)}, f32[1024]{0:T(1024)}, u32[]{:S(2)}) copy-start(f32[1024]{0:T(1024)} %get-tuple-element.21) | copy-start | bytes 12292
  186.8 17.9 %all-to-all-start.6 = ((bf16[8,512,128]{2,1,0:T(8,128)(2,1)}), bf16[8,512,128]{2,1,0:T(8,128)(2,1)S(1)}, u32[]{:S(2)}, u32[]{:S(2)}) async-start(bf16[8,512,128]{2,1,0:T(8,128)(2,1)} %broadcast_in_dim.77), calls=%async_computation.6 | async-start | bytes 2097152 | tf_op jit(solution)/shard_map/all_to_all | solution.py:17

commit v3 on v0

v3 whole, which is shorter than its diff:
```python
import jax
import jax.numpy as jnp
from jax import lax
from jax.experimental import pallas as pl
from jax.experimental.pallas import tpu as pltpu
from jax.sharding import Mesh, PartitionSpec as P

D = 4608
ROWS = 512
LAYER = ("x", "yl")
CHIPS = ("z", "yh")
LATENT = ("z", "yh", "c")
f32, bf16 = jnp.float32, jnp.bfloat16

penalty_weight = 0.5


def call(body, outs, *args, flops=0, smem=()):
    outs = [jax.ShapeDtypeStruct(shape, dtype) for shape, dtype in outs]
    size = sum(a.size * a.dtype.itemsize for a in args) + sum(o.size * o.dtype.itemsize for o in outs)
    return pl.pallas_call(
        body,
        out_shape=outs,
        in_specs=[
            pl.BlockSpec(memory_space=pltpu.SMEM if i in smem else pltpu.VMEM) for i in range(len(args))
        ],
        out_specs=[pl.BlockSpec(memory_space=pltpu.VMEM) for _ in outs],
        cost_estimate=pl.CostEstimate(flops=flops, bytes_accessed=size, transcendentals=0),
        compiler_params=pltpu.CompilerParams(vmem_limit_bytes=24 * 2**20),
    )(*args)


def matmul(a, b, dims):
    return lax.dot_general(a, b, (dims, ((), ())), preferred_element_type=f32)


def row_block(ref, lo, count):
    parts = [ref[pl.ds(lo, count), q * 64 : (q + 1) * 64, :].reshape(count * 64, 128) for q in range(8)]
    return jnp.concatenate(parts, axis=1)


def encode(rows_ref, w_ref, squares_ref, sent_ref, low_ref):
    rows = rows_ref[...]
    for n in range(4):
        part = matmul(rows, w_ref[:, n * 256 : (n + 1) * 256], ((1,), (0,)))
        high = part.astype(bf16)
        low = (part - high.astype(f32)).astype(bf16)
        for h in range(2):
            at = pl.ds((2 * n + h) * 64, 64)
            sent_ref[:, at, :] = high[:, h * 128 : (h + 1) * 128].reshape(8, 64, 128)
            low_ref[:, at, :] = low[:, h * 128 : (h + 1) * 128].reshape(8, 64, 128)
    sent_ref[:, 512:528, :] = jnp.broadcast_to(squares_ref[...][None], (8, 16, 128))


def activate(got_ref, bias_ref, acts_ref, pre_ref, norms_ref, penalty_ref):
    extra = jnp.sum(got_ref[:, 512:528, :].astype(f32), axis=0)
    norms = jnp.sqrt(extra[:8] + extra[8:] + 1e-06)
    norms_ref[...] = norms
    penalty = jnp.zeros((1, 128), f32)
    for q in range(8):
        at = pl.ds(q * 64, 64)
        pre = jnp.sum(got_ref[:, at, :].astype(f32), axis=0) + bias_ref[q : q + 1, :]
        pre_ref[at, :] = pre
        acts = jnp.maximum(pre, 0.0).astype(bf16)
        acts_ref[:, at, :] = jnp.broadcast_to(acts[None], (8, 64, 128))
        penalty = penalty + jnp.sum(acts.astype(f32), axis=0, keepdims=True) * norms[q : q + 1, :]
    penalty_ref[...] = penalty_weight * penalty


def decode(half_ref, acts_ref, w_ref, out_ref):
    acts = row_block(acts_ref, half_ref[0] * 4, 4)
    out_ref[...] = matmul(acts, w_ref[...], ((1,), (1,))).astype(out_ref.dtype)


def residue(got_ref, bias_ref, residual_ref, penalty_ref, out_ref):
    recon = jnp.sum(got_ref[...].astype(f32).reshape(32, 8, 576), axis=0) + bias_ref[...]
    err = recon - residual_ref[...]
    total = jnp.sum(err * err, axis=(0, 1), keepdims=True) + jnp.sum(penalty_ref[...], axis=(0, 1), keepdims=True)
    high = total.astype(bf16).astype(f32)
    row = lax.broadcasted_iota(jnp.int32, (8, 64), 0)
    lane = lax.broadcasted_iota(jnp.int32, (8, 64), 1)
    tail = jnp.where(row == 0, jnp.where(lane == 0, high, jnp.where(lane == 1, total - high, 0.0)), 0.0)
    block = jnp.concatenate([err / 8.0, tail], axis=1)
    out_ref[...] = jnp.broadcast_to(block[None], (32, 8, 640)).reshape(256, 640).astype(bf16)


def decode_back(err_ref, w_ref, sent_ref):
    err = err_ref[:, :576]
    lane = lax.broadcasted_iota(jnp.int32, (512, 128), 1)
    tail = jnp.where(lane >= 64, err_ref[:, 512:640].astype(f32), 0.0)
    total = jnp.sum(tail, axis=(0, 1), keepdims=True)
    high = total.astype(bf16).astype(f32)
    row = lax.broadcasted_iota(jnp.int32, (16, 128), 0)
    lane = lax.broadcasted_iota(jnp.int32, (16, 128), 1)
    tail = jnp.where(row == 0, jnp.where(lane == 0, high, jnp.where(lane == 1, total - high, 0.0)), 0.0)
    sent_ref[:, 512:528, :] = jnp.broadcast_to(tail.astype(bf16)[None], (8, 16, 128))
    for n in range(4):
        part = matmul(err, w_ref[:, n * 256 : (n + 1) * 256], ((1,), (0,))).astype(bf16)
        for h in range(2):
            at = pl.ds((2 * n + h) * 64, 64)
            sent_ref[:, at, :] = part[:, h * 128 : (h + 1) * 128].reshape(8, 64, 128)


def mask(got_ref, pre_ref, fine_ref, norms_ref, out_ref, loss_ref):
    for q in range(8):
        at = pl.ds(q * 64, 64)
        d_acts = jnp.sum(got_ref[:, at, :].astype(f32), axis=0)
        d_acts = d_acts + penalty_weight / 16.0 * norms_ref[q : q + 1, :]
        d_pre = jnp.where(pre_ref[at, :] + fine_ref[at, :] > 0, d_acts, 0.0).astype(bf16)
        out_ref[:, at, :] = jnp.broadcast_to(d_pre[None], (8, 64, 128))
    total = jnp.sum(got_ref[:, 512:528, :].astype(f32), axis=0)
    loss_ref[...] = jnp.sum(total, axis=(0, 1), keepdims=True) / (ROWS * D)


def decoder_gradient(acts_ref, err_ref, w_ref, norms_ref, out_ref, bias_ref):
    err = err_ref[:, :576]
    bias_ref[...] = jnp.sum(err.astype(f32), axis=0, keepdims=True)
    for n in range(4):
        at = slice(n * 256, (n + 1) * 256)
        acts = jnp.concatenate(
            [acts_ref[:, q * 64 : (q + 1) * 64, :].reshape(512, 128) for q in (2 * n, 2 * n + 1)], axis=1
        )
        norms = jnp.concatenate([norms_ref[q : q + 1, :] for q in (2 * n, 2 * n + 1)], axis=1)
        scale = penalty_weight / 16.0 * jnp.sum(acts.astype(f32), axis=0, keepdims=True) / norms
        outer = matmul(err, acts, ((0,), (0,)))
        out_ref[:, at] = (outer + scale * w_ref[:, at].astype(f32)).astype(bf16)


def encoder_gradient(rows_ref, d_pre_ref, out_ref, bias_ref):
    rows = rows_ref[...]
    for n in range(4):
        pair = [d_pre_ref[:, q * 64 : (q + 1) * 64, :].reshape(512, 128) for q in (2 * n, 2 * n + 1)]
        for h in range(2):
            bias_ref[2 * n + h : 2 * n + h + 1, :] = jnp.sum(pair[h].astype(f32), axis=0, keepdims=True)
        d_pre = jnp.concatenate(pair, axis=1)
        out_ref[:, n * 256 : (n + 1) * 256] = matmul(rows, d_pre, ((0,), (0,))).astype(bf16)


def exchange(blocks, axes):
    return lax.all_to_all(blocks, axes, 0, 0, tiled=True)


def block_at(array, at):
    return lax.dynamic_index_in_dim(array, at, 0, keepdims=False)


def split(value):
    high = lax.reduce_precision(value, exponent_bits=8, mantissa_bits=7)
    return high.astype(bf16), (value - high).astype(bf16)


def local(residual, w_enc, b_enc, w_dec, b_dec):
    core, at_x, at_y = lax.axis_index("c"), lax.axis_index("x"), lax.axis_index("yl")
    w_across = w_dec.T
    bias = b_enc.reshape(8, 128)
    work = 2 * 512 * 576 * 1024
    near = exchange(jnp.broadcast_to(residual[None], (32, 8, 576)), CHIPS).reshape(256, 576)
    rows_all = lax.all_gather(near, "c", axis=0, tiled=True)
    wide = w_across.astype(f32)
    squares = jnp.concatenate(split(jnp.sum(wide * wide, axis=0).reshape(8, 128)), axis=0)

    sent, low = call(encode, [((8, 528, 128), bf16), ((8, 512, 128), bf16)], rows_all, w_enc, squares, flops=work)
    acts, pre, norms, penalty = call(
        activate,
        [((8, 512, 128), bf16), ((512, 128), f32), ((8, 128), f32), ((1, 128), f32)],
        exchange(sent, LAYER),
        bias,
    )
    acts = exchange(acts, LAYER)

    half = core.astype(jnp.int32).reshape(1)
    other = call(decode, [((256, 576), bf16)], 1 - half, acts, w_across, flops=work // 2, smem=(0,))[0]
    other = lax.ppermute(other, "c", [(0, 1), (1, 0)])
    mine = call(decode, [((256, 576), f32)], half, acts, w_across, flops=work // 2, smem=(0,))[0]
    pair = (mine + other.astype(f32)).astype(bf16)

    pair, low = lax.optimization_barrier((pair, low))
    low = low.reshape(4, 1024, 128)
    away = at_x ^ 1
    over = jnp.stack([block_at(low, away), block_at(low, 3 - away)])
    over = lax.ppermute(over, "x", [(i, i ^ 1) for i in range(4)])
    recon, over = lax.optimization_barrier((exchange(pair.reshape(32, 8, 576), CHIPS), over))
    own = block_at(low, at_x).astype(f32) + over[0].astype(f32)
    mirror = (block_at(low, 3 - at_x).astype(f32) + over[1].astype(f32)).astype(bf16)

    packed = call(
        residue,
        [((256, 640), bf16)],
        recon.reshape(256, 576),
        b_dec.reshape(1, 576),
        residual.astype(f32),
        penalty,
    )[0]
    packed, mirror = lax.optimization_barrier((packed, mirror))
    mirror = lax.ppermute(mirror, "x", [(i, 3 - i) for i in range(4)])
    packed, mirror = lax.optimization_barrier((exchange(packed.reshape(32, 8, 640), CHIPS), mirror))
    err = lax.all_gather(packed.reshape(256, 640), "c", axis=0, tiled=True)

    sent = call(decode_back, [((8, 528, 128), bf16)], err, w_across, flops=work)[0]
    sent, mirror = lax.optimization_barrier((sent, mirror))
    own = (own + mirror.astype(f32)).reshape(2, 512, 128)
    fine = lax.ppermute(block_at(own, 1 - at_y).astype(bf16), "yl", [(0, 1), (1, 0)])
    fine = block_at(own, at_y) + fine.astype(f32)
    d_pre, loss = call(
        mask, [((8, 512, 128), bf16), ((1, 1), f32)], exchange(sent, LAYER), pre, fine, norms
    )
    grad_dec, grad_bdec = call(
        decoder_gradient, [((576, 1024), bf16), ((1, 576), f32)], acts, err, w_across, norms, flops=work
    )
    grad_enc, grad_benc = call(
        encoder_gradient, [((576, 1024), bf16), ((8, 128), f32)], rows_all, exchange(d_pre, LAYER), flops=work
    )
    return (
        grad_enc,
        grad_benc.astype(bf16).reshape(1024),
        grad_dec.T,
        grad_bdec.astype(bf16).reshape(576),
        loss.reshape(()),
    )


def solution(mesh):
    fine = Mesh(mesh.devices.reshape(4, 2, 8, 4, 2), ("x", "yl", "z", "yh", "c"))
    placed = (P(LATENT, LAYER), P(LAYER, LATENT), P(LATENT), P(LATENT, LAYER), P(LAYER))
    return jax.shard_map(
        local,
        mesh=fine,
        in_specs=placed,
        out_specs=(P(LAYER, LATENT), P(LATENT), P(LATENT, LAYER), P(LAYER), P()),
        check_vma=False,
    )
```

time: 882 us -> 190 us (0.22)
  waiting for transfers between devices: 632 us -> 72.2 us
  blocking collectives: 209 us -> 30.3 us
  starting transfers between devices: 0.12 us -> 57 us
  between operations: 17 us -> 0.88 us
  Pallas kernels: 0 us -> 12.2 us
  matrix products: 11.7 us -> 0 us
    psum x3 -> x0, waiting for transfers between devices: 632 us -> none  [the longest x1 537 us: local(): recon = lax.psum(recon_part, 'latent') + b_dec]
    psum x2 -> x0, blocking collectives: 117 us -> none  [the longest x1 100 us: local(): lax.psum(jnp.sum(err * err) * first_latent + penalty_part * first_layer,...]
    all_gather x1 -> x2, blocking collectives: 92.3 us -> 10.8 us  [the longest x1 6.09 us: local(): err = lax.all_gather(packed.reshape(256, 640), 'c', axis=0, tiled=True)]
    all_to_all x0 -> x6, starting transfers between devices: none -> 44.8 us  [exchange(): return lax.all_to_all(blocks, axes, 0, 0, tiled=True)]
    all_to_all x0 -> x6, waiting for transfers between devices: none -> 41.1 us  [exchange(): return lax.all_to_all(blocks, axes, 0, 0, tiled=True)]
    ppermute x0 -> x4, waiting for transfers between devices: none -> 31 us  [the longest x1 12.9 us: local(): over = lax.ppermute(over, 'x', [(i, i ^ 1) for i in range(4)])]
    all_to_all x0 -> x1, blocking collectives: none -> 19.5 us  [exchange(): return lax.all_to_all(blocks, axes, 0, 0, tiled=True)]
    pallas_call x0 -> x9, Pallas kernels: none -> 12.2 us  [call(): pl.pallas_call(body, out_shape=outs, in_specs=[pl.BlockSpec(memory_space=...]
  transfers between devices with their start and end apart: 3 -> 10, of which waited for: 3 -> 8; matrix products, arithmetic and copies ran while one was open for 1% -> 4% of each run, Pallas kernels for 0% -> 1%
where the time goes in v3:
time: 190 us; the launch traced here: 189 us
  waiting for transfers between devices  72.2 us (38%)
  starting transfers between devices  57 us (30%)
  blocking collectives  30.3 us (16%)
  Pallas kernels  12.2 us (6%)
  other arithmetic  9.4 us (5%)
  local copies, waits for them, and re-layouts  7.17 us (4%)
    all_to_all x6, starting transfers between devices, exchange(): return lax.all_to_all(blocks, axes, 0, 0, tiled=True)  44.8 us
    all_to_all x6, waiting for transfers between devices, exchange(): return lax.all_to_all(blocks, axes, 0, 0, tiled=True)  41.1 us
    all_to_all x1, blocking collectives, exchange(): return lax.all_to_all(blocks, axes, 0, 0, tiled=True)  19.5 us
    ppermute x1, waiting for transfers between devices, local(): over = lax.ppermute(over, 'x', [(i, i ^ 1) for i in range(4)])  12.9 us
    pallas_call x9, Pallas kernels, call(): pl.pallas_call(body, out_shape=outs, in_specs=[pl.BlockSpec(memory_space=...  12.2 us
    ppermute x1, waiting for transfers between devices, local(): lax.ppermute(block_at(own, 1 - at_y).astype(bf16), 'yl', [(0, 1), (1, 0)])  10.9 us
    ppermute x1, waiting for transfers between devices, local(): mirror = lax.ppermute(mirror, 'x', [(i, 3 - i) for i in range(4)])  6.59 us
    all_gather x1, blocking collectives, local(): err = lax.all_gather(packed.reshape(256, 640), 'c', axis=0, tiled=True)  6.09 us
  transfers between devices with their start and end apart: 10, of which 8 were waited for; matrix products, arithmetic and copies ran while one was open for 4% of the time, Pallas kernels for 1%

profile of v3, /device:TPU:1, one launch (start us, length us, event | category | flops | bytes accessed | tf_op | source)
XLA Modules:
  0.0 189.2 jit_solution(8449769868533245182)
XLA Ops:
  0.6 1.5 broadcast_in_dim.2
  2.1 16.5 %all-to-all-start = ((bf16[32,8,576]{2,1,0:T(8,128)(2,1)}), bf16[32,8,576]{2,1,0:T(8,128)(2,1)S(1)}, u32[]{:S(2)}, u32[]{:S(2)}) async-start(bf16[32,8,576]{2,1,0:T(8,128)(2,1)} %broadcast_in_dim.2), calls=%async_computation | async-start | bytes 655360 | tf_op jit(solution)/shard_map/all_to_all | solution.py:140
  18.6 0.0 copy-start.7
  18.6 1.6 multiply_reduce_fusion
  20.3 11.9 %all-to-all-done = bf16[32,8,576]{2,1,0:T(8,128)(2,1)S(1)} async-done(((bf16[32,8,576]{2,1,0:T(8,128)(2,1)}), bf16[32,8,576]{2,1,0:T(8,128)(2,1)S(1)}, u32[]{:S(2)}, u32[]{:S(2)}) %all-to-all-start) | async-done | bytes 294944 | tf_op jit(solution)/shard_map/all_to_all | solution.py:140
  32.2 4.7 %all_gather.6.rows_ref = bf16[512,576]{1,0:T(8,128)(2,1)S(1)} all-gather(bf16[256,576]{1,0:T(8,128)(2,1)S(1)} %bitcast.35), channel_id=1, replica_groups=mesh['x'=4,'yl'=2,'z'=8,'yh'=4,'c'=2] {'c'}, dimensions={0}, use_global_device_ids=true | all-gather | bytes 884736 | tf_op jit(solution)/shard_map/all_gather | solution.py:158
  36.9 0.0 copy-done.7
  36.9 1.0 shard_map.92
  37.9 0.0 copy-start.2
  37.9 1.0 copy-done.2
  38.9 0.0 copy-start.6
  38.9 19.5 %all_to_all.35.got_ref = bf16[8,528,128]{2,1,0:T(8,128)(2,1)S(1)} all-to-all(bf16[8,528,128]{2,1,0:T(8,128)(2,1)S(1)} %get-tuple-element.27), channel_id=1, replica_groups=mesh['x'=4,'yl'=2,'z'=8,'yh'=4,'c'=2] {'x','yl'}, dimensions={0} | all-to-all | bytes 2162688 | tf_op jit(solution)/shard_map/all_to_all | solution.py:140
  58.4 0.0 copy-done.4
  58.4 0.0 copy-done.6
  58.4 1.1 shard_map.93
  59.6 0.0 copy-start
  59.6 3.7 %all-to-all-start.2 = ((bf16[8,512,128]{2,1,0:T(8,128)(2,1)}), bf16[8,512,128]{2,1,0:T(8,128)(2,1)S(1)}, u32[]{:S(2)}, u32[]{:S(2)}) async-start(bf16[8,512,128]{2,1,0:T(8,128)(2,1)} %get-tuple-element.28), calls=%async_computation.2 | async-start | bytes 2097152 | tf_op jit(solution)/shard_map/all_to_all | solution.py:140
  63.3 13.9 %all-to-all-done.2.acts_ref = bf16[8,512,128]{2,1,0:T(8,128)(2,1)S(1)} async-done(((bf16[8,512,128]{2,1,0:T(8,128)(2,1)}), bf16[8,512,128]{2,1,0:T(8,128)(2,1)S(1)}, u32[]{:S(2)}, u32[]{:S(2)}) %all-to-all-start.2) | async-done | bytes 1048608 | tf_op jit(solution)/shard_map/all_to_all | solution.py:140
  77.2 0.0 copy-done
  77.2 0.6 shard_map.95
  77.8 4.5 %collective-permute-start = (bf16[256,576]{1,0:T(8,128)(2,1)S(1)}, bf16[256,576]{1,0:T(8,128)(2,1)S(1)}, u32[]{:S(2)}, u32[]{:S(2)}) collective-permute-start(bf16[256,576]{1,0:T(8,128)(2,1)S(1)} %shard_map.95), channel_id=1, source_target_pairs={{0,1},{1,0},{2,3},{3,2},{4,5},{5,4},{6,7},{7,6},{8,9},{9,8},{10,11... | collective-permute-start | bytes 884744 | tf_op jit(solution)/shard_map/ppermute | solution.py:173
  82.4 0.6 shard_map.94
  83.0 0.6 collective-permute-done
  83.6 0.8 add_convert_fusion
  84.4 4.8 %all-to-all-start.3 = ((bf16[32,8,576]{2,1,0:T(8,128)(2,1)}), bf16[32,8,576]{2,1,0:T(8,128)(2,1)S(1)}, u32[]{:S(2)}, u32[]{:S(2)}) async-start(bf16[32,8,576]{2,1,0:T(8,128)(2,1)} %bitcast.5), calls=%async_computation.3 | async-start | bytes 655360 | tf_op jit(solution)/shard_map/all_to_all | solution.py:140
  89.2 0.0 copy-start.10
  89.2 0.0 copy-start.11
  89.3 1.1 constant_dynamic-slice_fusion.1
  90.3 0.8 pad_maximum_fusion
  91.2 1.9 %collective-permute-start.1 = (bf16[2,1024,128]{2,1,0:T(8,128)(2,1)}, bf16[2,1024,128]{2,1,0:T(8,128)(2,1)S(1)}, u32[]{:S(2)}, u32[]{:S(2)}) collective-permute-start(bf16[2,1024,128]{2,1,0:T(8,128)(2,1)} %pad_maximum_fusion), channel_id=1, source_target_pairs={{0,128},{128,0},{256,384},{384,256},{1,129},{129,1},{257,385},{385... | collective-permute-start | bytes 1572872 | tf_op jit(solution)/shard_map/ppermute | solution.py:181
  93.1 0.0 copy-done.10
  93.1 0.0 copy-done.11
  93.1 12.9 %collective-permute-done.1 = bf16[2,1024,128]{2,1,0:T(8,128)(2,1)S(1)} collective-permute-done((bf16[2,1024,128]{2,1,0:T(8,128)(2,1)}, bf16[2,1024,128]{2,1,0:T(8,128)(2,1)S(1)}, u32[]{:S(2)}, u32[]{:S(2)}) %collective-permute-start.1) | collective-permute-done | bytes 524320 | tf_op jit(solution)/shard_map/ppermute | solution.py:181
  106.1 0.0 copy-start.9
  106.1 0.0 all-to-all-done.3
  106.1 1.9 %fusion = bf16[1024,128]{1,0:T(8,128)(2,1)} fusion(bf16[2,1024,128]{2,1,0:T(8,128)(2,1)S(1)} %collective-permute-done.1, bf16[4,1024,128]{2,1,0:T(8,128)(2,1)} %bitcast.32, s32[]{:T(128)S(6)} %select_n.22), kind=kLoop, calls=%fused_computation.5 | loop fusion | flops 524288 | bytes 786436 | tf_op jit(solution)/shard_map/convert_element_type | solution.py:184
  108.0 1.0 shard_map.96
  109.0 11.3 %all-to-all-start.4 = ((bf16[32,8,640]{2,1,0:T(8,128)(2,1)}), bf16[32,8,640]{2,1,0:T(8,128)(2,1)S(1)}, u32[]{:S(2)}, u32[]{:S(2)}) async-start(bf16[32,8,640]{2,1,0:T(8,128)(2,1)} %bitcast.9), calls=%async_computation.4 | async-start | bytes 655360 | tf_op jit(solution)/shard_map/all_to_all | solution.py:140
  120.3 2.5 %collective-permute-start.2 = (bf16[1024,128]{1,0:T(8,128)(2,1)}, bf16[1024,128]{1,0:T(8,128)(2,1)}, u32[]{:S(2)}, u32[]{:S(2)}) collective-permute-start(bf16[1024,128]{1,0:T(8,128)(2,1)} %fusion), channel_id=1, source_target_pairs={{0,384},{128,256},{256,128},{384,0},{1,385},{129,257},{257,129},{3... | collective-permute-start | bytes 786440 | tf_op jit(solution)/shard_map/ppermute | solution.py:195
  122.8 6.6 %collective-permute-done.2 = bf16[1024,128]{1,0:T(8,128)(2,1)} collective-permute-done((bf16[1024,128]{1,0:T(8,128)(2,1)}, bf16[1024,128]{1,0:T(8,128)(2,1)}, u32[]{:S(2)}, u32[]{:S(2)}) %collective-permute-start.2) | collective-permute-done | bytes 262176 | tf_op jit(solution)/shard_map/ppermute | solution.py:195
  129.4 3.4 %all-to-all-done.4 = bf16[32,8,640]{2,1,0:T(8,128)(2,1)S(1)} async-done(((bf16[32,8,640]{2,1,0:T(8,128)(2,1)}), bf16[32,8,640]{2,1,0:T(8,128)(2,1)S(1)}, u32[]{:S(2)}, u32[]{:S(2)}) %all-to-all-start.4) | async-done | bytes 327712 | tf_op jit(solution)/shard_map/all_to_all | solution.py:140
  132.8 0.0 copy-done.9
  132.8 0.7 copy-done.8
  133.5 6.1 %all_gather.7.err_ref = bf16[512,640]{1,0:T(8,128)(2,1)S(1)} all-gather(bf16[256,640]{1,0:T(8,128)(2,1)} %bitcast.36), channel_id=1, replica_groups=mesh['x'=4,'yl'=2,'z'=8,'yh'=4,'c'=2] {'c'}, dimensions={0}, use_global_device_ids=true | all-gather | bytes 983040 | tf_op jit(solution)/shard_map/all_gather | solution.py:197
  139.6 1.0 shard_map.97
  140.6 0.0 copy-start.1
  140.6 1.0 copy-done.1
  141.6 4.2 %all-to-all-start.5 = ((bf16[8,528,128]{2,1,0:T(8,128)(2,1)}), bf16[8,528,128]{2,1,0:T(8,128)(2,1)}, u32[]{:S(2)}, u32[]{:S(2)}) async-start(bf16[8,528,128]{2,1,0:T(8,128)(2,1)} %copy-done.1), calls=%async_computation.5 | async-start | bytes 2162688 | tf_op jit(solution)/shard_map/all_to_all | solution.py:140
  145.8 2.0 %bitcast_add_fusion = f32[1024,128]{1,0:T(8,128)} fusion(bf16[1024,128]{1,0:T(8,128)(2,1)} %collective-permute-done.2, bf16[2,1024,128]{2,1,0:T(8,128)(2,1)} %copy-done.9, bf16[4,1024,128]{2,1,0:T(8,128)(2,1)} %bitcast.33, s32[]{:T(128)S(6)} %select_n.23), kind=kLoop, calls=%fused_computation.3 | loop fusion | flops 655360 | bytes 1310724 | tf_op jit(solution)/shard_map/add | solution.py:201
  147.8 1.0 fusion.1
  148.8 3.2 %collective-permute-start.3 = (bf16[512,128]{1,0:T(8,128)(2,1)S(1)}, bf16[512,128]{1,0:T(8,128)(2,1)}, u32[]{:S(2)}, u32[]{:S(2)}) collective-permute-start(bf16[512,128]{1,0:T(8,128)(2,1)S(1)} %fusion.1), channel_id=1, source_target_pairs={{0,64},{64,0},{1,65},{65,1},{2,66},{66,2},{3,67},{67,3},{4,68},{68... | collective-permute-start | bytes 393224 | tf_op jit(solution)/shard_map/ppermute | solution.py:202
  152.1 10.9 %collective-permute-done.3 = bf16[512,128]{1,0:T(8,128)(2,1)} collective-permute-done((bf16[512,128]{1,0:T(8,128)(2,1)S(1)}, bf16[512,128]{1,0:T(8,128)(2,1)}, u32[]{:S(2)}, u32[]{:S(2)}) %collective-permute-start.3) | collective-permute-done | bytes 131104 | tf_op jit(solution)/shard_map/ppermute | solution.py:202
  163.0 1.0 bitcast_add_fusion.1.fine_ref
  164.0 0.0 all-to-all-done.5.got_ref
  164.0 2.0 %shard_map.98 = (bf16[8,512,128]{2,1,0:T(8,128)(2,1)S(1)}, f32[1,1]{1,0:T(1,128)}) custom-call(bf16[8,528,128]{2,1,0:T(8,128)(2,1)} %all-to-all-done.5.got_ref, f32[512,128]{1,0:T(8,128)S(1)} %get-tuple-element.40.pre_ref, f32[512,128]{1,0:T(8,128)S(1)} %bitcast_add_fusion.1.fine_ref, f32[8,128]{1,0:T(8,128)S(1)} %get-tuple-element.42.norms_ref), custom_call_target="tpu_custom_call" | custom-call | bytes 2658308 | tf_op jit(solution)/shard_map/pallas_call | solution.py:21
  166.1 1.0 copy-done.3
  167.0 4.2 %all-to-all-start.6 = ((bf16[8,512,128]{2,1,0:T(8,128)(2,1)}), bf16[8,512,128]{2,1,0:T(8,128)(2,1)}, u32[]{:S(2)}, u32[]{:S(2)}) async-start(bf16[8,512,128]{2,1,0:T(8,128)(2,1)} %copy-done.3), calls=%async_computation.6 | async-start | bytes 2097152 | tf_op jit(solution)/shard_map/all_to_all | solution.py:140
  171.3 0.0 copy-start.5
  171.3 1.8 shard_map.100
  173.1 0.6 convert_reduce_fusion
  173.7 11.8 %all-to-all-done.6.d_pre_ref = bf16[8,512,128]{2,1,0:T(8,128)(2,1)} async-done(((bf16[8,512,128]{2,1,0:T(8,128)(2,1)}), bf16[8,512,128]{2,1,0:T(8,128)(2,1)}, u32[]{:S(2)}, u32[]{:S(2)}) %all-to-all-start.6) | async-done | bytes 1048608 | tf_op jit(solution)/shard_map/all_to_all | solution.py:140
  185.5 0.0 copy-done.5
  185.5 3.0 %shard_map.99 = (bf16[576,1024]{1,0:T(8,128)(2,1)}, f32[8,128]{1,0:T(8,128)S(1)}) custom-call(bf16[512,576]{1,0:T(8,128)(2,1)S(1)} %copy-done.5, bf16[8,512,128]{2,1,0:T(8,128)(2,1)} %all-to-all-done.6.d_pre_ref), custom_call_target="tpu_custom_call" | custom-call | flops 603979776 | bytes 2822144 | tf_op jit(solution)/shard_map/pallas_call | solution.py:21
  188.6 0.6 convert_bitcast_fusion
  (7 shorter events, 0.0 us)
Async XLA Ops:
  2.1 30.1 %all-to-all-start = ((bf16[32,8,576]{2,1,0:T(8,128)(2,1)}), bf16[32,8,576]{2,1,0:T(8,128)(2,1)S(1)}, u32[]{:S(2)}, u32[]{:S(2)}) async-start(bf16[32,8,576]{2,1,0:T(8,128)(2,1)} %broadcast_in_dim.2), calls=%async_computation | async-start | bytes 655360 | tf_op jit(solution)/shard_map/all_to_all | solution.py:140
  18.6 18.3 %copy-start.7 = (bf16[576,1024]{1,0:T(8,128)(2,1)S(1)}, bf16[576,1024]{1,0:T(8,128)(2,1)}, u32[]{:S(2)}) copy-start(bf16[576,1024]{1,0:T(8,128)(2,1)} %w_ref.1) | copy-start | bytes 3538948
  36.9 21.5 %copy-start.4 = (bf16[512,576]{1,0:T(8,128)(2,1)}, bf16[512,576]{1,0:T(8,128)(2,1)S(1)}, u32[]{:S(2)}) copy-start(bf16[512,576]{1,0:T(8,128)(2,1)S(1)} %all_gather.6.rows_ref) | copy-start | bytes 1769476
  37.9 1.0 copy-start.2
  38.9 19.5 %copy-start.6 = (f32[1024]{0:T(1024)S(1)}, f32[1024]{0:T(1024)}, u32[]{:S(2)}) copy-start(f32[1024]{0:T(1024)} %param.7) | copy-start | bytes 12292
  59.6 17.7 %copy-start = (bf16[1024,576]{0,1:T(8,128)(2,1)S(1)}, bf16[1024,576]{0,1:T(8,128)(2,1)}, u32[]{:S(2)}) copy-start(bf16[1024,576]{0,1:T(8,128)(2,1)} %param.8) | copy-start | bytes 3538948
  59.6 17.7 %all-to-all-start.2 = ((bf16[8,512,128]{2,1,0:T(8,128)(2,1)}), bf16[8,512,128]{2,1,0:T(8,128)(2,1)S(1)}, u32[]{:S(2)}, u32[]{:S(2)}) async-start(bf16[8,512,128]{2,1,0:T(8,128)(2,1)} %get-tuple-element.28), calls=%async_computation.2 | async-start | bytes 2097152 | tf_op jit(solution)/shard_map/all_to_all | solution.py:140
  77.8 5.8 %collective-permute-start = (bf16[256,576]{1,0:T(8,128)(2,1)S(1)}, bf16[256,576]{1,0:T(8,128)(2,1)S(1)}, u32[]{:S(2)}, u32[]{:S(2)}) collective-permute-start(bf16[256,576]{1,0:T(8,128)(2,1)S(1)} %shard_map.95), channel_id=1, source_target_pairs={{0,1},{1,0},{2,3},{3,2},{4,5},{5,4},{6,7},{7,6},{8,9},{9,8},{10,11... | collective-permute-start | bytes 884744 | tf_op jit(solution)/shard_map/ppermute | solution.py:173
  84.4 21.7 %all-to-all-start.3 = ((bf16[32,8,576]{2,1,0:T(8,128)(2,1)}), bf16[32,8,576]{2,1,0:T(8,128)(2,1)S(1)}, u32[]{:S(2)}, u32[]{:S(2)}) async-start(bf16[32,8,576]{2,1,0:T(8,128)(2,1)} %bitcast.5), calls=%async_computation.3 | async-start | bytes 655360 | tf_op jit(solution)/shard_map/all_to_all | solution.py:140
  89.2 3.9 %copy-start.10 = (bf16[8,576]{1,0:T(8,128)(2,1)S(1)}, bf16[8,576]{1,0:T(8,128)(2,1)}, u32[]{:S(2)}) copy-start(bf16[8,576]{1,0:T(8,128)(2,1)} %param.5) | copy-start | bytes 27652
  89.2 3.9 %copy-start.11 = (f32[576]{0:T(1024)S(1)}, f32[576]{0:T(1024)}, u32[]{:S(2)}) copy-start(f32[576]{0:T(1024)} %param.9) | copy-start | bytes 6916
  91.2 14.9 %collective-permute-start.1 = (bf16[2,1024,128]{2,1,0:T(8,128)(2,1)}, bf16[2,1024,128]{2,1,0:T(8,128)(2,1)S(1)}, u32[]{:S(2)}, u32[]{:S(2)}) collective-permute-start(bf16[2,1024,128]{2,1,0:T(8,128)(2,1)} %pad_maximum_fusion), channel_id=1, source_target_pairs={{0,128},{128,0},{256,384},{384,256},{1,129},{129,1},{257,385},{385... | collective-permute-start | bytes 1572872 | tf_op jit(solution)/shard_map/ppermute | solution.py:181
  106.1 26.7 %copy-start.9 = (bf16[2,1024,128]{2,1,0:T(8,128)(2,1)}, bf16[2,1024,128]{2,1,0:T(8,128)(2,1)S(1)}, u32[]{:S(2)}) copy-start(bf16[2,1024,128]{2,1,0:T(8,128)(2,1)S(1)} %collective-permute-done.1) | copy-start | bytes 1572868
  109.0 23.8 %all-to-all-start.4 = ((bf16[32,8,640]{2,1,0:T(8,128)(2,1)}), bf16[32,8,640]{2,1,0:T(8,128)(2,1)S(1)}, u32[]{:S(2)}, u32[]{:S(2)}) async-start(bf16[32,8,640]{2,1,0:T(8,128)(2,1)} %bitcast.9), calls=%async_computation.4 | async-start | bytes 655360 | tf_op jit(solution)/shard_map/all_to_all | solution.py:140
  120.3 9.1 %collective-permute-start.2 = (bf16[1024,128]{1,0:T(8,128)(2,1)}, bf16[1024,128]{1,0:T(8,128)(2,1)}, u32[]{:S(2)}, u32[]{:S(2)}) collective-permute-start(bf16[1024,128]{1,0:T(8,128)(2,1)} %fusion), channel_id=1, source_target_pairs={{0,384},{128,256},{256,128},{384,0},{1,385},{129,257},{257,129},{3... | collective-permute-start | bytes 786440 | tf_op jit(solution)/shard_map/ppermute | solution.py:195
  132.8 0.7 copy-start.8
  140.6 1.0 copy-start.1
  141.6 22.4 %all-to-all-start.5 = ((bf16[8,528,128]{2,1,0:T(8,128)(2,1)}), bf16[8,528,128]{2,1,0:T(8,128)(2,1)}, u32[]{:S(2)}, u32[]{:S(2)}) async-start(bf16[8,528,128]{2,1,0:T(8,128)(2,1)} %copy-done.1), calls=%async_computation.5 | async-start | bytes 2162688 | tf_op jit(solution)/shard_map/all_to_all | solution.py:140
  148.8 14.1 %collective-permute-start.3 = (bf16[512,128]{1,0:T(8,128)(2,1)S(1)}, bf16[512,128]{1,0:T(8,128)(2,1)}, u32[]{:S(2)}, u32[]{:S(2)}) collective-permute-start(bf16[512,128]{1,0:T(8,128)(2,1)S(1)} %fusion.1), channel_id=1, source_target_pairs={{0,64},{64,0},{1,65},{65,1},{2,66},{66,2},{3,67},{67,3},{4,68},{68... | collective-permute-start | bytes 393224 | tf_op jit(solution)/shard_map/ppermute | solution.py:202
  166.1 1.0 copy-start.3
  167.0 18.5 %all-to-all-start.6 = ((bf16[8,512,128]{2,1,0:T(8,128)(2,1)}), bf16[8,512,128]{2,1,0:T(8,128)(2,1)}, u32[]{:S(2)}, u32[]{:S(2)}) async-start(bf16[8,512,128]{2,1,0:T(8,128)(2,1)} %copy-done.3), calls=%async_computation.6 | async-start | bytes 2097152 | tf_op jit(solution)/shard_map/all_to_all | solution.py:140
  171.3 14.2 %copy-start.5 = (bf16[512,576]{1,0:T(8,128)(2,1)S(1)}, bf16[512,576]{1,0:T(8,128)(2,1)}, u32[]{:S(2)}) copy-start(bf16[512,576]{1,0:T(8,128)(2,1)} %copy-done.4) | copy-start | bytes 1769476

commit v4 on v3

v4 whole, which is shorter than its diff:
```python
import math

import jax
import jax.numpy as jnp
from jax import lax
from jax.experimental import pallas as pl
from jax.experimental.pallas import tpu as pltpu
from jax.sharding import Mesh, PartitionSpec as P

D = 4608
ROWS = 512
LAYER = ("x", "yl")
TURNS = ("yl", "x")
CHIPS = ("z", "yh")
LATENT = ("z", "yh", "c")
f32, bf16 = jnp.float32, jnp.bfloat16

penalty_weight = 0.5


def call(body, outs, *args, flops=0, smem=(), far=(), far_in=(), scratch=()):
    outs = [pltpu.HBM(*o) if i in far else jax.ShapeDtypeStruct(*o) for i, o in enumerate(outs)]
    size = sum(math.prod(a.shape) * jnp.dtype(a.dtype).itemsize for a in list(args) + outs)

    args = [pltpu.with_memory_space_constraint(a, pltpu.HBM) if i in far_in else a for i, a in enumerate(args)]

    def space(i):
        return pltpu.SMEM if i in smem else pltpu.HBM if i in far_in else pltpu.VMEM

    return pl.pallas_call(
        body,
        out_shape=outs,
        in_specs=[pl.BlockSpec(memory_space=space(i)) for i in range(len(args))],
        out_specs=[pl.BlockSpec(memory_space=pltpu.HBM if i in far else pltpu.VMEM) for i in range(len(outs))],
        scratch_shapes=list(scratch),
        cost_estimate=pl.CostEstimate(flops=flops, bytes_accessed=size, transcendentals=0),
        compiler_params=pltpu.CompilerParams(vmem_limit_bytes=24 * 2**20),
    )(*args)


def copies(source, target, sem, pieces):
    return [pltpu.make_async_copy(source.at[at], target.at[at], sem.at[i]) for i, at in enumerate(pieces)]


def rows_of(lo, hi):
    return (slice(None), pl.ds(lo, hi - lo), slice(None))


def lanes_of(lo, hi):
    return (slice(None), pl.ds(lo, hi - lo))


def matmul(a, b, dims):
    return lax.dot_general(a, b, (dims, ((), ())), preferred_element_type=f32)


def row_block(ref, lo, count):
    parts = [ref[pl.ds(lo, count), q * 64 : (q + 1) * 64, :].reshape(count * 64, 128) for q in range(8)]
    return jnp.concatenate(parts, axis=1)


def spread_rows(rows_ref, out_ref):
    rows = rows_ref[...].astype(f32)
    out_ref[...] = jnp.broadcast_to(rows[None], (32, 8, 576)).reshape(256, 576).astype(bf16)


QUARTERS = [(0, 128), (128, 256), (256, 384), (384, 528)]


def encode(rows_ref, w_ref, squares_ref, sent_ref, low_ref, sent, low, sem, low_sem):
    out = copies(sent, sent_ref, sem, [rows_of(*at) for at in QUARTERS])
    low_out = copies(low, low_ref, low_sem, [rows_of(n * 128, n * 128 + 128) for n in range(4)])
    sent[:, 512:528, :] = jnp.broadcast_to(squares_ref[...][None], (8, 16, 128))
    rows = rows_ref[...]
    for n in range(4):
        part = matmul(rows, w_ref[:, n * 256 : (n + 1) * 256], ((1,), (0,)))
        high = part.astype(bf16)
        rest = (part - high.astype(f32)).astype(bf16)
        for h in range(2):
            at = pl.ds((2 * n + h) * 64, 64)
            sent[:, at, :] = high[:, h * 128 : (h + 1) * 128].reshape(8, 64, 128)
            low[:, at, :] = rest[:, h * 128 : (h + 1) * 128].reshape(8, 64, 128)
        out[n].start()
        low_out[n].start()
    for copy in out + low_out:
        copy.wait()


def arrange(to_ref, low_ref, *out_refs):
    for o, ref in enumerate(out_refs):
        half = pl.ds(256 * (o % 2), 256)
        for y in range(2):
            for slot in range(2):
                ref[y, slot] = low_ref[y * 4 + to_ref[2 * o + slot], half, :]


def add_first(keep_a, keep_b, got_a, got_b, own_ref, pass_a, pass_b):
    for h, (keep, got, over) in enumerate(((keep_a, got_a, pass_a), (keep_b, got_b, pass_b))):
        for y in range(2):
            own_ref[y, 256 * h : 256 * h + 256, :] = keep[y, 0].astype(f32) + got[y, 0].astype(f32)
            over[y] = (keep[y, 1].astype(f32) + got[y, 1].astype(f32)).astype(bf16)


def add_second(y_ref, own_ref, got_a, got_b, keep_ref, pass_ref):
    y = y_ref[0]
    for h, got in enumerate((got_a, got_b)):
        half = slice(256 * h, 256 * h + 256)
        keep_ref[half, :] = own_ref[y, half, :] + got[y].astype(f32)
        pass_ref[half, :] = (own_ref[1 - y, half, :] + got[1 - y].astype(f32)).astype(bf16)


EIGHTHS = [(q * 64, q * 64 + 64) for q in range(8)]


def activate(got_ref, bias_ref, out_ref, pre_out, norms_ref, penalty_ref, acts_ref, pre_ref, sem, pre_sem):
    out = copies(acts_ref, out_ref, sem, [rows_of(*at) for at in EIGHTHS])
    extra = jnp.sum(got_ref[:, 512:528, :].astype(f32), axis=0)
    norms = jnp.sqrt(extra[:8] + extra[8:] + 1e-06)
    norms_ref[...] = norms
    penalty = jnp.zeros((1, 128), f32)
    for q in range(8):
        at = pl.ds(q * 64, 64)
        pre = jnp.sum(got_ref[:, at, :].astype(f32), axis=0) + bias_ref[q : q + 1, :]
        pre_ref[at, :] = pre
        acts = jnp.maximum(pre, 0.0).astype(bf16)
        acts_ref[:, at, :] = jnp.broadcast_to(acts[None], (8, 64, 128))
        out[q].start()
        penalty = penalty + jnp.sum(acts.astype(f32), axis=0, keepdims=True) * norms[q : q + 1, :]
    last = pltpu.make_async_copy(pre_ref, pre_out, pre_sem)
    last.start()
    penalty_ref[...] = penalty_weight * penalty
    last.wait()
    for copy in out:
        copy.wait()


def decode(half_ref, acts_ref, w_ref, out_ref):
    acts = row_block(acts_ref, half_ref[0] * 4, 4)
    out_ref[...] = matmul(acts, w_ref[...], ((1,), (1,))).astype(out_ref.dtype)


def residue(got_ref, bias_ref, residual_ref, penalty_far, out_ref, penalty_ref, sem):
    copy = pltpu.make_async_copy(penalty_far, penalty_ref, sem)
    copy.start()
    recon = jnp.sum(got_ref[...].astype(f32).reshape(32, 8, 576), axis=0) + bias_ref[...]
    err = recon - residual_ref[...]
    copy.wait()
    total = jnp.sum(err * err, axis=(0, 1), keepdims=True) + jnp.sum(penalty_ref[...], axis=(0, 1), keepdims=True)
    high = total.astype(bf16).astype(f32)
    row = lax.broadcasted_iota(jnp.int32, (8, 64), 0)
    lane = lax.broadcasted_iota(jnp.int32, (8, 64), 1)
    tail = jnp.where(row == 0, jnp.where(lane == 0, high, jnp.where(lane == 1, total - high, 0.0)), 0.0)
    block = jnp.concatenate([err / 8.0, tail], axis=1)
    out_ref[...] = jnp.broadcast_to(block[None], (32, 8, 640)).reshape(256, 640).astype(bf16)


def decode_back(err_ref, w_ref, out_ref, sent_ref, sem):
    out = copies(sent_ref, out_ref, sem, [rows_of(*at) for at in QUARTERS])
    err = err_ref[:, :576]
    lane = lax.broadcasted_iota(jnp.int32, (512, 128), 1)
    tail = jnp.where(lane >= 64, err_ref[:, 512:640].astype(f32), 0.0)
    total = jnp.sum(tail, axis=(0, 1), keepdims=True)
    high = total.astype(bf16).astype(f32)
    row = lax.broadcasted_iota(jnp.int32, (16, 128), 0)
    lane = lax.broadcasted_iota(jnp.int32, (16, 128), 1)
    tail = jnp.where(row == 0, jnp.where(lane == 0, high, jnp.where(lane == 1, total - high, 0.0)), 0.0)
    sent_ref[:, 512:528, :] = jnp.broadcast_to(tail.astype(bf16)[None], (8, 16, 128))
    for n in range(4):
        part = matmul(err, w_ref[:, n * 256 : (n + 1) * 256], ((1,), (0,))).astype(bf16)
        for h in range(2):
            at = pl.ds((2 * n + h) * 64, 64)
            sent_ref[:, at, :] = part[:, h * 128 : (h + 1) * 128].reshape(8, 64, 128)
        out[n].start()
    for copy in out:
        copy.wait()


def mask(*refs):
    far_ref, pre_far, fine_far, rest_far, norms_ref, out_ref, loss_ref = refs[:7]
    got_ref, d_pre_ref, pre_ref, fine_ref, rest_ref, in_sem, sem, more_sem = refs[7:]
    more = [
        pltpu.make_async_copy(a, b, more_sem.at[i])
        for i, (a, b) in enumerate(((pre_far, pre_ref), (fine_far, fine_ref), (rest_far, rest_ref)))
    ]
    for copy in more:
        copy.start()
    into = copies(far_ref, got_ref, in_sem, [rows_of(*at) for at in EIGHTHS + [(512, 528)]])
    out = copies(d_pre_ref, out_ref, sem, [rows_of(*at) for at in EIGHTHS])
    for copy in into:
        copy.start()
    for copy in more:
        copy.wait()
    for q in range(8):
        at = pl.ds(q * 64, 64)
        exact = pre_ref[at, :] + (fine_ref[at, :] + rest_ref[at, :].astype(f32))
        into[q].wait()
        d_acts = jnp.sum(got_ref[:, at, :].astype(f32), axis=0)
        d_acts = d_acts + penalty_weight / 16.0 * norms_ref[q : q + 1, :]
        d_pre = jnp.where(exact > 0, d_acts, 0.0).astype(bf16)
        d_pre_ref[:, at, :] = jnp.broadcast_to(d_pre[None], (8, 64, 128))
        out[q].start()
    into[8].wait()
    total = jnp.sum(got_ref[:, 512:528, :].astype(f32), axis=0)
    loss_ref[...] = jnp.sum(total, axis=(0, 1), keepdims=True) / (ROWS * D)
    for copy in out:
        copy.wait()


def decoder_gradient(acts_ref, err_ref, w_ref, norms_ref, out_ref, bias_ref):
    err = err_ref[:, :576]
    bias_ref[...] = jnp.sum(err.astype(f32), axis=0, keepdims=True)
    for n in range(4):
        at = slice(n * 256, (n + 1) * 256)
        acts = jnp.concatenate(
            [acts_ref[:, q * 64 : (q + 1) * 64, :].reshape(512, 128) for q in (2 * n, 2 * n + 1)], axis=1
        )
        norms = jnp.concatenate([norms_ref[q : q + 1, :] for q in (2 * n, 2 * n + 1)], axis=1)
        scale = penalty_weight / 16.0 * jnp.sum(acts.astype(f32), axis=0, keepdims=True) / norms
        outer = matmul(err, acts, ((0,), (0,)))
        out_ref[:, at] = (outer + scale * w_ref[:, at].astype(f32)).astype(bf16)


def turn(rows_ref, out_ref):
    out_ref[...] = rows_ref[...].T


def encoder_gradient(*refs):
    across_far, far_ref, out_ref, bias_ref, across_ref, d_pre_ref, grad_ref, across_sem, in_sem, sem = refs
    first = pltpu.make_async_copy(across_far, across_ref, across_sem)
    first.start()
    into = copies(far_ref, d_pre_ref, in_sem, [rows_of(n * 128, n * 128 + 128) for n in range(4)])
    out = copies(grad_ref, out_ref, sem, [lanes_of(n * 256, n * 256 + 256) for n in range(4)])
    for copy in into:
        copy.start()
    first.wait()
    across = across_ref[...]
    sums = []
    for n in range(4):
        into[n].wait()
        pair = [d_pre_ref[:, q * 64 : (q + 1) * 64, :].reshape(512, 128) for q in (2 * n, 2 * n + 1)]
        d_pre = jnp.concatenate(pair, axis=1)
        grad_ref[:, n * 256 : (n + 1) * 256] = matmul(across, d_pre, ((1,), (0,))).astype(bf16)
        out[n].start()
        sums += [jnp.sum(part.astype(f32), axis=0, keepdims=True) for part in pair]
    bias_ref[...] = jnp.concatenate(sums, axis=0).astype(bf16)
    for copy in out:
        copy.wait()


def exchange(blocks, axes):
    return lax.all_to_all(blocks, axes, 0, 0, tiled=True)


def split(value):
    high = lax.reduce_precision(value, exponent_bits=8, mantissa_bits=7)
    return high.astype(bf16), (value - high).astype(bf16)


def local(residual, w_enc, b_enc, w_dec, b_dec):
    core, at_x, at_y = lax.axis_index("c"), lax.axis_index("x"), lax.axis_index("yl")
    w_across = w_dec.T
    bias = b_enc.reshape(8, 128)
    work = 2 * 512 * 576 * 1024
    block = pltpu.VMEM((8, 528, 128), bf16)
    wide = pltpu.VMEM((8, 512, 128), bf16)
    sems = pltpu.SemaphoreType.DMA
    near = call(spread_rows, [((256, 576), bf16)], residual)[0]
    near = exchange(near.reshape(32, 8, 576), CHIPS).reshape(256, 576)
    rows_all = lax.all_gather(near, "c", axis=0, tiled=True)
    w_wide = w_across.astype(f32)
    squares = jnp.concatenate(split(jnp.sum(w_wide * w_wide, axis=0).reshape(8, 128)), axis=0)

    sent, low = call(
        encode,
        [((8, 528, 128), bf16), ((8, 512, 128), bf16)],
        rows_all,
        w_enc,
        squares,
        flops=work,
        far=(0, 1),
        scratch=(block, wide, sems((4,)), sems((4,))),
    )
    acts, pre, norms, penalty = call(
        activate,
        [((8, 512, 128), bf16), ((512, 128), f32), ((8, 128), f32), ((1, 128), f32)],
        exchange(sent, TURNS),
        bias,
        far=(0, 1),
        scratch=(wide, pltpu.VMEM((512, 128), f32), sems((8,)), sems),
    )
    near_x, far_x = at_x ^ 1, 3 - at_x
    to = jnp.stack([near_x, 3 - near_x, far_x, far_x ^ 1, at_x, far_x, at_x, near_x]).astype(jnp.int32)
    piece = ((2, 2, 256, 128), bf16)
    over_a, over_b, keep_a, keep_b = call(arrange, [piece] * 4, to, low, smem=(0,))
    acts, over_a, over_b = lax.optimization_barrier((exchange(acts, TURNS), over_a, over_b))

    half = core.astype(jnp.int32).reshape(1)
    other = call(decode, [((256, 576), bf16)], 1 - half, acts, w_across, flops=work // 2, smem=(0,))[0]
    other = lax.ppermute(other, "c", [(0, 1), (1, 0)])
    mine = call(decode, [((256, 576), f32)], half, acts, w_across, flops=work // 2, smem=(0,))[0]
    pair = (mine + other.astype(f32)).astype(bf16)

    by_near = [(i, i ^ 1) for i in range(4)]
    by_far = [(i, 3 - i) for i in range(4)]
    pair, over_a, over_b = lax.optimization_barrier((pair, over_a, over_b))
    over_a = lax.ppermute(over_a, "x", by_near)
    over_b = lax.ppermute(over_b, "x", by_far)
    recon, over_a, over_b = lax.optimization_barrier((exchange(pair.reshape(32, 8, 576), CHIPS), over_a, over_b))
    packed = call(
        residue,
        [((256, 640), bf16)],
        recon.reshape(256, 576),
        b_dec.reshape(1, 576),
        residual.astype(f32),
        penalty,
        far_in=(3,),
        scratch=(pltpu.VMEM((1, 128), f32), sems),
    )[0]
    packed, over_a, over_b = lax.optimization_barrier((packed, over_a, over_b))
    part = ((2, 256, 128), bf16)
    own, over_a, over_b = call(add_first, [((2, 512, 128), f32), part, part], keep_a, keep_b, over_a, over_b)
    over_a = lax.ppermute(over_a, "x", by_far)
    over_b = lax.ppermute(over_b, "x", by_near)
    packed = exchange(packed.reshape(32, 8, 640), CHIPS).reshape(256, 640)
    err = lax.all_gather(packed, "c", axis=0, tiled=True)
    err, over_a, over_b = lax.optimization_barrier((err, over_a, over_b))

    sent = call(
        decode_back,
        [((8, 528, 128), bf16)],
        err,
        w_across,
        flops=work,
        far=(0,),
        scratch=(block, sems((4,))),
    )[0]
    sent, over_a, over_b = lax.optimization_barrier((sent, over_a, over_b))
    fine, rest = call(
        add_second,
        [((512, 128), f32), ((512, 128), bf16)],
        at_y.astype(jnp.int32).reshape(1),
        own,
        over_a,
        over_b,
        smem=(0,),
    )
    rest = lax.ppermute(rest, "yl", [(0, 1), (1, 0)])
    d_pre, loss = call(
        mask,
        [((8, 512, 128), bf16), ((1, 1), f32)],
        exchange(sent, TURNS),
        pre,
        fine,
        rest,
        norms,
        far=(0,),
        far_in=(0, 1, 2, 3),
        scratch=(
            block,
            wide,
            pltpu.VMEM((512, 128), f32),
            pltpu.VMEM((512, 128), f32),
            pltpu.VMEM((512, 128), bf16),
            sems((9,)),
            sems((8,)),
            sems((3,)),
        ),
    )
    grad_dec, grad_bdec = call(
        decoder_gradient, [((576, 1024), bf16), ((1, 576), f32)], acts, err, w_across, norms, flops=work
    )
    across = call(turn, [((576, 512), bf16)], rows_all)[0]
    grad_enc, grad_benc = call(
        encoder_gradient,
        [((576, 1024), bf16), ((8, 128), bf16)],
        across,
        exchange(d_pre, TURNS),
        flops=work,
        far=(0,),
        far_in=(0, 1),
        scratch=(
            pltpu.VMEM((576, 512), bf16),
            wide,
            pltpu.VMEM((576, 1024), bf16),
            sems,
            sems((4,)),
            sems((4,)),
        ),
    )
    return (
        grad_enc,
        grad_benc.reshape(1024),
        grad_dec.T,
        grad_bdec.astype(bf16).reshape(576),
        loss.reshape(()),
    )


def solution(mesh):
    fine = Mesh(mesh.devices.reshape(4, 2, 8, 4, 2), ("x", "yl", "z", "yh", "c"))
    placed = (P(LATENT, LAYER), P(LAYER, LATENT), P(LATENT), P(LATENT, LAYER), P(LAYER))
    return jax.shard_map(
        local,
        mesh=fine,
        in_specs=placed,
        out_specs=(P(LAYER, LATENT), P(LATENT), P(LATENT, LAYER), P(LAYER), P()),
        check_vma=False,
    )
```

time: 190 us -> 186 us (0.979)
  waiting for transfers between devices: 72.2 us -> 53.2 us
  Pallas kernels: 12.2 us -> 20.7 us
  other arithmetic: 9.4 us -> 3.05 us
  starting transfers between devices: 57 us -> 63 us
  local copies, waits for them, and re-layouts: 7.17 us -> 12.6 us
    ppermute x3 -> x5, waiting for transfers between devices: 30.4 us -> 16.8 us  [the longest x1 10.5 us: local(): rest = lax.ppermute(rest, 'yl', [(0, 1), (1, 0)])]
    unnamed x24 -> x46, local copies, waits for them, and re-layouts: 3.67 us -> 12.5 us
    pallas_call x9 -> x14, Pallas kernels: 12.2 us -> 20.7 us  [call(): pl.pallas_call(body, out_shape=outs, in_specs=[pl.BlockSpec(memory_space=...]
    ppermute x3 -> x5, starting transfers between devices: 7.63 us -> 13.9 us  [the longest x1 3.25 us: local(): rest = lax.ppermute(rest, 'yl', [(0, 1), (1, 0)])]
    all_to_all x6, waiting for transfers between devices: 41.1 us -> 35.8 us  [exchange(): return lax.all_to_all(blocks, axes, 0, 0, tiled=True)]
    add x2 -> x0, other arithmetic: 3.05 us -> none  [the longest x1 2.01 us: local(): own = (own + mirror.astype(f32)).reshape(2, 512, 128)]
  transfers between devices with their start and end apart: 10 -> 12, of which waited for: 8 -> 8; matrix products, arithmetic and copies ran while one was open for 4% -> 1% of each run, Pallas kernels for 1% -> 3%
where the time goes in v4:
time: 186 us; the launch traced here: 184 us
  starting transfers between devices  63 us (34%)
  waiting for transfers between devices  53.2 us (29%)
  blocking collectives  30.9 us (17%)
  Pallas kernels  20.7 us (11%)
  local copies, waits for them, and re-layouts  12.6 us (7%)
  other arithmetic  3.05 us (2%)
    all_to_all x6, starting transfers between devices, exchange(): return lax.all_to_all(blocks, axes, 0, 0, tiled=True)  45 us
    all_to_all x6, waiting for transfers between devices, exchange(): return lax.all_to_all(blocks, axes, 0, 0, tiled=True)  35.8 us
    pallas_call x14, Pallas kernels, call(): pl.pallas_call(body, out_shape=outs, in_specs=[pl.BlockSpec(memory_space=...  20.7 us
    all_to_all x1, blocking collectives, exchange(): return lax.all_to_all(blocks, axes, 0, 0, tiled=True)  19.6 us
    unnamed x46, local copies, waits for them, and re-layouts  12.5 us
    ppermute x1, waiting for transfers between devices, local(): rest = lax.ppermute(rest, 'yl', [(0, 1), (1, 0)])  10.5 us
    all_gather x1, blocking collectives, local(): err = lax.all_gather(packed, 'c', axis=0, tiled=True)  6.62 us
    all_gather x1, blocking collectives, local(): rows_all = lax.all_gather(near, 'c', axis=0, tiled=True)  4.67 us
  transfers between devices with their start and end apart: 12, of which 8 were waited for; matrix products, arithmetic and copies ran while one was open for 1% of the time, Pallas kernels for 3%

profile of v4, /device:TPU:1, one launch (start us, length us, event | category | flops | bytes accessed | tf_op | source)
XLA Modules:
  0.0 184.5 jit_solution(13652580252277827865)
XLA Ops:
  0.6 0.0 copy-start.14
  0.6 0.7 copy-done.14
  1.3 0.8 shard_map.92
  2.1 16.5 %all-to-all-start = ((bf16[32,8,576]{2,1,0:T(8,128)(2,1)}), bf16[32,8,576]{2,1,0:T(8,128)(2,1)S(1)}, u32[]{:S(2)}, u32[]{:S(2)}) async-start(bf16[32,8,576]{2,1,0:T(8,128)(2,1)} %bitcast), calls=%async_computation | async-start | bytes 655360 | tf_op jit(solution)/shard_map/all_to_all | solution.py:251
  18.6 0.0 copy-start.18
  18.6 1.6 multiply_reduce_fusion
  20.3 11.9 %all-to-all-done = bf16[32,8,576]{2,1,0:T(8,128)(2,1)S(1)} async-done(((bf16[32,8,576]{2,1,0:T(8,128)(2,1)}), bf16[32,8,576]{2,1,0:T(8,128)(2,1)S(1)}, u32[]{:S(2)}, u32[]{:S(2)}) %all-to-all-start) | async-done | bytes 294944 | tf_op jit(solution)/shard_map/all_to_all | solution.py:251
  32.2 4.7 %all_gather.6.rows_ref = bf16[512,576]{1,0:T(8,128)(2,1)S(1)} all-gather(bf16[256,576]{1,0:T(8,128)(2,1)S(1)} %bitcast.30), channel_id=1, replica_groups=mesh['x'=4,'yl'=2,'z'=8,'yh'=4,'c'=2] {'c'}, dimensions={0}, use_global_device_ids=true | all-gather | bytes 884736 | tf_op jit(solution)/shard_map/all_gather | solution.py:269
  36.9 2.1 %shard_map.94 = (bf16[8,528,128]{2,1,0:T(8,128)(2,1)}, bf16[8,512,128]{2,1,0:T(8,128)(2,1)}) custom-call(bf16[512,576]{1,0:T(8,128)(2,1)S(1)} %all_gather.6.rows_ref, bf16[576,1024]{1,0:T(8,128)(2,1)S(1)} %copy-done.18, bf16[16,128]{1,0:T(8,128)(2,1)S(1)} %pad_maximum_fusion.squares_ref), custom_call_target="tpu_custom_call" | custom-call | flops 603979776 | bytes 3903488 | tf_op jit(solution)/shard_map/pallas_call | solution.py:30
  39.0 0.0 copy-start.16
  39.0 19.6 %all_to_all.35.got_ref = bf16[8,528,128]{2,1,0:T(8,128)(2,1)S(1)} all-to-all(bf16[8,528,128]{2,1,0:T(8,128)(2,1)} %get-tuple-element.44), channel_id=1, replica_groups=mesh['x'=4,'yl'=2,'z'=8,'yh'=4,'c'=2] {'yl','x'}, dimensions={0} | all-to-all | bytes 2162688 | tf_op jit(solution)/shard_map/all_to_all | solution.py:251
  58.6 1.1 shard_map.95
  59.8 0.0 copy-start.17
  59.8 0.0 copy-start
  59.8 3.7 %all-to-all-start.2 = ((bf16[8,512,128]{2,1,0:T(8,128)(2,1)}), bf16[8,512,128]{2,1,0:T(8,128)(2,1)S(1)}, u32[]{:S(2)}, u32[]{:S(2)}) async-start(bf16[8,512,128]{2,1,0:T(8,128)(2,1)} %get-tuple-element.45), calls=%async_computation.2 | async-start | bytes 2097152 | tf_op jit(solution)/shard_map/all_to_all | solution.py:251
  63.5 0.1 stack.26.to_ref
  63.6 1.2 copy-done.1
  64.8 0.6 shard_map.96
  65.5 0.0 copy-start.5
  65.5 0.7 copy-done.5
  66.2 0.7 copy-done.19
  66.9 0.7 copy-done.20
  67.6 9.4 %all-to-all-done.2.acts_ref = bf16[8,512,128]{2,1,0:T(8,128)(2,1)S(1)} async-done(((bf16[8,512,128]{2,1,0:T(8,128)(2,1)}), bf16[8,512,128]{2,1,0:T(8,128)(2,1)S(1)}, u32[]{:S(2)}, u32[]{:S(2)}) %all-to-all-start.2) | async-done | bytes 1048608 | tf_op jit(solution)/shard_map/all_to_all | solution.py:251
  77.0 0.6 shard_map.98
  77.7 4.0 %collective-permute-start = (bf16[256,576]{1,0:T(8,128)(2,1)S(1)}, bf16[256,576]{1,0:T(8,128)(2,1)S(1)}, u32[]{:S(2)}, u32[]{:S(2)}) collective-permute-start(bf16[256,576]{1,0:T(8,128)(2,1)S(1)} %shard_map.98), channel_id=1, source_target_pairs={{0,1},{1,0},{2,3},{3,2},{4,5},{5,4},{6,7},{7,6},{8,9},{9,8},{10,11... | collective-permute-start | bytes 884744 | tf_op jit(solution)/shard_map/ppermute | solution.py:299
  81.7 0.6 shard_map.97
  82.3 0.0 copy-start.22
  82.4 0.6 collective-permute-done
  83.0 0.8 add_convert_fusion
  83.8 4.9 %all-to-all-start.3 = ((bf16[32,8,576]{2,1,0:T(8,128)(2,1)}), bf16[32,8,576]{2,1,0:T(8,128)(2,1)S(1)}, u32[]{:S(2)}, u32[]{:S(2)}) async-start(bf16[32,8,576]{2,1,0:T(8,128)(2,1)} %bitcast.28), calls=%async_computation.3 | async-start | bytes 655360 | tf_op jit(solution)/shard_map/all_to_all | solution.py:251
  88.7 2.5 %collective-permute-start.1 = (bf16[2,2,256,128]{3,2,1,0:T(8,128)(2,1)}, bf16[2,2,256,128]{3,2,1,0:T(8,128)(2,1)S(1)}, u32[]{:S(2)}, u32[]{:S(2)}) collective-permute-start(bf16[2,2,256,128]{3,2,1,0:T(8,128)(2,1)} %copy-done.20), channel_id=1, source_target_pairs={{0,128},{128,0},{256,384},{384,256},{1,129},{129,1},{257,385},{385... | collective-permute-start | bytes 786440 | tf_op jit(solution)/shard_map/ppermute | solution.py:306
  91.2 3.1 %collective-permute-start.2 = (bf16[2,2,256,128]{3,2,1,0:T(8,128)(2,1)}, bf16[2,2,256,128]{3,2,1,0:T(8,128)(2,1)S(1)}, u32[]{:S(2)}, u32[]{:S(2)}) collective-permute-start(bf16[2,2,256,128]{3,2,1,0:T(8,128)(2,1)} %copy-done.19), channel_id=1, source_target_pairs={{0,384},{128,256},{256,128},{384,0},{1,385},{129,257},{257,129},{3... | collective-permute-start | bytes 786440 | tf_op jit(solution)/shard_map/ppermute | solution.py:307
  94.4 3.6 %collective-permute-done.1.got_a = bf16[2,2,256,128]{3,2,1,0:T(8,128)(2,1)S(1)} collective-permute-done((bf16[2,2,256,128]{3,2,1,0:T(8,128)(2,1)}, bf16[2,2,256,128]{3,2,1,0:T(8,128)(2,1)S(1)}, u32[]{:S(2)}, u32[]{:S(2)}) %collective-permute-start.1) | collective-permute-done | bytes 262176 | tf_op jit(solution)/shard_map/ppermute | solution.py:306
  98.0 0.7 copy-done.9
  98.7 2.7 %collective-permute-done.2.got_b = bf16[2,2,256,128]{3,2,1,0:T(8,128)(2,1)S(1)} collective-permute-done((bf16[2,2,256,128]{3,2,1,0:T(8,128)(2,1)}, bf16[2,2,256,128]{3,2,1,0:T(8,128)(2,1)S(1)}, u32[]{:S(2)}, u32[]{:S(2)}) %collective-permute-start.2) | collective-permute-done | bytes 262176 | tf_op jit(solution)/shard_map/ppermute | solution.py:307
  101.4 0.7 copy-done.11
  102.1 1.6 shard_map.99
  103.7 11.3 %all-to-all-start.4 = ((bf16[32,8,640]{2,1,0:T(8,128)(2,1)}), bf16[32,8,640]{2,1,0:T(8,128)(2,1)S(1)}, u32[]{:S(2)}, u32[]{:S(2)}) async-start(bf16[32,8,640]{2,1,0:T(8,128)(2,1)} %bitcast.13), calls=%async_computation.4 | async-start | bytes 655360 | tf_op jit(solution)/shard_map/all_to_all | solution.py:251
  115.1 0.9 copy-done.8
  116.0 0.9 copy-done.10
  117.0 0.9 copy-done.12
  117.9 0.7 shard_map.100
  118.7 0.8 copy-done.3
  119.4 3.1 %collective-permute-start.3 = (bf16[2,256,128]{2,1,0:T(8,128)(2,1)}, bf16[2,256,128]{2,1,0:T(8,128)(2,1)}, u32[]{:S(2)}, u32[]{:S(2)}) collective-permute-start(bf16[2,256,128]{2,1,0:T(8,128)(2,1)} %get-tuple-element.64), channel_id=1, source_target_pairs={{0,384},{128,256},{256,128},{384,0},{1,385},{129,257},{257,129},{3... | collective-permute-start | bytes 393224 | tf_op jit(solution)/shard_map/ppermute | solution.py:322
  122.6 1.9 %collective-permute-start.4 = (bf16[2,256,128]{2,1,0:T(8,128)(2,1)}, bf16[2,256,128]{2,1,0:T(8,128)(2,1)}, u32[]{:S(2)}, u32[]{:S(2)}) collective-permute-start(bf16[2,256,128]{2,1,0:T(8,128)(2,1)} %get-tuple-element.65), channel_id=1, source_target_pairs={{0,128},{128,0},{256,384},{384,256},{1,129},{129,1},{257,385},{385... | collective-permute-start | bytes 393224 | tf_op jit(solution)/shard_map/ppermute | solution.py:323
  124.5 2.8 %all-to-all-done.4 = bf16[32,8,640]{2,1,0:T(8,128)(2,1)S(1)} async-done(((bf16[32,8,640]{2,1,0:T(8,128)(2,1)}), bf16[32,8,640]{2,1,0:T(8,128)(2,1)S(1)}, u32[]{:S(2)}, u32[]{:S(2)}) %all-to-all-start.4) | async-done | bytes 327712 | tf_op jit(solution)/shard_map/all_to_all | solution.py:251
  127.3 0.7 copy-done.21
  128.0 6.6 %all_gather.7.err_ref = bf16[512,640]{1,0:T(8,128)(2,1)S(1)} all-gather(bf16[256,640]{1,0:T(8,128)(2,1)} %bitcast.29), channel_id=1, replica_groups=mesh['x'=4,'yl'=2,'z'=8,'yh'=4,'c'=2] {'c'}, dimensions={0}, use_global_device_ids=true | all-gather | bytes 983040 | tf_op jit(solution)/shard_map/all_gather | solution.py:325
  134.7 1.9 %shard_map.101 = bf16[8,528,128]{2,1,0:T(8,128)(2,1)} custom-call(bf16[512,640]{1,0:T(8,128)(2,1)S(1)} %all_gather.7.err_ref, bf16[576,1024]{1,0:T(8,128)(2,1)S(1)} %bitcast.24), custom_call_target="tpu_custom_call" | custom-call | flops 603979776 | bytes 2916352 | tf_op jit(solution)/shard_map/pallas_call | solution.py:30
  136.5 4.3 %all-to-all-start.5 = ((bf16[8,528,128]{2,1,0:T(8,128)(2,1)}), bf16[8,528,128]{2,1,0:T(8,128)(2,1)}, u32[]{:S(2)}, u32[]{:S(2)}) async-start(bf16[8,528,128]{2,1,0:T(8,128)(2,1)} %shard_map.101), calls=%async_computation.5 | async-start | bytes 2162688 | tf_op jit(solution)/shard_map/all_to_all | solution.py:251
  140.8 0.0 copy-start.4
  140.8 1.0 copy-done.4
  141.8 1.0 shard_map.102
  142.9 0.7 copy-done.13
  143.6 3.2 %collective-permute-start.5 = (bf16[512,128]{1,0:T(8,128)(2,1)S(1)}, bf16[512,128]{1,0:T(8,128)(2,1)}, u32[]{:S(2)}, u32[]{:S(2)}) collective-permute-start(bf16[512,128]{1,0:T(8,128)(2,1)S(1)} %get-tuple-element.75), channel_id=1, source_target_pairs={{0,64},{64,0},{1,65},{65,1},{2,66},{66,2},{3,67},{67,3},{4,68},{68... | collective-permute-start | bytes 393224 | tf_op jit(solution)/shard_map/ppermute | solution.py:347
  146.8 10.5 %collective-permute-done.5.refs_3_ = bf16[512,128]{1,0:T(8,128)(2,1)} collective-permute-done((bf16[512,128]{1,0:T(8,128)(2,1)S(1)}, bf16[512,128]{1,0:T(8,128)(2,1)}, u32[]{:S(2)}, u32[]{:S(2)}) %collective-permute-start.5) | collective-permute-done | bytes 131104 | tf_op jit(solution)/shard_map/ppermute | solution.py:347
  157.4 3.2 %shard_map.103 = (bf16[8,512,128]{2,1,0:T(8,128)(2,1)}, f32[1,1]{1,0:T(1,128)}) custom-call(bf16[8,528,128]{2,1,0:T(8,128)(2,1)} %all-to-all-done.5.refs_0_, f32[512,128]{1,0:T(8,128)} %get-tuple-element.70.refs_1_, f32[512,128]{1,0:T(8,128)} %copy-done.13, bf16[512,128]{1,0:T(8,128)(2,1)} %collective-permute-done.5.refs_3_, ...), custom_call_target="tpu_custom_call" | custom-call | bytes 2789380 | tf_op jit(solution)/shard_map/pallas_call | solution.py:30
  160.5 4.3 %all-to-all-start.6 = ((bf16[8,512,128]{2,1,0:T(8,128)(2,1)}), bf16[8,512,128]{2,1,0:T(8,128)(2,1)}, u32[]{:S(2)}, u32[]{:S(2)}) async-start(bf16[8,512,128]{2,1,0:T(8,128)(2,1)} %get-tuple-element.77), calls=%async_computation.6 | async-start | bytes 2097152 | tf_op jit(solution)/shard_map/all_to_all | solution.py:251
  164.8 0.2 shard_map.93.refs_0_
  165.0 0.8 copy-done.2
  165.9 1.8 shard_map.105
  167.7 0.6 convert_reduce_fusion
  168.3 11.6 %all-to-all-done.6.refs_1_ = bf16[8,512,128]{2,1,0:T(8,128)(2,1)} async-done(((bf16[8,512,128]{2,1,0:T(8,128)(2,1)}), bf16[8,512,128]{2,1,0:T(8,128)(2,1)}, u32[]{:S(2)}, u32[]{:S(2)}) %all-to-all-start.6) | async-done | bytes 1048608 | tf_op jit(solution)/shard_map/all_to_all | solution.py:251
  179.9 4.5 %shard_map.104 = (bf16[576,1024]{1,0:T(8,128)(2,1)}, bf16[8,128]{1,0:T(8,128)(2,1)}) custom-call(bf16[576,512]{1,0:T(8,128)(2,1)} %copy-done.2, bf16[8,512,128]{2,1,0:T(8,128)(2,1)} %all-to-all-done.6.refs_1_), custom_call_target="tpu_custom_call" | custom-call | flops 603979776 | bytes 2820096 | tf_op jit(solution)/shard_map/pallas_call | solution.py:30
  (31 shorter events, 0.1 us)
Async XLA Ops:
  0.6 0.7 copy-start.14
  2.1 30.1 %all-to-all-start = ((bf16[32,8,576]{2,1,0:T(8,128)(2,1)}), bf16[32,8,576]{2,1,0:T(8,128)(2,1)S(1)}, u32[]{:S(2)}, u32[]{:S(2)}) async-start(bf16[32,8,576]{2,1,0:T(8,128)(2,1)} %bitcast), calls=%async_computation | async-start | bytes 655360 | tf_op jit(solution)/shard_map/all_to_all | solution.py:251
  18.6 18.3 %copy-start.18 = (bf16[576,1024]{1,0:T(8,128)(2,1)S(1)}, bf16[576,1024]{1,0:T(8,128)(2,1)}, u32[]{:S(2)}) copy-start(bf16[576,1024]{1,0:T(8,128)(2,1)} %w_ref.1) | copy-start | bytes 3538948
  39.0 19.6 %copy-start.16 = (f32[1024]{0:T(1024)S(1)}, f32[1024]{0:T(1024)}, u32[]{:S(2)}) copy-start(f32[1024]{0:T(1024)} %param.7) | copy-start | bytes 12292
  59.8 3.7 %copy-start.17 = (f32[1,128]{1,0:T(1,128)}, f32[1,128]{1,0:T(1,128)S(1)}, u32[]{:S(2)}) copy-start(f32[1,128]{1,0:T(1,128)S(1)} %get-tuple-element.56.penalty_far) | copy-start | bytes 1540
  59.8 17.3 %copy-start = (bf16[1024,576]{0,1:T(8,128)(2,1)S(1)}, bf16[1024,576]{0,1:T(8,128)(2,1)}, u32[]{:S(2)}) copy-start(bf16[1024,576]{0,1:T(8,128)(2,1)} %param.8) | copy-start | bytes 3538948
  59.8 17.2 %all-to-all-start.2 = ((bf16[8,512,128]{2,1,0:T(8,128)(2,1)}), bf16[8,512,128]{2,1,0:T(8,128)(2,1)S(1)}, u32[]{:S(2)}, u32[]{:S(2)}) async-start(bf16[8,512,128]{2,1,0:T(8,128)(2,1)} %get-tuple-element.45), calls=%async_computation.2 | async-start | bytes 2097152 | tf_op jit(solution)/shard_map/all_to_all | solution.py:251
  63.6 1.2 copy-start.1
  65.5 0.7 copy-start.5
  66.2 0.7 copy-start.19
  66.9 0.7 copy-start.20
  67.6 10.1 %copy-start.7 = (bf16[2,2,256,128]{3,2,1,0:T(8,128)(2,1)}, bf16[2,2,256,128]{3,2,1,0:T(8,128)(2,1)S(1)}, u32[]{:S(2)}) copy-start(bf16[2,2,256,128]{3,2,1,0:T(8,128)(2,1)S(1)} %get-tuple-element.61.keep_b) | copy-start | bytes 786436
  77.7 5.3 %collective-permute-start = (bf16[256,576]{1,0:T(8,128)(2,1)S(1)}, bf16[256,576]{1,0:T(8,128)(2,1)S(1)}, u32[]{:S(2)}, u32[]{:S(2)}) collective-permute-start(bf16[256,576]{1,0:T(8,128)(2,1)S(1)} %shard_map.98), channel_id=1, source_target_pairs={{0,1},{1,0},{2,3},{3,2},{4,5},{5,4},{6,7},{7,6},{8,9},{9,8},{10,11... | collective-permute-start | bytes 884744 | tf_op jit(solution)/shard_map/ppermute | solution.py:299
  82.3 12.0 %copy-start.15 = (bf16[8,576]{1,0:T(8,128)(2,1)S(1)}, bf16[8,576]{1,0:T(8,128)(2,1)}, u32[]{:S(2)}) copy-start(bf16[8,576]{1,0:T(8,128)(2,1)} %rows_ref.1) | copy-start | bytes 27652
  82.3 12.0 %copy-start.22 = (f32[576]{0:T(1024)S(1)}, f32[576]{0:T(1024)}, u32[]{:S(2)}) copy-start(f32[576]{0:T(1024)} %param.9) | copy-start | bytes 6916
  83.7 31.3 %copy-start.6 = (bf16[2,2,256,128]{3,2,1,0:T(8,128)(2,1)S(1)}, bf16[2,2,256,128]{3,2,1,0:T(8,128)(2,1)}, u32[]{:S(2)}) copy-start(bf16[2,2,256,128]{3,2,1,0:T(8,128)(2,1)} %copy-done.5) | copy-start | bytes 786436
  83.8 18.4 %all-to-all-start.3 = ((bf16[32,8,576]{2,1,0:T(8,128)(2,1)}), bf16[32,8,576]{2,1,0:T(8,128)(2,1)S(1)}, u32[]{:S(2)}, u32[]{:S(2)}) async-start(bf16[32,8,576]{2,1,0:T(8,128)(2,1)} %bitcast.28), calls=%async_computation.3 | async-start | bytes 655360 | tf_op jit(solution)/shard_map/all_to_all | solution.py:251
  88.7 9.3 %collective-permute-start.1 = (bf16[2,2,256,128]{3,2,1,0:T(8,128)(2,1)}, bf16[2,2,256,128]{3,2,1,0:T(8,128)(2,1)S(1)}, u32[]{:S(2)}, u32[]{:S(2)}) collective-permute-start(bf16[2,2,256,128]{3,2,1,0:T(8,128)(2,1)} %copy-done.20), channel_id=1, source_target_pairs={{0,128},{128,0},{256,384},{384,256},{1,129},{129,1},{257,385},{385... | collective-permute-start | bytes 786440 | tf_op jit(solution)/shard_map/ppermute | solution.py:306
  91.2 10.2 %collective-permute-start.2 = (bf16[2,2,256,128]{3,2,1,0:T(8,128)(2,1)}, bf16[2,2,256,128]{3,2,1,0:T(8,128)(2,1)S(1)}, u32[]{:S(2)}, u32[]{:S(2)}) collective-permute-start(bf16[2,2,256,128]{3,2,1,0:T(8,128)(2,1)} %copy-done.19), channel_id=1, source_target_pairs={{0,384},{128,256},{256,128},{384,0},{1,385},{129,257},{257,129},{3... | collective-permute-start | bytes 786440 | tf_op jit(solution)/shard_map/ppermute | solution.py:307
  98.0 0.7 copy-start.9
  101.4 0.7 copy-start.11
  103.7 23.6 %all-to-all-start.4 = ((bf16[32,8,640]{2,1,0:T(8,128)(2,1)}), bf16[32,8,640]{2,1,0:T(8,128)(2,1)S(1)}, u32[]{:S(2)}, u32[]{:S(2)}) async-start(bf16[32,8,640]{2,1,0:T(8,128)(2,1)} %bitcast.13), calls=%async_computation.4 | async-start | bytes 655360 | tf_op jit(solution)/shard_map/all_to_all | solution.py:251
  115.1 1.0 copy-start.8
  116.0 0.9 copy-start.10
  117.0 0.9 copy-start.12
  118.7 0.8 copy-start.3
  119.4 15.2 %collective-permute-start.3 = (bf16[2,256,128]{2,1,0:T(8,128)(2,1)}, bf16[2,256,128]{2,1,0:T(8,128)(2,1)}, u32[]{:S(2)}, u32[]{:S(2)}) collective-permute-start(bf16[2,256,128]{2,1,0:T(8,128)(2,1)} %get-tuple-element.64), channel_id=1, source_target_pairs={{0,384},{128,256},{256,128},{384,0},{1,385},{129,257},{257,129},{3... | collective-permute-start | bytes 393224 | tf_op jit(solution)/shard_map/ppermute | solution.py:322
  122.6 12.1 %collective-permute-start.4 = (bf16[2,256,128]{2,1,0:T(8,128)(2,1)}, bf16[2,256,128]{2,1,0:T(8,128)(2,1)}, u32[]{:S(2)}, u32[]{:S(2)}) collective-permute-start(bf16[2,256,128]{2,1,0:T(8,128)(2,1)} %get-tuple-element.65), channel_id=1, source_target_pairs={{0,128},{128,0},{256,384},{384,256},{1,129},{129,1},{257,385},{385... | collective-permute-start | bytes 393224 | tf_op jit(solution)/shard_map/ppermute | solution.py:323
  127.3 0.7 copy-start.21
  136.5 20.9 %all-to-all-start.5 = ((bf16[8,528,128]{2,1,0:T(8,128)(2,1)}), bf16[8,528,128]{2,1,0:T(8,128)(2,1)}, u32[]{:S(2)}, u32[]{:S(2)}) async-start(bf16[8,528,128]{2,1,0:T(8,128)(2,1)} %shard_map.101), calls=%async_computation.5 | async-start | bytes 2162688 | tf_op jit(solution)/shard_map/all_to_all | solution.py:251
  140.8 1.0 copy-start.4
  142.9 0.7 copy-start.13
  143.6 13.8 %collective-permute-start.5 = (bf16[512,128]{1,0:T(8,128)(2,1)S(1)}, bf16[512,128]{1,0:T(8,128)(2,1)}, u32[]{:S(2)}, u32[]{:S(2)}) collective-permute-start(bf16[512,128]{1,0:T(8,128)(2,1)S(1)} %get-tuple-element.75), channel_id=1, source_target_pairs={{0,64},{64,0},{1,65},{65,1},{2,66},{66,2},{3,67},{67,3},{4,68},{68... | collective-permute-start | bytes 393224 | tf_op jit(solution)/shard_map/ppermute | solution.py:347
  160.5 19.4 %all-to-all-start.6 = ((bf16[8,512,128]{2,1,0:T(8,128)(2,1)}), bf16[8,512,128]{2,1,0:T(8,128)(2,1)}, u32[]{:S(2)}, u32[]{:S(2)}) async-start(bf16[8,512,128]{2,1,0:T(8,128)(2,1)} %get-tuple-element.77), calls=%async_computation.6 | async-start | bytes 2097152 | tf_op jit(solution)/shard_map/all_to_all | solution.py:251
  165.0 0.8 copy-start.2

commit v5 on v3

--- a/solution.py
+++ b/solution.py
@@ -39,27 +39,42 @@
     return jnp.concatenate(parts, axis=1)
 
 
-def encode(rows_ref, w_ref, squares_ref, sent_ref, low_ref):
+STEPS = 252.0
+
+
+def spread_rows(rows_ref, out_ref):
+    rows = rows_ref[...].astype(f32)
+    out_ref[...] = jnp.broadcast_to(rows[None], (32, 8, 576)).reshape(256, 576).astype(bf16)
+
+
+def encode(rows_ref, w_ref, squares_ref, sent_ref):
     rows = rows_ref[...]
-    for n in range(4):
-        part = matmul(rows, w_ref[:, n * 256 : (n + 1) * 256], ((1,), (0,)))
-        high = part.astype(bf16)
-        low = (part - high.astype(f32)).astype(bf16)
+    tops = []
+    for n in range(4):
+        part = matmul(rows, w_ref[:, n * 256 : (n + 1) * 256], ((1,), (0,))).reshape(8, 64, 256)
+        size = jnp.abs(part)
+        top = (jnp.max(size, axis=1, keepdims=True) * (1 + 2.0**-7) + 1e-30).astype(bf16).astype(f32)
+        code = jnp.exp2(size * (STEPS / top) - 126.0)
+        code = jnp.where(part < 0, -code, code).astype(bf16)
         for h in range(2):
             at = pl.ds((2 * n + h) * 64, 64)
-            sent_ref[:, at, :] = high[:, h * 128 : (h + 1) * 128].reshape(8, 64, 128)
-            low_ref[:, at, :] = low[:, h * 128 : (h + 1) * 128].reshape(8, 64, 128)
-    sent_ref[:, 512:528, :] = jnp.broadcast_to(squares_ref[...][None], (8, 16, 128))
+            lanes = slice(h * 128, (h + 1) * 128)
+            sent_ref[:, at, :] = code[:, :, lanes]
+            tops.append(top[:, :, lanes])
+    squares = jnp.broadcast_to(squares_ref[...][None], (8, 8, 128))
+    sent_ref[:, 512:528, :] = jnp.concatenate([squares] + tops, axis=1).astype(bf16)
 
 
 def activate(got_ref, bias_ref, acts_ref, pre_ref, norms_ref, penalty_ref):
-    extra = jnp.sum(got_ref[:, 512:528, :].astype(f32), axis=0)
-    norms = jnp.sqrt(extra[:8] + extra[8:] + 1e-06)
+    extra = got_ref[:, 512:528, :].astype(f32)
+    norms = jnp.sqrt(jnp.sum(extra[:, :8, :], axis=0) + 1e-06)
     norms_ref[...] = norms
     penalty = jnp.zeros((1, 128), f32)
     for q in range(8):
         at = pl.ds(q * 64, 64)
-        pre = jnp.sum(got_ref[:, at, :].astype(f32), axis=0) + bias_ref[q : q + 1, :]
+        code = got_ref[:, at, :].astype(f32)
+        part = (jnp.log2(jnp.abs(code)) + 126.0) * (extra[:, 8 + q : 9 + q, :] / STEPS)
+        pre = jnp.sum(jnp.where(code < 0, -part, part), axis=0) + bias_ref[q : q + 1, :]
         pre_ref[at, :] = pre
         acts = jnp.maximum(pre, 0.0).astype(bf16)
         acts_ref[:, at, :] = jnp.broadcast_to(acts[None], (8, 64, 128))
@@ -101,12 +116,12 @@
             sent_ref[:, at, :] = part[:, h * 128 : (h + 1) * 128].reshape(8, 64, 128)
 
 
-def mask(got_ref, pre_ref, fine_ref, norms_ref, out_ref, loss_ref):
+def mask(got_ref, pre_ref, norms_ref, out_ref, loss_ref):
     for q in range(8):
         at = pl.ds(q * 64, 64)
         d_acts = jnp.sum(got_ref[:, at, :].astype(f32), axis=0)
         d_acts = d_acts + penalty_weight / 16.0 * norms_ref[q : q + 1, :]
-        d_pre = jnp.where(pre_ref[at, :] + fine_ref[at, :] > 0, d_acts, 0.0).astype(bf16)
+        d_pre = jnp.where(pre_ref[at, :] > 0, d_acts, 0.0).astype(bf16)
         out_ref[:, at, :] = jnp.broadcast_to(d_pre[None], (8, 64, 128))
     total = jnp.sum(got_ref[:, 512:528, :].astype(f32), axis=0)
     loss_ref[...] = jnp.sum(total, axis=(0, 1), keepdims=True) / (ROWS * D)
@@ -114,7 +129,7 @@
 
 def decoder_gradient(acts_ref, err_ref, w_ref, norms_ref, out_ref, bias_ref):
     err = err_ref[:, :576]
-    bias_ref[...] = jnp.sum(err.astype(f32), axis=0, keepdims=True)
+    bias_ref[...] = jnp.sum(err.astype(f32), axis=0, keepdims=True).astype(bf16)
     for n in range(4):
         at = slice(n * 256, (n + 1) * 256)
         acts = jnp.concatenate(
@@ -128,94 +143,75 @@
 
 def encoder_gradient(rows_ref, d_pre_ref, out_ref, bias_ref):
     rows = rows_ref[...]
+    sums = []
     for n in range(4):
         pair = [d_pre_ref[:, q * 64 : (q + 1) * 64, :].reshape(512, 128) for q in (2 * n, 2 * n + 1)]
-        for h in range(2):
-            bias_ref[2 * n + h : 2 * n + h + 1, :] = jnp.sum(pair[h].astype(f32), axis=0, keepdims=True)
+        sums += [jnp.sum(part.astype(f32), axis=0, keepdims=True) for part in pair]
         d_pre = jnp.concatenate(pair, axis=1)
         out_ref[:, n * 256 : (n + 1) * 256] = matmul(rows, d_pre, ((0,), (0,))).astype(bf16)
+    bias_ref[...] = jnp.concatenate(sums, axis=0).astype(bf16)
 
 
 def exchange(blocks, axes):
     return lax.all_to_all(blocks, axes, 0, 0, tiled=True)
 
 
-def block_at(array, at):
-    return lax.dynamic_index_in_dim(array, at, 0, keepdims=False)
-
-
-def split(value):
-    high = lax.reduce_precision(value, exponent_bits=8, mantissa_bits=7)
-    return high.astype(bf16), (value - high).astype(bf16)
-
-
 def local(residual, w_enc, b_enc, w_dec, b_dec):
-    core, at_x, at_y = lax.axis_index("c"), lax.axis_index("x"), lax.axis_index("yl")
     w_across = w_dec.T
-    bias = b_enc.reshape(8, 128)
     work = 2 * 512 * 576 * 1024
-    near = exchange(jnp.broadcast_to(residual[None], (32, 8, 576)), CHIPS).reshape(256, 576)
+    near = call(spread_rows, [((256, 576), bf16)], residual)[0]
+    half = lax.axis_index("c").astype(jnp.int32).reshape(1)
+    small = (half, 1 - half, b_dec.reshape(1, 576), residual.astype(f32), b_enc.reshape(8, 128))
+    near, small = lax.optimization_barrier((exchange(near.reshape(32, 8, 576), CHIPS), small))
+    half, other_half, bias_dec, residual, bias_enc = small
+    near = near.reshape(256, 576)
     rows_all = lax.all_gather(near, "c", axis=0, tiled=True)
     wide = w_across.astype(f32)
-    squares = jnp.concatenate(split(jnp.sum(wide * wide, axis=0).reshape(8, 128)), axis=0)
-
-    sent, low = call(encode, [((8, 528, 128), bf16), ((8, 512, 128), bf16)], rows_all, w_enc, squares, flops=work)
+    squares = jnp.sum(wide * wide, axis=0).reshape(8, 128)
+
+    sent = call(encode, [((8, 528, 128), bf16)], rows_all, w_enc, squares, flops=work)[0]
     acts, pre, norms, penalty = call(
         activate,
         [((8, 512, 128), bf16), ((512, 128), f32), ((8, 128), f32), ((1, 128), f32)],
         exchange(sent, LAYER),
-        bias,
+        bias_enc,
     )
     acts = exchange(acts, LAYER)
 
-    half = core.astype(jnp.int32).reshape(1)
-    other = call(decode, [((256, 576), bf16)], 1 - half, acts, w_across, flops=work // 2, smem=(0,))[0]
+    other = call(decode, [((256, 576), bf16)], other_half, acts, w_across, flops=work // 2, smem=(0,))[0]
     other = lax.ppermute(other, "c", [(0, 1), (1, 0)])
     mine = call(decode, [((256, 576), f32)], half, acts, w_across, flops=work // 2, smem=(0,))[0]
     pair = (mine + other.astype(f32)).astype(bf16)
-
-    pair, low = lax.optimization_barrier((pair, low))
-    low = low.reshape(4, 1024, 128)
-    away = at_x ^ 1
-    over = jnp.stack([block_at(low, away), block_at(low, 3 - away)])
-    over = lax.ppermute(over, "x", [(i, i ^ 1) for i in range(4)])
-    recon, over = lax.optimization_barrier((exchange(pair.reshape(32, 8, 576), CHIPS), over))
-    own = block_at(low, at_x).astype(f32) + over[0].astype(f32)
-    mirror = (block_at(low, 3 - at_x).astype(f32) + over[1].astype(f32)).astype(bf16)
-
+    recon = exchange(pair.reshape(32, 8, 576), CHIPS)
     packed = call(
         residue,
         [((256, 640), bf16)],
         recon.reshape(256, 576),
-        b_dec.reshape(1, 576),
-        residual.astype(f32),
+        bias_dec,
+        residual,
         penalty,
     )[0]
-    packed, mirror = lax.optimization_barrier((packed, mirror))
-    mirror = lax.ppermute(mirror, "x", [(i, 3 - i) for i in range(4)])
-    packed, mirror = lax.optimization_barrier((exchange(packed.reshape(32, 8, 640), CHIPS), mirror))
-    err = lax.all_gather(packed.reshape(256, 640), "c", axis=0, tiled=True)
+    packed = exchange(packed.reshape(32, 8, 640), CHIPS).reshape(256, 640)
+    err = lax.all_gather(packed, "c", axis=0, tiled=True)
 
     sent = call(decode_back, [((8, 528, 128), bf16)], err, w_across, flops=work)[0]
-    sent, mirror = lax.optimization_barrier((sent, mirror))
-    own = (own + mirror.astype(f32)).reshape(2, 512, 128)
-    fine = lax.ppermute(block_at(own, 1 - at_y).astype(bf16), "yl", [(0, 1), (1, 0)])
-    fine = block_at(own, at_y) + fine.astype(f32)
-    d_pre, loss = call(
-        mask, [((8, 512, 128), bf16), ((1, 1), f32)], exchange(sent, LAYER), pre, fine, norms
-    )
+    got, acts, err = lax.optimization_barrier((exchange(sent, LAYER), acts, err))
+    d_pre, loss = call(mask, [((8, 512, 128), bf16), ((1, 1), f32)], got, pre, norms)
     grad_dec, grad_bdec = call(
-        decoder_gradient, [((576, 1024), bf16), ((1, 576), f32)], acts, err, w_across, norms, flops=work
+        decoder_gradient, [((576, 1024), bf16), ((1, 576), bf16)], acts, err, w_across, norms, flops=work
+    )
+    d_pre, grad_dec, grad_bdec, loss = lax.optimization_barrier(
+        (d_pre, grad_dec, grad_bdec.reshape(576), loss.reshape(()))
     )
     grad_enc, grad_benc = call(
-        encoder_gradient, [((576, 1024), bf16), ((8, 128), f32)], rows_all, exchange(d_pre, LAYER), flops=work
+        encoder_gradient, [((576, 1024), bf16), ((8, 128), bf16)], rows_all, exchange(d_pre, LAYER), flops=work
     )
     return (
         grad_enc,
-        grad_benc.astype(bf16).reshape(1024),
+        grad_benc.reshape(1024),
         grad_dec.T,
-        grad_bdec.astype(bf16).reshape(576),
-        loss.reshape(()),
+        grad_bdec,
+        loss,
     )
 
 

time: 190 us -> 167 us (0.88)
  blocking collectives: 30.3 us -> 119 us
  waiting for transfers between devices: 72.2 us -> 11.9 us
  starting transfers between devices: 57 us -> 20.6 us
  other arithmetic: 9.4 us -> 2.22 us
  local copies, waits for them, and re-layouts: 7.17 us -> 1.5 us
  Pallas kernels: 12.2 us -> 9.87 us
    all_to_all x1 -> x6, blocking collectives: 19.5 us -> 109 us  [exchange(): return lax.all_to_all(blocks, axes, 0, 0, tiled=True)]
    ppermute x3 -> x0, waiting for transfers between devices: 30.4 us -> none  [the longest x1 12.9 us: local(): over = lax.ppermute(over, 'x', [(i, i ^ 1) for i in range(4)])]
    all_to_all x6 -> x1, waiting for transfers between devices: 41.1 us -> 11.3 us  [exchange(): return lax.all_to_all(blocks, axes, 0, 0, tiled=True)]
    all_to_all x6 -> x1, starting transfers between devices: 44.8 us -> 16.5 us  [exchange(): return lax.all_to_all(blocks, axes, 0, 0, tiled=True)]
    ppermute x3 -> x0, starting transfers between devices: 7.63 us -> none  [the longest x1 3.23 us: local(): lax.ppermute(block_at(own, 1 - at_y).astype(bf16), 'yl', [(0, 1), (1, 0)])]
    convert_element_type x4 -> x0, other arithmetic: 3.28 us -> none  [the longest x1 1.89 us: local(): (block_at(low, 3 - at_x).astype(f32) + over[1].astype(f32)).astype(bf16)]
    add x2 -> x0, other arithmetic: 3.05 us -> none  [the longest x1 2.01 us: local(): own = (own + mirror.astype(f32)).reshape(2, 512, 128)]
    unnamed x24 -> x8, local copies, waits for them, and re-layouts: 3.67 us -> 0.71 us
  transfers between devices with their start and end apart: 10 -> 2, of which waited for: 8 -> 2; matrix products, arithmetic and copies ran while one was open for 4% -> 1% of each run, Pallas kernels for 1% -> 0%
where the time goes in v5:
time: 167 us; the launch traced here: 166 us
  blocking collectives  119 us (71%)
  starting transfers between devices  20.6 us (12%)
  waiting for transfers between devices  11.9 us (7%)
  Pallas kernels  9.87 us (6%)
  other arithmetic  2.22 us (1%)
    all_to_all x6, blocking collectives, exchange(): return lax.all_to_all(blocks, axes, 0, 0, tiled=True)  109 us
    all_to_all x1, starting transfers between devices, exchange(): return lax.all_to_all(blocks, axes, 0, 0, tiled=True)  16.5 us
    all_to_all x1, waiting for transfers between devices, exchange(): return lax.all_to_all(blocks, axes, 0, 0, tiled=True)  11.3 us
    pallas_call x10, Pallas kernels, call(): pl.pallas_call(body, out_shape=outs, in_specs=[pl.BlockSpec(memory_space=...  9.87 us
    all_gather x1, blocking collectives, local(): err = lax.all_gather(packed, 'c', axis=0, tiled=True)  5.24 us
    all_gather x1, blocking collectives, local(): rows_all = lax.all_gather(near, 'c', axis=0, tiled=True)  4.67 us
    ppermute x1, starting transfers between devices, local(): other = lax.ppermute(other, 'c', [(0, 1), (1, 0)])  4.12 us
  transfers between devices with their start and end apart: 2, of which 2 were waited for; matrix products, arithmetic and copies ran while one was open for 1% of the time, Pallas kernels for 0%

profile of v5, /device:TPU:1, one launch (start us, length us, event | category | flops | bytes accessed | tf_op | source)
XLA Modules:
  0.0 166.2 jit_solution(14460848354440428354)
XLA Ops:
  0.6 0.0 copy-start.2
  0.6 0.7 copy-done.2
  1.3 0.8 shard_map.92
  2.1 16.5 %all-to-all-start = ((bf16[32,8,576]{2,1,0:T(8,128)(2,1)}), bf16[32,8,576]{2,1,0:T(8,128)(2,1)S(1)}, u32[]{:S(2)}, u32[]{:S(2)}) async-start(bf16[32,8,576]{2,1,0:T(8,128)(2,1)} %bitcast), calls=%async_computation | async-start | bytes 655360 | tf_op jit(solution)/shard_map/all_to_all | solution.py:156
  18.6 0.0 copy-start.1
  18.6 0.8 reshape.51.bias_ref
  19.4 1.5 multiply_reduce_fusion
  21.0 11.3 %all-to-all-done = bf16[32,8,576]{2,1,0:T(8,128)(2,1)S(1)} async-done(((bf16[32,8,576]{2,1,0:T(8,128)(2,1)}), bf16[32,8,576]{2,1,0:T(8,128)(2,1)S(1)}, u32[]{:S(2)}, u32[]{:S(2)}) %all-to-all-start) | async-done | bytes 294944 | tf_op jit(solution)/shard_map/all_to_all | solution.py:156
  32.2 4.7 %all_gather.6.rows_ref = bf16[512,576]{1,0:T(8,128)(2,1)S(1)} all-gather(bf16[256,576]{1,0:T(8,128)(2,1)S(1)} %bitcast.23), channel_id=1, replica_groups=mesh['x'=4,'yl'=2,'z'=8,'yh'=4,'c'=2] {'c'}, dimensions={0}, use_global_device_ids=true | all-gather | bytes 884736 | tf_op jit(solution)/shard_map/all_gather | solution.py:168
  36.9 0.0 copy-done.1
  36.9 1.5 shard_map.93
  38.4 0.0 copy-start.3
  38.5 19.4 %all_to_all.35.got_ref = bf16[8,528,128]{2,1,0:T(8,128)(2,1)S(1)} all-to-all(bf16[8,528,128]{2,1,0:T(8,128)(2,1)S(1)} %shard_map.93), channel_id=1, replica_groups=mesh['x'=4,'yl'=2,'z'=8,'yh'=4,'c'=2] {'x','yl'}, dimensions={0} | all-to-all | bytes 2162688 | tf_op jit(solution)/shard_map/all_to_all | solution.py:156
  57.9 0.0 copy-done.3
  57.9 0.7 shard_map.94
  58.6 0.0 copy-start
  58.6 17.3 %all_to_all.36.acts_ref = bf16[8,512,128]{2,1,0:T(8,128)(2,1)S(1)} all-to-all(bf16[8,512,128]{2,1,0:T(8,128)(2,1)S(1)} %get-tuple-element.31), channel_id=1, replica_groups=mesh['x'=4,'yl'=2,'z'=8,'yh'=4,'c'=2] {'x','yl'}, dimensions={0} | all-to-all | bytes 2097152 | tf_op jit(solution)/shard_map/all_to_all | solution.py:156
  75.9 0.0 copy-done
  75.9 0.6 shard_map.96
  76.5 4.1 %collective-permute-start = (bf16[256,576]{1,0:T(8,128)(2,1)S(1)}, bf16[256,576]{1,0:T(8,128)(2,1)S(1)}, u32[]{:S(2)}, u32[]{:S(2)}) collective-permute-start(bf16[256,576]{1,0:T(8,128)(2,1)S(1)} %shard_map.96), channel_id=1, source_target_pairs={{0,1},{1,0},{2,3},{3,2},{4,5},{5,4},{6,7},{7,6},{8,9},{9,8},{10,11... | collective-permute-start | bytes 884744 | tf_op jit(solution)/shard_map/ppermute | solution.py:182
  80.6 0.6 shard_map.95
  81.2 0.6 collective-permute-done
  81.9 0.1 fusion
  81.9 17.6 %all_to_all.37 = bf16[32,8,576]{2,1,0:T(8,128)(2,1)S(1)} all-to-all(bf16[32,8,576]{2,1,0:T(8,128)(2,1)S(1)} %fusion), channel_id=1, replica_groups=mesh['x'=4,'yl'=2,'z'=8,'yh'=4,'c'=2] {'z','yh'}, dimensions={0} | all-to-all | bytes 589824 | tf_op jit(solution)/shard_map/all_to_all | solution.py:156
  99.5 0.3 shard_map.97
  99.8 18.8 %all_to_all.38 = bf16[32,8,640]{2,1,0:T(8,128)(2,1)S(1)} all-to-all(bf16[32,8,640]{2,1,0:T(8,128)(2,1)S(1)} %bitcast.20), channel_id=1, replica_groups=mesh['x'=4,'yl'=2,'z'=8,'yh'=4,'c'=2] {'z','yh'}, dimensions={0} | all-to-all | bytes 655360 | tf_op jit(solution)/shard_map/all_to_all | solution.py:156
  118.6 5.2 %all_gather.7.err_ref = bf16[512,640]{1,0:T(8,128)(2,1)S(1)} all-gather(bf16[256,640]{1,0:T(8,128)(2,1)S(1)} %bitcast.24), channel_id=1, replica_groups=mesh['x'=4,'yl'=2,'z'=8,'yh'=4,'c'=2] {'c'}, dimensions={0}, use_global_device_ids=true | all-gather | bytes 983040 | tf_op jit(solution)/shard_map/all_gather | solution.py:195
  123.8 1.0 shard_map.98
  124.8 19.1 %all_to_all.39.got_ref = bf16[8,528,128]{2,1,0:T(8,128)(2,1)S(1)} all-to-all(bf16[8,528,128]{2,1,0:T(8,128)(2,1)S(1)} %shard_map.98), channel_id=1, replica_groups=mesh['x'=4,'yl'=2,'z'=8,'yh'=4,'c'=2] {'x','yl'}, dimensions={0} | all-to-all | bytes 2162688 | tf_op jit(solution)/shard_map/all_to_all | solution.py:156
  143.9 0.8 shard_map.99
  144.7 1.8 %shard_map.100 = (bf16[576,1024]{1,0:T(8,128)(2,1)}, bf16[1,576]{1,0:T(2,128)(2,1)S(1)}) custom-call(bf16[8,512,128]{2,1,0:T(8,128)(2,1)S(1)} %all_to_all.36.acts_ref, bf16[512,640]{1,0:T(8,128)(2,1)S(1)} %all_gather.7.err_ref, bf16[576,1024]{1,0:T(8,128)(2,1)S(1)} %bitcast.18, f32[8,128]{1,0:T(8,128)S(1)} %get-tuple-element.38.norms_ref), custom_call_target="tpu_custom_call" | custom-call | flops 603979776 | bytes 4068480 | tf_op jit(solution)/shard_map/pallas_call | solution.py:21
  146.6 0.6 reduce
  147.2 17.2 %all_to_all.40.d_pre_ref = bf16[8,512,128]{2,1,0:T(8,128)(2,1)S(1)} all-to-all(bf16[8,512,128]{2,1,0:T(8,128)(2,1)S(1)} %get-tuple-element.45), channel_id=1, replica_groups=mesh['x'=4,'yl'=2,'z'=8,'yh'=4,'c'=2] {'x','yl'}, dimensions={0} | all-to-all | bytes 2097152 | tf_op jit(solution)/shard_map/all_to_all | solution.py:156
  164.3 1.8 %shard_map.101 = (bf16[576,1024]{1,0:T(8,128)(2,1)}, bf16[8,128]{1,0:T(8,128)(2,1)}) custom-call(bf16[512,576]{1,0:T(8,128)(2,1)S(1)} %all_gather.6.rows_ref, bf16[8,512,128]{2,1,0:T(8,128)(2,1)S(1)} %all_to_all.40.d_pre_ref), custom_call_target="tpu_custom_call" | custom-call | flops 603979776 | bytes 2820096 | tf_op jit(solution)/shard_map/pallas_call | solution.py:21
  (1 shorter events, 0.0 us)
Async XLA Ops:
  0.6 0.7 copy-start.2
  2.1 30.1 %all-to-all-start = ((bf16[32,8,576]{2,1,0:T(8,128)(2,1)}), bf16[32,8,576]{2,1,0:T(8,128)(2,1)S(1)}, u32[]{:S(2)}, u32[]{:S(2)}) async-start(bf16[32,8,576]{2,1,0:T(8,128)(2,1)} %bitcast), calls=%async_computation | async-start | bytes 655360 | tf_op jit(solution)/shard_map/all_to_all | solution.py:156
  18.6 18.3 %copy-start.1 = (bf16[576,1024]{1,0:T(8,128)(2,1)S(1)}, bf16[576,1024]{1,0:T(8,128)(2,1)}, u32[]{:S(2)}) copy-start(bf16[576,1024]{1,0:T(8,128)(2,1)} %w_ref.1) | copy-start | bytes 3538948
  38.4 19.4 %copy-start.3 = (f32[1024]{0:T(1024)S(1)}, f32[1024]{0:T(1024)}, u32[]{:S(2)}) copy-start(f32[1024]{0:T(1024)} %param.7) | copy-start | bytes 12292
  58.6 17.3 %copy-start = (bf16[1024,576]{0,1:T(8,128)(2,1)S(1)}, bf16[1024,576]{0,1:T(8,128)(2,1)}, u32[]{:S(2)}) copy-start(bf16[1024,576]{0,1:T(8,128)(2,1)} %param.8) | copy-start | bytes 3538948
  76.5 5.4 %collective-permute-start = (bf16[256,576]{1,0:T(8,128)(2,1)S(1)}, bf16[256,576]{1,0:T(8,128)(2,1)S(1)}, u32[]{:S(2)}, u32[]{:S(2)}) collective-permute-start(bf16[256,576]{1,0:T(8,128)(2,1)S(1)} %shard_map.96), channel_id=1, source_target_pairs={{0,1},{1,0},{2,3},{3,2},{4,5},{5,4},{6,7},{7,6},{8,9},{9,8},{10,11... | collective-permute-start | bytes 884744 | tf_op jit(solution)/shard_map/ppermute | solution.py:182

commit v6 on v5

--- a/solution.py
+++ b/solution.py
@@ -1,3 +1,5 @@
+import math
+
 import jax
 import jax.numpy as jnp
 from jax import lax
@@ -15,19 +17,25 @@
 penalty_weight = 0.5
 
 
-def call(body, outs, *args, flops=0, smem=()):
-    outs = [jax.ShapeDtypeStruct(shape, dtype) for shape, dtype in outs]
-    size = sum(a.size * a.dtype.itemsize for a in args) + sum(o.size * o.dtype.itemsize for o in outs)
+def call(body, outs, *args, flops=0, smem=(), far=(), scratch=()):
+    outs = [pltpu.HBM(*o) if i in far else jax.ShapeDtypeStruct(*o) for i, o in enumerate(outs)]
+    size = sum(math.prod(a.shape) * jnp.dtype(a.dtype).itemsize for a in list(args) + outs)
     return pl.pallas_call(
         body,
         out_shape=outs,
         in_specs=[
             pl.BlockSpec(memory_space=pltpu.SMEM if i in smem else pltpu.VMEM) for i in range(len(args))
         ],
-        out_specs=[pl.BlockSpec(memory_space=pltpu.VMEM) for _ in outs],
+        out_specs=[pl.BlockSpec(memory_space=pltpu.HBM if i in far else pltpu.VMEM) for i in range(len(outs))],
+        scratch_shapes=list(scratch),
         cost_estimate=pl.CostEstimate(flops=flops, bytes_accessed=size, transcendentals=0),
         compiler_params=pltpu.CompilerParams(vmem_limit_bytes=24 * 2**20),
     )(*args)
+
+
+def quarters(source, target, sem):
+    at = [(slice(None), pl.ds(n * 256, 256)) for n in range(4)]
+    return [pltpu.make_async_copy(source.at[i], target.at[i], sem.at[n]) for n, i in enumerate(at)]
 
 
 def matmul(a, b, dims):
@@ -82,9 +90,15 @@
     penalty_ref[...] = penalty_weight * penalty
 
 
-def decode(half_ref, acts_ref, w_ref, out_ref):
-    acts = row_block(acts_ref, half_ref[0] * 4, 4)
-    out_ref[...] = matmul(acts, w_ref[...], ((1,), (1,))).astype(out_ref.dtype)
+def decode(half_ref, acts_ref, w_ref, other_ref, mine_ref):
+    for half, ref in ((1 - half_ref[0], other_ref), (half_ref[0], mine_ref)):
+        acts = row_block(acts_ref, half * 4, 4)
+        ref[...] = matmul(acts, w_ref[...], ((1,), (1,))).astype(ref.dtype)
+
+
+def add_pair(half_ref, both_ref, mine_ref, out_ref):
+    other = both_ref[pl.ds(pl.multiple_of((1 - half_ref[0]) * 256, 256), 256), :]
+    out_ref[...] = (mine_ref[...] + other.astype(f32)).astype(bf16)
 
 
 def residue(got_ref, bias_ref, residual_ref, penalty_ref, out_ref):
@@ -127,9 +141,10 @@
     loss_ref[...] = jnp.sum(total, axis=(0, 1), keepdims=True) / (ROWS * D)
 
 
-def decoder_gradient(acts_ref, err_ref, w_ref, norms_ref, out_ref, bias_ref):
+def decoder_gradient(acts_ref, err_ref, w_ref, norms_ref, far_ref, bias_ref, out_ref, sem):
+    out = quarters(out_ref, far_ref, sem)
     err = err_ref[:, :576]
-    bias_ref[...] = jnp.sum(err.astype(f32), axis=0, keepdims=True).astype(bf16)
+    bias_ref[...] = jnp.sum(err.astype(f32), axis=0).astype(bf16)
     for n in range(4):
         at = slice(n * 256, (n + 1) * 256)
         acts = jnp.concatenate(
@@ -139,9 +154,13 @@
         scale = penalty_weight / 16.0 * jnp.sum(acts.astype(f32), axis=0, keepdims=True) / norms
         outer = matmul(err, acts, ((0,), (0,)))
         out_ref[:, at] = (outer + scale * w_ref[:, at].astype(f32)).astype(bf16)
-
-
-def encoder_gradient(rows_ref, d_pre_ref, out_ref, bias_ref):
+        out[n].start()
+    for copy in out:
+        copy.wait()
+
+
+def encoder_gradient(rows_ref, d_pre_ref, far_ref, bias_ref, out_ref, sem):
+    out = quarters(out_ref, far_ref, sem)
     rows = rows_ref[...]
     sums = []
     for n in range(4):
@@ -149,7 +168,10 @@
         sums += [jnp.sum(part.astype(f32), axis=0, keepdims=True) for part in pair]
         d_pre = jnp.concatenate(pair, axis=1)
         out_ref[:, n * 256 : (n + 1) * 256] = matmul(rows, d_pre, ((0,), (0,))).astype(bf16)
+        out[n].start()
     bias_ref[...] = jnp.concatenate(sums, axis=0).astype(bf16)
+    for copy in out:
+        copy.wait()
 
 
 def exchange(blocks, axes):
@@ -161,9 +183,9 @@
     work = 2 * 512 * 576 * 1024
     near = call(spread_rows, [((256, 576), bf16)], residual)[0]
     half = lax.axis_index("c").astype(jnp.int32).reshape(1)
-    small = (half, 1 - half, b_dec.reshape(1, 576), residual.astype(f32), b_enc.reshape(8, 128))
+    small = (half, b_dec.reshape(1, 576), residual.astype(f32), b_enc.reshape(8, 128))
     near, small = lax.optimization_barrier((exchange(near.reshape(32, 8, 576), CHIPS), small))
-    half, other_half, bias_dec, residual, bias_enc = small
+    half, bias_dec, residual, bias_enc = small
     near = near.reshape(256, 576)
     rows_all = lax.all_gather(near, "c", axis=0, tiled=True)
     wide = w_across.astype(f32)
@@ -178,10 +200,11 @@
     )
     acts = exchange(acts, LAYER)
 
-    other = call(decode, [((256, 576), bf16)], other_half, acts, w_across, flops=work // 2, smem=(0,))[0]
-    other = lax.ppermute(other, "c", [(0, 1), (1, 0)])
-    mine = call(decode, [((256, 576), f32)], half, acts, w_across, flops=work // 2, smem=(0,))[0]
-    pair = (mine + other.astype(f32)).astype(bf16)
+    other, mine = call(
+        decode, [((256, 576), bf16), ((256, 576), f32)], half, acts, w_across, flops=work, smem=(0,)
+    )
+    both = lax.all_gather(other, "c", axis=0, tiled=True)
+    pair = call(add_pair, [((256, 576), bf16)], half, both, mine, smem=(0,))[0]
     recon = exchange(pair.reshape(32, 8, 576), CHIPS)
     packed = call(
         residue,
@@ -197,14 +220,15 @@
     sent = call(decode_back, [((8, 528, 128), bf16)], err, w_across, flops=work)[0]
     got, acts, err = lax.optimization_barrier((exchange(sent, LAYER), acts, err))
     d_pre, loss = call(mask, [((8, 512, 128), bf16), ((1, 1), f32)], got, pre, norms)
+    kept = dict(flops=work, far=(0,), scratch=(pltpu.VMEM((576, 1024), bf16), pltpu.SemaphoreType.DMA((4,))))
     grad_dec, grad_bdec = call(
-        decoder_gradient, [((576, 1024), bf16), ((1, 576), bf16)], acts, err, w_across, norms, flops=work
+        decoder_gradient, [((576, 1024), bf16), ((576,), bf16)], acts, err, w_across, norms, **kept
     )
     d_pre, grad_dec, grad_bdec, loss = lax.optimization_barrier(
         (d_pre, grad_dec, grad_bdec.reshape(576), loss.reshape(()))
     )
     grad_enc, grad_benc = call(
-        encoder_gradient, [((576, 1024), bf16), ((8, 128), bf16)], rows_all, exchange(d_pre, LAYER), flops=work
+        encoder_gradient, [((576, 1024), bf16), ((8, 128), bf16)], rows_all, exchange(d_pre, LAYER), **kept
     )
     return (
         grad_enc,

time: 167 us -> 166 us (level)
  starting transfers between devices: 20.6 us -> 16.5 us
  blocking collectives: 119 us -> 123 us
    ppermute x1 -> x0, starting transfers between devices: 4.12 us -> none  [local(): other = lax.ppermute(other, 'c', [(0, 1), (1, 0)])]
    all_gather x0 -> x1, blocking collectives: none -> 4.11 us  [local(): both = lax.all_gather(other, 'c', axis=0, tiled=True)]
  transfers between devices with their start and end apart: 2 -> 1, of which waited for: 2 -> 1; matrix products, arithmetic and copies ran while one was open for 1% -> 2% of each run, Pallas kernels for 0% -> 0%
where the time goes in v6:
time: 166 us
  blocking collectives  123 us (74%)
  starting transfers between devices  16.5 us (10%)
  Pallas kernels  10.6 us (6%)
  waiting for transfers between devices  10.6 us (6%)
  other arithmetic  2.35 us (1%)
    all_to_all x6, blocking collectives, exchange(): return lax.all_to_all(blocks, axes, 0, 0, tiled=True)  109 us
    all_to_all x1, starting transfers between devices, exchange(): return lax.all_to_all(blocks, axes, 0, 0, tiled=True)  16.5 us
    pallas_call x10, Pallas kernels, call(): pl.pallas_call(body, out_shape=outs, in_specs=[pl.BlockSpec(memory_space=...  10.6 us
    all_to_all x1, waiting for transfers between devices, exchange(): return lax.all_to_all(blocks, axes, 0, 0, tiled=True)  10.6 us
    all_gather x1, blocking collectives, local(): err = lax.all_gather(packed, 'c', axis=0, tiled=True)  5.21 us
    all_gather x1, blocking collectives, local(): rows_all = lax.all_gather(near, 'c', axis=0, tiled=True)  4.67 us
    all_gather x1, blocking collectives, local(): both = lax.all_gather(other, 'c', axis=0, tiled=True)  4.11 us
  transfers between devices with their start and end apart: 1, of which 1 were waited for; matrix products, arithmetic and copies ran while one was open for 2% of the time, Pallas kernels for 0%

profile of v6, /device:TPU:1, one launch (start us, length us, event | category | flops | bytes accessed | tf_op | source)
XLA Modules:
  0.0 165.6 jit_solution(906623581989045523)
XLA Ops:
  0.6 0.0 copy-start.2
  0.6 0.7 copy-done.2
  1.3 0.8 shard_map.92
  2.1 16.5 %all-to-all-start = ((bf16[32,8,576]{2,1,0:T(8,128)(2,1)}), bf16[32,8,576]{2,1,0:T(8,128)(2,1)S(1)}, u32[]{:S(2)}, u32[]{:S(2)}) async-start(bf16[32,8,576]{2,1,0:T(8,128)(2,1)} %bitcast), calls=%async_computation | async-start | bytes 655360 | tf_op jit(solution)/shard_map/all_to_all | solution.py:178
  18.6 0.0 copy-start.1
  18.6 0.8 convert_element_type.6.residual_ref
  19.4 0.7 reshape.48.bias_ref
  20.1 1.5 multiply_reduce_fusion
  21.7 10.6 %all-to-all-done = bf16[32,8,576]{2,1,0:T(8,128)(2,1)S(1)} async-done(((bf16[32,8,576]{2,1,0:T(8,128)(2,1)}), bf16[32,8,576]{2,1,0:T(8,128)(2,1)S(1)}, u32[]{:S(2)}, u32[]{:S(2)}) %all-to-all-start) | async-done | bytes 294944 | tf_op jit(solution)/shard_map/all_to_all | solution.py:178
  32.2 4.7 %all_gather.9.rows_ref = bf16[512,576]{1,0:T(8,128)(2,1)S(1)} all-gather(bf16[256,576]{1,0:T(8,128)(2,1)S(1)} %bitcast.22), channel_id=1, replica_groups=mesh['x'=4,'yl'=2,'z'=8,'yh'=4,'c'=2] {'c'}, dimensions={0}, use_global_device_ids=true | all-gather | bytes 884736 | tf_op jit(solution)/shard_map/all_gather | solution.py:190
  36.9 0.0 copy-done.1
  36.9 1.5 shard_map.93
  38.4 0.0 copy-start.3
  38.5 19.4 %all_to_all.35.got_ref = bf16[8,528,128]{2,1,0:T(8,128)(2,1)S(1)} all-to-all(bf16[8,528,128]{2,1,0:T(8,128)(2,1)S(1)} %shard_map.93), channel_id=1, replica_groups=mesh['x'=4,'yl'=2,'z'=8,'yh'=4,'c'=2] {'x','yl'}, dimensions={0} | all-to-all | bytes 2162688 | tf_op jit(solution)/shard_map/all_to_all | solution.py:178
  57.9 0.0 copy-done.3
  57.9 0.7 shard_map.94
  58.6 0.0 copy-start
  58.6 17.3 %all_to_all.36.acts_ref = bf16[8,512,128]{2,1,0:T(8,128)(2,1)S(1)} all-to-all(bf16[8,512,128]{2,1,0:T(8,128)(2,1)S(1)} %get-tuple-element.32), channel_id=1, replica_groups=mesh['x'=4,'yl'=2,'z'=8,'yh'=4,'c'=2] {'x','yl'}, dimensions={0} | all-to-all | bytes 2097152 | tf_op jit(solution)/shard_map/all_to_all | solution.py:178
  75.9 0.0 copy-done
  75.9 1.0 shard_map.95
  76.9 4.1 %all_gather.10.both_ref = bf16[512,576]{1,0:T(8,128)(2,1)S(1)} all-gather(bf16[256,576]{1,0:T(8,128)(2,1)S(1)} %get-tuple-element.33), channel_id=1, replica_groups=mesh['x'=4,'yl'=2,'z'=8,'yh'=4,'c'=2] {'c'}, dimensions={0}, use_global_device_ids=true | all-gather | bytes 884736 | tf_op jit(solution)/shard_map/all_gather | solution.py:206
  81.0 0.1 shard_map.96
  81.1 17.6 %all_to_all.37 = bf16[32,8,576]{2,1,0:T(8,128)(2,1)S(1)} all-to-all(bf16[32,8,576]{2,1,0:T(8,128)(2,1)S(1)} %bitcast.19), channel_id=1, replica_groups=mesh['x'=4,'yl'=2,'z'=8,'yh'=4,'c'=2] {'z','yh'}, dimensions={0} | all-to-all | bytes 589824 | tf_op jit(solution)/shard_map/all_to_all | solution.py:178
  98.7 0.3 shard_map.97
  98.9 18.8 %all_to_all.38 = bf16[32,8,640]{2,1,0:T(8,128)(2,1)S(1)} all-to-all(bf16[32,8,640]{2,1,0:T(8,128)(2,1)S(1)} %bitcast.18), channel_id=1, replica_groups=mesh['x'=4,'yl'=2,'z'=8,'yh'=4,'c'=2] {'z','yh'}, dimensions={0} | all-to-all | bytes 655360 | tf_op jit(solution)/shard_map/all_to_all | solution.py:178
  117.7 5.2 %all_gather.11.err_ref = bf16[512,640]{1,0:T(8,128)(2,1)S(1)} all-gather(bf16[256,640]{1,0:T(8,128)(2,1)S(1)} %bitcast.23), channel_id=1, replica_groups=mesh['x'=4,'yl'=2,'z'=8,'yh'=4,'c'=2] {'c'}, dimensions={0}, use_global_device_ids=true | all-gather | bytes 983040 | tf_op jit(solution)/shard_map/all_gather | solution.py:218
  122.9 1.0 shard_map.98
  123.9 19.1 %all_to_all.39.got_ref = bf16[8,528,128]{2,1,0:T(8,128)(2,1)S(1)} all-to-all(bf16[8,528,128]{2,1,0:T(8,128)(2,1)S(1)} %shard_map.98), channel_id=1, replica_groups=mesh['x'=4,'yl'=2,'z'=8,'yh'=4,'c'=2] {'x','yl'}, dimensions={0} | all-to-all | bytes 2162688 | tf_op jit(solution)/shard_map/all_to_all | solution.py:178
  143.1 0.8 shard_map.99
  143.9 2.3 %shard_map.100 = (bf16[576,1024]{1,0:T(8,128)(2,1)}, bf16[576]{0:T(1024)(128)(2,1)}) custom-call(bf16[8,512,128]{2,1,0:T(8,128)(2,1)S(1)} %all_to_all.36.acts_ref, bf16[512,640]{1,0:T(8,128)(2,1)S(1)} %all_gather.11.err_ref, bf16[576,1024]{1,0:T(8,128)(2,1)S(1)} %bitcast.16, f32[8,128]{1,0:T(8,128)S(1)} %get-tuple-element.40.norms_ref), custom_call_target="tpu_custom_call" | custom-call | flops 603979776 | bytes 4068480 | tf_op jit(solution)/shard_map/pallas_call | solution.py:23
  146.2 17.2 %all_to_all.40.d_pre_ref = bf16[8,512,128]{2,1,0:T(8,128)(2,1)S(1)} all-to-all(bf16[8,512,128]{2,1,0:T(8,128)(2,1)S(1)} %get-tuple-element.47), channel_id=1, replica_groups=mesh['x'=4,'yl'=2,'z'=8,'yh'=4,'c'=2] {'x','yl'}, dimensions={0} | all-to-all | bytes 2097152 | tf_op jit(solution)/shard_map/all_to_all | solution.py:178
  163.3 2.3 %shard_map.101 = (bf16[576,1024]{1,0:T(8,128)(2,1)}, bf16[8,128]{1,0:T(8,128)(2,1)}) custom-call(bf16[512,576]{1,0:T(8,128)(2,1)S(1)} %all_gather.9.rows_ref, bf16[8,512,128]{2,1,0:T(8,128)(2,1)S(1)} %all_to_all.40.d_pre_ref), custom_call_target="tpu_custom_call" | custom-call | flops 603979776 | bytes 2820096 | tf_op jit(solution)/shard_map/pallas_call | solution.py:23
Async XLA Ops:
  0.6 0.7 copy-start.2
  2.1 30.1 %all-to-all-start = ((bf16[32,8,576]{2,1,0:T(8,128)(2,1)}), bf16[32,8,576]{2,1,0:T(8,128)(2,1)S(1)}, u32[]{:S(2)}, u32[]{:S(2)}) async-start(bf16[32,8,576]{2,1,0:T(8,128)(2,1)} %bitcast), calls=%async_computation | async-start | bytes 655360 | tf_op jit(solution)/shard_map/all_to_all | solution.py:178
  18.6 18.3 %copy-start.1 = (bf16[576,1024]{1,0:T(8,128)(2,1)S(1)}, bf16[576,1024]{1,0:T(8,128)(2,1)}, u32[]{:S(2)}) copy-start(bf16[576,1024]{1,0:T(8,128)(2,1)} %w_ref.1) | copy-start | bytes 3538948
  38.4 19.4 %copy-start.3 = (f32[1024]{0:T(1024)S(1)}, f32[1024]{0:T(1024)}, u32[]{:S(2)}) copy-start(f32[1024]{0:T(1024)} %param.7) | copy-start | bytes 12292
  58.6 17.3 %copy-start = (bf16[1024,576]{0,1:T(8,128)(2,1)S(1)}, bf16[1024,576]{0,1:T(8,128)(2,1)}, u32[]{:S(2)}) copy-start(bf16[1024,576]{0,1:T(8,128)(2,1)} %param.8) | copy-start | bytes 3538948

commit v7 on v6

--- a/solution.py
+++ b/solution.py
@@ -18,26 +18,24 @@
 
 
 def call(body, outs, *args, flops=0, smem=(), far=(), scratch=()):
-    outs = [pltpu.HBM(*o) if i in far else jax.ShapeDtypeStruct(*o) for i, o in enumerate(outs)]
+    outs = [jax.ShapeDtypeStruct(*o) for o in outs]
     size = sum(math.prod(a.shape) * jnp.dtype(a.dtype).itemsize for a in list(args) + outs)
+    args = [pltpu.with_memory_space_constraint(a, pltpu.HBM) if i in far else a for i, a in enumerate(args)]
+
+    def space(i):
+        return pltpu.SMEM if i in smem else pltpu.HBM if i in far else pltpu.VMEM
+
     return pl.pallas_call(
         body,
         out_shape=outs,
-        in_specs=[
-            pl.BlockSpec(memory_space=pltpu.SMEM if i in smem else pltpu.VMEM) for i in range(len(args))
-        ],
-        out_specs=[pl.BlockSpec(memory_space=pltpu.HBM if i in far else pltpu.VMEM) for i in range(len(outs))],
+        in_specs=[pl.BlockSpec(memory_space=space(i)) for i in range(len(args))],
+        out_specs=[pl.BlockSpec(memory_space=pltpu.VMEM) for _ in outs],
         scratch_shapes=list(scratch),
         cost_estimate=pl.CostEstimate(flops=flops, bytes_accessed=size, transcendentals=0),
         compiler_params=pltpu.CompilerParams(vmem_limit_bytes=24 * 2**20),
     )(*args)
 
 
-def quarters(source, target, sem):
-    at = [(slice(None), pl.ds(n * 256, 256)) for n in range(4)]
-    return [pltpu.make_async_copy(source.at[i], target.at[i], sem.at[n]) for n, i in enumerate(at)]
-
-
 def matmul(a, b, dims):
     return lax.dot_general(a, b, (dims, ((), ())), preferred_element_type=f32)
 
@@ -55,10 +53,19 @@
     out_ref[...] = jnp.broadcast_to(rows[None], (32, 8, 576)).reshape(256, 576).astype(bf16)
 
 
-def encode(rows_ref, w_ref, squares_ref, sent_ref):
+def encode(rows_ref, w_far, across_ref, sent_ref, w_ref, sem):
+    quarters = [(slice(None), pl.ds(n * 256, 256)) for n in range(4)]
+    fetch = [pltpu.make_async_copy(w_far.at[at], w_ref.at[at], sem.at[n]) for n, at in enumerate(quarters)]
+    for copy in fetch:
+        copy.start()
+    squares = []
+    for q in range(8):
+        wide = across_ref[:, q * 128 : (q + 1) * 128].astype(f32)
+        squares.append(jnp.sum(wide * wide, axis=0, keepdims=True))
     rows = rows_ref[...]
     tops = []
     for n in range(4):
+        fetch[n].wait()
         part = matmul(rows, w_ref[:, n * 256 : (n + 1) * 256], ((1,), (0,))).reshape(8, 64, 256)
         size = jnp.abs(part)
         top = (jnp.max(size, axis=1, keepdims=True) * (1 + 2.0**-7) + 1e-30).astype(bf16).astype(f32)
@@ -69,7 +76,7 @@
             lanes = slice(h * 128, (h + 1) * 128)
             sent_ref[:, at, :] = code[:, :, lanes]
             tops.append(top[:, :, lanes])
-    squares = jnp.broadcast_to(squares_ref[...][None], (8, 8, 128))
+    squares = jnp.broadcast_to(jnp.concatenate(squares, axis=0)[None], (8, 8, 128))
     sent_ref[:, 512:528, :] = jnp.concatenate([squares] + tops, axis=1).astype(bf16)
 
 
@@ -102,8 +109,8 @@
 
 
 def residue(got_ref, bias_ref, residual_ref, penalty_ref, out_ref):
-    recon = jnp.sum(got_ref[...].astype(f32).reshape(32, 8, 576), axis=0) + bias_ref[...]
-    err = recon - residual_ref[...]
+    recon = jnp.sum(got_ref[...].astype(f32).reshape(32, 8, 576), axis=0) + bias_ref[...][None, :]
+    err = recon - residual_ref[...].astype(f32)
     total = jnp.sum(err * err, axis=(0, 1), keepdims=True) + jnp.sum(penalty_ref[...], axis=(0, 1), keepdims=True)
     high = total.astype(bf16).astype(f32)
     row = lax.broadcasted_iota(jnp.int32, (8, 64), 0)
@@ -141,8 +148,7 @@
     loss_ref[...] = jnp.sum(total, axis=(0, 1), keepdims=True) / (ROWS * D)
 
 
-def decoder_gradient(acts_ref, err_ref, w_ref, norms_ref, far_ref, bias_ref, out_ref, sem):
-    out = quarters(out_ref, far_ref, sem)
+def decoder_gradient(acts_ref, err_ref, w_ref, norms_ref, out_ref, bias_ref):
     err = err_ref[:, :576]
     bias_ref[...] = jnp.sum(err.astype(f32), axis=0).astype(bf16)
     for n in range(4):
@@ -154,13 +160,9 @@
         scale = penalty_weight / 16.0 * jnp.sum(acts.astype(f32), axis=0, keepdims=True) / norms
         outer = matmul(err, acts, ((0,), (0,)))
         out_ref[:, at] = (outer + scale * w_ref[:, at].astype(f32)).astype(bf16)
-        out[n].start()
-    for copy in out:
-        copy.wait()
-
-
-def encoder_gradient(rows_ref, d_pre_ref, far_ref, bias_ref, out_ref, sem):
-    out = quarters(out_ref, far_ref, sem)
+
+
+def encoder_gradient(rows_ref, d_pre_ref, out_ref, bias_ref):
     rows = rows_ref[...]
     sums = []
     for n in range(4):
@@ -168,10 +170,7 @@
         sums += [jnp.sum(part.astype(f32), axis=0, keepdims=True) for part in pair]
         d_pre = jnp.concatenate(pair, axis=1)
         out_ref[:, n * 256 : (n + 1) * 256] = matmul(rows, d_pre, ((0,), (0,))).astype(bf16)
-        out[n].start()
     bias_ref[...] = jnp.concatenate(sums, axis=0).astype(bf16)
-    for copy in out:
-        copy.wait()
 
 
 def exchange(blocks, axes):
@@ -183,20 +182,24 @@
     work = 2 * 512 * 576 * 1024
     near = call(spread_rows, [((256, 576), bf16)], residual)[0]
     half = lax.axis_index("c").astype(jnp.int32).reshape(1)
-    small = (half, b_dec.reshape(1, 576), residual.astype(f32), b_enc.reshape(8, 128))
-    near, small = lax.optimization_barrier((exchange(near.reshape(32, 8, 576), CHIPS), small))
-    half, bias_dec, residual, bias_enc = small
-    near = near.reshape(256, 576)
+    near, half = lax.optimization_barrier((near, half))
+    near = exchange(near.reshape(32, 8, 576), CHIPS).reshape(256, 576)
     rows_all = lax.all_gather(near, "c", axis=0, tiled=True)
-    wide = w_across.astype(f32)
-    squares = jnp.sum(wide * wide, axis=0).reshape(8, 128)
-
-    sent = call(encode, [((8, 528, 128), bf16)], rows_all, w_enc, squares, flops=work)[0]
+    sent = call(
+        encode,
+        [((8, 528, 128), bf16)],
+        rows_all,
+        w_enc,
+        w_across,
+        flops=work,
+        far=(1,),
+        scratch=(pltpu.VMEM((576, 1024), bf16), pltpu.SemaphoreType.DMA((4,))),
+    )[0]
     acts, pre, norms, penalty = call(
         activate,
         [((8, 512, 128), bf16), ((512, 128), f32), ((8, 128), f32), ((1, 128), f32)],
         exchange(sent, LAYER),
-        bias_enc,
+        b_enc.reshape(8, 128),
     )
     acts = exchange(acts, LAYER)
 
@@ -210,7 +213,7 @@
         residue,
         [((256, 640), bf16)],
         recon.reshape(256, 576),
-        bias_dec,
+        b_dec,
         residual,
         penalty,
     )[0]
@@ -220,15 +223,14 @@
     sent = call(decode_back, [((8, 528, 128), bf16)], err, w_across, flops=work)[0]
     got, acts, err = lax.optimization_barrier((exchange(sent, LAYER), acts, err))
     d_pre, loss = call(mask, [((8, 512, 128), bf16), ((1, 1), f32)], got, pre, norms)
-    kept = dict(flops=work, far=(0,), scratch=(pltpu.VMEM((576, 1024), bf16), pltpu.SemaphoreType.DMA((4,))))
     grad_dec, grad_bdec = call(
-        decoder_gradient, [((576, 1024), bf16), ((576,), bf16)], acts, err, w_across, norms, **kept
+        decoder_gradient, [((576, 1024), bf16), ((576,), bf16)], acts, err, w_across, norms, flops=work
     )
     d_pre, grad_dec, grad_bdec, loss = lax.optimization_barrier(
         (d_pre, grad_dec, grad_bdec.reshape(576), loss.reshape(()))
     )
     grad_enc, grad_benc = call(
-        encoder_gradient, [((576, 1024), bf16), ((8, 128), bf16)], rows_all, exchange(d_pre, LAYER), **kept
+        encoder_gradient, [((576, 1024), bf16), ((8, 128), bf16)], rows_all, exchange(d_pre, LAYER), flops=work
     )
     return (
         grad_enc,

time: 166 us -> 166 us (level)
  blocking collectives: 123 us -> 153 us
  starting transfers between devices: 16.5 us -> 0 us
  waiting for transfers between devices: 10.6 us -> 0 us
  other arithmetic: 2.35 us -> 0 us
    all_to_all x6 -> x7, blocking collectives: 109 us -> 139 us  [exchange(): return lax.all_to_all(blocks, axes, 0, 0, tiled=True)]
    all_to_all x1 -> x0, starting transfers between devices: 16.5 us -> none  [exchange(): return lax.all_to_all(blocks, axes, 0, 0, tiled=True)]
    all_to_all x1 -> x0, waiting for transfers between devices: 10.6 us -> none  [exchange(): return lax.all_to_all(blocks, axes, 0, 0, tiled=True)]
  transfers between devices with their start and end apart: 1 -> 0, of which waited for: 1 -> 0; matrix products, arithmetic and copies ran while one was open for 2% -> 0% of each run, Pallas kernels for 0% -> 0%
where the time goes in v7:
time: 166 us
  blocking collectives  153 us (92%)
  Pallas kernels  11 us (7%)
    all_to_all x7, blocking collectives, exchange(): return lax.all_to_all(blocks, axes, 0, 0, tiled=True)  139 us
    pallas_call x10, Pallas kernels, call(): pl.pallas_call(body, out_shape=outs, in_specs=[pl.BlockSpec(memory_space=...  11 us
    all_gather x1, blocking collectives, local(): err = lax.all_gather(packed, 'c', axis=0, tiled=True)  5.22 us
    all_gather x1, blocking collectives, local(): rows_all = lax.all_gather(near, 'c', axis=0, tiled=True)  4.67 us
    all_gather x1, blocking collectives, local(): both = lax.all_gather(other, 'c', axis=0, tiled=True)  4.11 us

profile of v7, /device:TPU:1, one launch (start us, length us, event | category | flops | bytes accessed | tf_op | source)
XLA Modules:
  0.0 165.8 jit_solution(4245065624980606451)
XLA Ops:
  0.6 0.0 copy-start
  0.6 0.0 copy-start.1
  0.7 0.8 copy-done.1
  1.5 29.9 %all_to_all.35 = bf16[32,8,576]{2,1,0:T(8,128)(2,1)S(1)} all-to-all(bf16[32,8,576]{2,1,0:T(8,128)(2,1)S(1)} %bitcast.18), channel_id=1, replica_groups=mesh['x'=4,'yl'=2,'z'=8,'yh'=4,'c'=2] {'z','yh'}, dimensions={0} | all-to-all | bytes 589824 | tf_op jit(solution)/shard_map/all_to_all | solution.py:177
  31.4 4.7 %all_gather.9.rows_ref = bf16[512,576]{1,0:T(8,128)(2,1)S(1)} all-gather(bf16[256,576]{1,0:T(8,128)(2,1)S(1)} %bitcast.21), channel_id=1, replica_groups=mesh['x'=4,'yl'=2,'z'=8,'yh'=4,'c'=2] {'c'}, dimensions={0}, use_global_device_ids=true | all-gather | bytes 884736 | tf_op jit(solution)/shard_map/all_gather | solution.py:187
  36.1 0.0 copy-done
  36.1 3.5 %shard_map.93 = bf16[8,528,128]{2,1,0:T(8,128)(2,1)S(1)} custom-call(bf16[512,576]{1,0:T(8,128)(2,1)S(1)} %all_gather.9.rows_ref, bf16[576,1024]{1,0:T(8,128)(2,1)} %w_far.1, bf16[576,1024]{1,0:T(8,128)(2,1)S(1)} %bitcast.12), custom_call_target="tpu_custom_call" | custom-call | flops 603979776 | bytes 4030464 | tf_op jit(solution)/shard_map/pallas_call | solution.py:28
  39.6 0.0 copy-start.3
  39.7 19.4 %all_to_all.36.got_ref = bf16[8,528,128]{2,1,0:T(8,128)(2,1)S(1)} all-to-all(bf16[8,528,128]{2,1,0:T(8,128)(2,1)S(1)} %shard_map.93), channel_id=1, replica_groups=mesh['x'=4,'yl'=2,'z'=8,'yh'=4,'c'=2] {'x','yl'}, dimensions={0} | all-to-all | bytes 2162688 | tf_op jit(solution)/shard_map/all_to_all | solution.py:177
  59.1 0.0 copy-done.3
  59.1 0.7 shard_map.94
  59.8 17.2 %all_to_all.37.acts_ref = bf16[8,512,128]{2,1,0:T(8,128)(2,1)S(1)} all-to-all(bf16[8,512,128]{2,1,0:T(8,128)(2,1)S(1)} %get-tuple-element.28), channel_id=1, replica_groups=mesh['x'=4,'yl'=2,'z'=8,'yh'=4,'c'=2] {'x','yl'}, dimensions={0} | all-to-all | bytes 2097152 | tf_op jit(solution)/shard_map/all_to_all | solution.py:177
  76.9 1.0 shard_map.95
  78.0 4.1 %all_gather.10.both_ref = bf16[512,576]{1,0:T(8,128)(2,1)S(1)} all-gather(bf16[256,576]{1,0:T(8,128)(2,1)S(1)} %get-tuple-element.29), channel_id=1, replica_groups=mesh['x'=4,'yl'=2,'z'=8,'yh'=4,'c'=2] {'c'}, dimensions={0}, use_global_device_ids=true | all-gather | bytes 884736 | tf_op jit(solution)/shard_map/all_gather | solution.py:209
  82.1 0.0 copy-start.2
  82.1 0.0 copy-start.4
  82.1 0.1 shard_map.96
  82.1 17.6 %all_to_all.38 = bf16[32,8,576]{2,1,0:T(8,128)(2,1)S(1)} all-to-all(bf16[32,8,576]{2,1,0:T(8,128)(2,1)S(1)} %bitcast.19), channel_id=1, replica_groups=mesh['x'=4,'yl'=2,'z'=8,'yh'=4,'c'=2] {'z','yh'}, dimensions={0} | all-to-all | bytes 589824 | tf_op jit(solution)/shard_map/all_to_all | solution.py:177
  99.7 0.0 copy-done.2
  99.7 0.0 copy-done.4
  99.7 0.3 shard_map.97
  100.0 18.8 %all_to_all.39 = bf16[32,8,640]{2,1,0:T(8,128)(2,1)S(1)} all-to-all(bf16[32,8,640]{2,1,0:T(8,128)(2,1)S(1)} %bitcast.17), channel_id=1, replica_groups=mesh['x'=4,'yl'=2,'z'=8,'yh'=4,'c'=2] {'z','yh'}, dimensions={0} | all-to-all | bytes 655360 | tf_op jit(solution)/shard_map/all_to_all | solution.py:177
  118.8 5.2 %all_gather.11.err_ref = bf16[512,640]{1,0:T(8,128)(2,1)S(1)} all-gather(bf16[256,640]{1,0:T(8,128)(2,1)S(1)} %bitcast.22), channel_id=1, replica_groups=mesh['x'=4,'yl'=2,'z'=8,'yh'=4,'c'=2] {'c'}, dimensions={0}, use_global_device_ids=true | all-gather | bytes 983040 | tf_op jit(solution)/shard_map/all_gather | solution.py:221
  124.0 1.0 shard_map.98
  125.0 19.2 %all_to_all.40.got_ref = bf16[8,528,128]{2,1,0:T(8,128)(2,1)S(1)} all-to-all(bf16[8,528,128]{2,1,0:T(8,128)(2,1)S(1)} %shard_map.98), channel_id=1, replica_groups=mesh['x'=4,'yl'=2,'z'=8,'yh'=4,'c'=2] {'x','yl'}, dimensions={0} | all-to-all | bytes 2162688 | tf_op jit(solution)/shard_map/all_to_all | solution.py:177
  144.2 0.8 shard_map.99
  145.0 1.8 %shard_map.100 = (bf16[576,1024]{1,0:T(8,128)(2,1)}, bf16[576]{0:T(1024)(128)(2,1)}) custom-call(bf16[8,512,128]{2,1,0:T(8,128)(2,1)S(1)} %all_to_all.37.acts_ref, bf16[512,640]{1,0:T(8,128)(2,1)S(1)} %all_gather.11.err_ref, bf16[576,1024]{1,0:T(8,128)(2,1)S(1)} %bitcast.15, f32[8,128]{1,0:T(8,128)S(1)} %get-tuple-element.34.norms_ref), custom_call_target="tpu_custom_call" | custom-call | flops 603979776 | bytes 4068480 | tf_op jit(solution)/shard_map/pallas_call | solution.py:28
  146.8 17.2 %all_to_all.41.d_pre_ref = bf16[8,512,128]{2,1,0:T(8,128)(2,1)S(1)} all-to-all(bf16[8,512,128]{2,1,0:T(8,128)(2,1)S(1)} %get-tuple-element.41), channel_id=1, replica_groups=mesh['x'=4,'yl'=2,'z'=8,'yh'=4,'c'=2] {'x','yl'}, dimensions={0} | all-to-all | bytes 2097152 | tf_op jit(solution)/shard_map/all_to_all | solution.py:177
  164.0 1.8 %shard_map.101 = (bf16[576,1024]{1,0:T(8,128)(2,1)}, bf16[8,128]{1,0:T(8,128)(2,1)}) custom-call(bf16[512,576]{1,0:T(8,128)(2,1)S(1)} %all_gather.9.rows_ref, bf16[8,512,128]{2,1,0:T(8,128)(2,1)S(1)} %all_to_all.41.d_pre_ref), custom_call_target="tpu_custom_call" | custom-call | flops 603979776 | bytes 2820096 | tf_op jit(solution)/shard_map/pallas_call | solution.py:28
  (1 shorter events, 0.0 us)
Async XLA Ops:
  0.6 35.5 %copy-start = (bf16[1024,576]{0,1:T(8,128)(2,1)S(1)}, bf16[1024,576]{0,1:T(8,128)(2,1)}, u32[]{:S(2)}) copy-start(bf16[1024,576]{0,1:T(8,128)(2,1)} %param.8) | copy-start | bytes 3538948
  0.6 0.8 copy-start.1
  39.6 19.4 %copy-start.3 = (f32[1024]{0:T(1024)S(1)}, f32[1024]{0:T(1024)}, u32[]{:S(2)}) copy-start(f32[1024]{0:T(1024)} %param.7) | copy-start | bytes 12292
  82.1 17.7 %copy-start.2 = (bf16[8,576]{1,0:T(8,128)(2,1)S(1)}, bf16[8,576]{1,0:T(8,128)(2,1)}, u32[]{:S(2)}) copy-start(bf16[8,576]{1,0:T(8,128)(2,1)} %residual_ref.1) | copy-start | bytes 27652
  82.1 17.7 %copy-start.4 = (f32[576]{0:T(1024)S(1)}, f32[576]{0:T(1024)}, u32[]{:S(2)}) copy-start(f32[576]{0:T(1024)} %bias_ref.1) | copy-start | bytes 6916

commit v8 on v6

--- a/solution.py
+++ b/solution.py
@@ -33,11 +33,6 @@
     )(*args)
 
 
-def quarters(source, target, sem):
-    at = [(slice(None), pl.ds(n * 256, 256)) for n in range(4)]
-    return [pltpu.make_async_copy(source.at[i], target.at[i], sem.at[n]) for n, i in enumerate(at)]
-
-
 def matmul(a, b, dims):
     return lax.dot_general(a, b, (dims, ((), ())), preferred_element_type=f32)
 
@@ -50,9 +45,12 @@
 STEPS = 252.0
 
 
-def spread_rows(rows_ref, out_ref):
+def spread_rows(rows_ref, across_ref, out_ref, squares_ref):
     rows = rows_ref[...].astype(f32)
     out_ref[...] = jnp.broadcast_to(rows[None], (32, 8, 576)).reshape(256, 576).astype(bf16)
+    for q in range(8):
+        wide = across_ref[:, q * 128 : (q + 1) * 128].astype(f32)
+        squares_ref[q : q + 1, :] = jnp.sum(wide * wide, axis=0, keepdims=True)
 
 
 def encode(rows_ref, w_ref, squares_ref, sent_ref):
@@ -102,8 +100,8 @@
 
 
 def residue(got_ref, bias_ref, residual_ref, penalty_ref, out_ref):
-    recon = jnp.sum(got_ref[...].astype(f32).reshape(32, 8, 576), axis=0) + bias_ref[...]
-    err = recon - residual_ref[...]
+    recon = jnp.sum(got_ref[...].astype(f32).reshape(32, 8, 576), axis=0) + bias_ref[...][None, :]
+    err = recon - residual_ref[...].astype(f32)
     total = jnp.sum(err * err, axis=(0, 1), keepdims=True) + jnp.sum(penalty_ref[...], axis=(0, 1), keepdims=True)
     high = total.astype(bf16).astype(f32)
     row = lax.broadcasted_iota(jnp.int32, (8, 64), 0)
@@ -141,8 +139,7 @@
     loss_ref[...] = jnp.sum(total, axis=(0, 1), keepdims=True) / (ROWS * D)
 
 
-def decoder_gradient(acts_ref, err_ref, w_ref, norms_ref, far_ref, bias_ref, out_ref, sem):
-    out = quarters(out_ref, far_ref, sem)
+def decoder_gradient(acts_ref, err_ref, w_ref, norms_ref, out_ref, bias_ref):
     err = err_ref[:, :576]
     bias_ref[...] = jnp.sum(err.astype(f32), axis=0).astype(bf16)
     for n in range(4):
@@ -154,13 +151,9 @@
         scale = penalty_weight / 16.0 * jnp.sum(acts.astype(f32), axis=0, keepdims=True) / norms
         outer = matmul(err, acts, ((0,), (0,)))
         out_ref[:, at] = (outer + scale * w_ref[:, at].astype(f32)).astype(bf16)
-        out[n].start()
-    for copy in out:
-        copy.wait()
-
-
-def encoder_gradient(rows_ref, d_pre_ref, far_ref, bias_ref, out_ref, sem):
-    out = quarters(out_ref, far_ref, sem)
+
+
+def encoder_gradient(rows_ref, d_pre_ref, out_ref, bias_ref):
     rows = rows_ref[...]
     sums = []
     for n in range(4):
@@ -168,10 +161,19 @@
         sums += [jnp.sum(part.astype(f32), axis=0, keepdims=True) for part in pair]
         d_pre = jnp.concatenate(pair, axis=1)
         out_ref[:, n * 256 : (n + 1) * 256] = matmul(rows, d_pre, ((0,), (0,))).astype(bf16)
-        out[n].start()
     bias_ref[...] = jnp.concatenate(sums, axis=0).astype(bf16)
-    for copy in out:
-        copy.wait()
+
+
+def gradients(acts_ref, err_ref, w_ref, norms_ref, rows_ref, d_pre_ref, dec_far, dec_bias, enc_far, enc_bias, *own):
+    dec_ref, enc_ref, dec_sem, enc_sem = own
+    decoder_gradient(acts_ref, err_ref, w_ref, norms_ref, dec_ref, dec_bias)
+    dec_out = pltpu.make_async_copy(dec_ref, dec_far, dec_sem)
+    dec_out.start()
+    encoder_gradient(rows_ref, d_pre_ref, enc_ref, enc_bias)
+    enc_out = pltpu.make_async_copy(enc_ref, enc_far, enc_sem)
+    enc_out.start()
+    dec_out.wait()
+    enc_out.wait()
 
 
 def exchange(blocks, axes):
@@ -181,22 +183,17 @@
 def local(residual, w_enc, b_enc, w_dec, b_dec):
     w_across = w_dec.T
     work = 2 * 512 * 576 * 1024
-    near = call(spread_rows, [((256, 576), bf16)], residual)[0]
+    near, squares = call(spread_rows, [((256, 576), bf16), ((8, 128), f32)], residual, w_across)
     half = lax.axis_index("c").astype(jnp.int32).reshape(1)
-    small = (half, b_dec.reshape(1, 576), residual.astype(f32), b_enc.reshape(8, 128))
-    near, small = lax.optimization_barrier((exchange(near.reshape(32, 8, 576), CHIPS), small))
-    half, bias_dec, residual, bias_enc = small
-    near = near.reshape(256, 576)
+    near, half = lax.optimization_barrier((near, half))
+    near = exchange(near.reshape(32, 8, 576), CHIPS).reshape(256, 576)
     rows_all = lax.all_gather(near, "c", axis=0, tiled=True)
-    wide = w_across.astype(f32)
-    squares = jnp.sum(wide * wide, axis=0).reshape(8, 128)
-
     sent = call(encode, [((8, 528, 128), bf16)], rows_all, w_enc, squares, flops=work)[0]
     acts, pre, norms, penalty = call(
         activate,
         [((8, 512, 128), bf16), ((512, 128), f32), ((8, 128), f32), ((1, 128), f32)],
         exchange(sent, LAYER),
-        bias_enc,
+        b_enc.reshape(8, 128),
     )
     acts = exchange(acts, LAYER)
 
@@ -210,7 +207,7 @@
         residue,
         [((256, 640), bf16)],
         recon.reshape(256, 576),
-        bias_dec,
+        b_dec,
         residual,
         penalty,
     )[0]
@@ -218,17 +215,21 @@
     err = lax.all_gather(packed, "c", axis=0, tiled=True)
 
     sent = call(decode_back, [((8, 528, 128), bf16)], err, w_across, flops=work)[0]
-    got, acts, err = lax.optimization_barrier((exchange(sent, LAYER), acts, err))
-    d_pre, loss = call(mask, [((8, 512, 128), bf16), ((1, 1), f32)], got, pre, norms)
-    kept = dict(flops=work, far=(0,), scratch=(pltpu.VMEM((576, 1024), bf16), pltpu.SemaphoreType.DMA((4,))))
-    grad_dec, grad_bdec = call(
-        decoder_gradient, [((576, 1024), bf16), ((576,), bf16)], acts, err, w_across, norms, **kept
-    )
-    d_pre, grad_dec, grad_bdec, loss = lax.optimization_barrier(
-        (d_pre, grad_dec, grad_bdec.reshape(576), loss.reshape(()))
-    )
-    grad_enc, grad_benc = call(
-        encoder_gradient, [((576, 1024), bf16), ((8, 128), bf16)], rows_all, exchange(d_pre, LAYER), **kept
+    d_pre, loss = call(mask, [((8, 512, 128), bf16), ((1, 1), f32)], exchange(sent, LAYER), pre, norms)
+    d_pre, loss = lax.optimization_barrier((d_pre, loss.reshape(())))
+    weights, wide = ((576, 1024), bf16), pltpu.VMEM((576, 1024), bf16)
+    grad_dec, grad_bdec, grad_enc, grad_benc = call(
+        gradients,
+        [weights, ((576,), bf16), weights, ((8, 128), bf16)],
+        acts,
+        err,
+        w_across,
+        norms,
+        rows_all,
+        exchange(d_pre, LAYER),
+        flops=2 * work,
+        far=(0, 2),
+        scratch=(wide, wide, pltpu.SemaphoreType.DMA, pltpu.SemaphoreType.DMA),
     )
     return (
         grad_enc,

time: 166 us -> 166 us (level)
  blocking collectives: 123 us -> 153 us
  starting transfers between devices: 16.5 us -> 0 us
  waiting for transfers between devices: 10.6 us -> 0 us
  other arithmetic: 2.35 us -> 0 us
  Pallas kernels: 10.6 us -> 8.73 us
    all_to_all x6 -> x7, blocking collectives: 109 us -> 139 us  [exchange(): return lax.all_to_all(blocks, axes, 0, 0, tiled=True)]
    all_to_all x1 -> x0, starting transfers between devices: 16.5 us -> none  [exchange(): return lax.all_to_all(blocks, axes, 0, 0, tiled=True)]
    all_to_all x1 -> x0, waiting for transfers between devices: 10.6 us -> none  [exchange(): return lax.all_to_all(blocks, axes, 0, 0, tiled=True)]
    pallas_call x10 -> x9, Pallas kernels: 10.6 us -> 8.73 us  [call(): pl.pallas_call(body, out_shape=outs, in_specs=[pl.BlockSpec(memory_space=...]
  transfers between devices with their start and end apart: 1 -> 0, of which waited for: 1 -> 0; matrix products, arithmetic and copies ran while one was open for 2% -> 0% of each run, Pallas kernels for 0% -> 0%
where the time goes in v8:
time: 166 us; the launch traced here: 165 us
  blocking collectives  153 us (92%)
  Pallas kernels  8.73 us (5%)
  local copies, waits for them, and re-layouts  1.99 us (1%)
    all_to_all x7, blocking collectives, exchange(): return lax.all_to_all(blocks, axes, 0, 0, tiled=True)  139 us
    pallas_call x9, Pallas kernels, call(): pl.pallas_call(body, out_shape=outs, in_specs=[pl.BlockSpec(memory_space=...  8.73 us
    all_gather x1, blocking collectives, local(): err = lax.all_gather(packed, 'c', axis=0, tiled=True)  5.21 us
    all_gather x1, blocking collectives, local(): rows_all = lax.all_gather(near, 'c', axis=0, tiled=True)  4.67 us
    all_gather x1, blocking collectives, local(): both = lax.all_gather(other, 'c', axis=0, tiled=True)  4.11 us

profile of v8, /device:TPU:1, one launch (start us, length us, event | category | flops | bytes accessed | tf_op | source)
XLA Modules:
  0.0 164.9 jit_solution(2577724965756821205)
XLA Ops:
  0.6 0.0 copy-start
  0.6 1.3 copy-done
  1.9 0.0 copy-start.3
  1.9 0.7 copy-done.3
  2.6 0.0 copy-start.2
  2.6 0.3 shard_map.92
  2.9 30.1 %all_to_all.35 = bf16[32,8,576]{2,1,0:T(8,128)(2,1)S(1)} all-to-all(bf16[32,8,576]{2,1,0:T(8,128)(2,1)S(1)} %bitcast.19), channel_id=1, replica_groups=mesh['x'=4,'yl'=2,'z'=8,'yh'=4,'c'=2] {'z','yh'}, dimensions={0} | all-to-all | bytes 589824 | tf_op jit(solution)/shard_map/all_to_all | solution.py:180
  33.0 4.7 %all_gather.9.rows_ref = bf16[512,576]{1,0:T(8,128)(2,1)S(1)} all-gather(bf16[256,576]{1,0:T(8,128)(2,1)S(1)} %bitcast.21), channel_id=1, replica_groups=mesh['x'=4,'yl'=2,'z'=8,'yh'=4,'c'=2] {'c'}, dimensions={0}, use_global_device_ids=true | all-gather | bytes 884736 | tf_op jit(solution)/shard_map/all_gather | solution.py:190
  37.6 0.0 copy-done.2
  37.6 1.5 shard_map.93
  39.2 0.0 copy-start.5
  39.2 19.4 %all_to_all.36.got_ref = bf16[8,528,128]{2,1,0:T(8,128)(2,1)S(1)} all-to-all(bf16[8,528,128]{2,1,0:T(8,128)(2,1)S(1)} %shard_map.93), channel_id=1, replica_groups=mesh['x'=4,'yl'=2,'z'=8,'yh'=4,'c'=2] {'x','yl'}, dimensions={0} | all-to-all | bytes 2162688 | tf_op jit(solution)/shard_map/all_to_all | solution.py:180
  58.6 0.0 copy-done.5
  58.6 0.7 shard_map.94
  59.3 0.0 copy-start.1
  59.3 17.3 %all_to_all.37.acts_ref = bf16[8,512,128]{2,1,0:T(8,128)(2,1)S(1)} all-to-all(bf16[8,512,128]{2,1,0:T(8,128)(2,1)S(1)} %get-tuple-element.26), channel_id=1, replica_groups=mesh['x'=4,'yl'=2,'z'=8,'yh'=4,'c'=2] {'x','yl'}, dimensions={0} | all-to-all | bytes 2097152 | tf_op jit(solution)/shard_map/all_to_all | solution.py:180
  76.6 0.0 copy-done.1
  76.6 1.0 shard_map.95
  77.6 4.1 %all_gather.10.both_ref = bf16[512,576]{1,0:T(8,128)(2,1)S(1)} all-gather(bf16[256,576]{1,0:T(8,128)(2,1)S(1)} %get-tuple-element.28), channel_id=1, replica_groups=mesh['x'=4,'yl'=2,'z'=8,'yh'=4,'c'=2] {'c'}, dimensions={0}, use_global_device_ids=true | all-gather | bytes 884736 | tf_op jit(solution)/shard_map/all_gather | solution.py:203
  81.7 0.0 copy-start.4
  81.8 0.0 copy-start.6
  81.8 0.1 shard_map.96
  81.8 17.6 %all_to_all.38 = bf16[32,8,576]{2,1,0:T(8,128)(2,1)S(1)} all-to-all(bf16[32,8,576]{2,1,0:T(8,128)(2,1)S(1)} %bitcast.18), channel_id=1, replica_groups=mesh['x'=4,'yl'=2,'z'=8,'yh'=4,'c'=2] {'z','yh'}, dimensions={0} | all-to-all | bytes 589824 | tf_op jit(solution)/shard_map/all_to_all | solution.py:180
  99.4 0.0 copy-done.4
  99.4 0.0 copy-done.6
  99.4 0.3 shard_map.97
  99.7 18.8 %all_to_all.39 = bf16[32,8,640]{2,1,0:T(8,128)(2,1)S(1)} all-to-all(bf16[32,8,640]{2,1,0:T(8,128)(2,1)S(1)} %bitcast.17), channel_id=1, replica_groups=mesh['x'=4,'yl'=2,'z'=8,'yh'=4,'c'=2] {'z','yh'}, dimensions={0} | all-to-all | bytes 655360 | tf_op jit(solution)/shard_map/all_to_all | solution.py:180
  118.4 5.2 %all_gather.11.err_ref = bf16[512,640]{1,0:T(8,128)(2,1)S(1)} all-gather(bf16[256,640]{1,0:T(8,128)(2,1)S(1)} %bitcast.22), channel_id=1, replica_groups=mesh['x'=4,'yl'=2,'z'=8,'yh'=4,'c'=2] {'c'}, dimensions={0}, use_global_device_ids=true | all-gather | bytes 983040 | tf_op jit(solution)/shard_map/all_gather | solution.py:215
  123.7 1.0 shard_map.98
  124.6 19.1 %all_to_all.40.got_ref = bf16[8,528,128]{2,1,0:T(8,128)(2,1)S(1)} all-to-all(bf16[8,528,128]{2,1,0:T(8,128)(2,1)S(1)} %shard_map.98), channel_id=1, replica_groups=mesh['x'=4,'yl'=2,'z'=8,'yh'=4,'c'=2] {'x','yl'}, dimensions={0} | all-to-all | bytes 2162688 | tf_op jit(solution)/shard_map/all_to_all | solution.py:180
  143.8 0.8 shard_map.99
  144.6 17.2 %all_to_all.41.d_pre_ref = bf16[8,512,128]{2,1,0:T(8,128)(2,1)S(1)} all-to-all(bf16[8,512,128]{2,1,0:T(8,128)(2,1)S(1)} %get-tuple-element.35), channel_id=1, replica_groups=mesh['x'=4,'yl'=2,'z'=8,'yh'=4,'c'=2] {'x','yl'}, dimensions={0} | all-to-all | bytes 2097152 | tf_op jit(solution)/shard_map/all_to_all | solution.py:180
  161.8 3.1 %shard_map.100 = (bf16[576,1024]{1,0:T(8,128)(2,1)}, bf16[576]{0:T(1024)(128)(2,1)}, bf16[576,1024]{1,0:T(8,128)(2,1)}, bf16[8,128]{1,0:T(8,128)(2,1)}) custom-call(bf16[8,512,128]{2,1,0:T(8,128)(2,1)S(1)} %all_to_all.37.acts_ref, bf16[512,640]{1,0:T(8,128)(2,1)S(1)} %all_gather.11.err_ref, bf16[576,1024]{1,0:T(8,128)(2,1)S(1)} %bitcast.15, ...), custom_call_target="tpu_custom_call" | custom-call | flops 1207959552 | bytes 6888576 | tf_op jit(solution)/shard_map/pallas_call | solution.py:23
Async XLA Ops:
  0.6 1.3 copy-start
  1.9 0.7 copy-start.3
  2.6 35.0 %copy-start.2 = (bf16[576,1024]{1,0:T(8,128)(2,1)S(1)}, bf16[576,1024]{1,0:T(8,128)(2,1)}, u32[]{:S(2)}) copy-start(bf16[576,1024]{1,0:T(8,128)(2,1)} %w_ref.1) | copy-start | bytes 3538948
  39.2 19.4 %copy-start.5 = (f32[1024]{0:T(1024)S(1)}, f32[1024]{0:T(1024)}, u32[]{:S(2)}) copy-start(f32[1024]{0:T(1024)} %param.7) | copy-start | bytes 12292
  59.3 17.3 %copy-start.1 = (bf16[1024,576]{0,1:T(8,128)(2,1)S(1)}, bf16[1024,576]{0,1:T(8,128)(2,1)}, u32[]{:S(2)}) copy-start(bf16[1024,576]{0,1:T(8,128)(2,1)} %param.8) | copy-start | bytes 3538948
  81.7 17.6 %copy-start.4 = (bf16[8,576]{1,0:T(8,128)(2,1)S(1)}, bf16[8,576]{1,0:T(8,128)(2,1)}, u32[]{:S(2)}) copy-start(bf16[8,576]{1,0:T(8,128)(2,1)} %residual_ref.1) | copy-start | bytes 27652
  81.8 17.6 %copy-start.6 = (f32[576]{0:T(1024)S(1)}, f32[576]{0:T(1024)}, u32[]{:S(2)}) copy-start(f32[576]{0:T(1024)} %bias_ref.1) | copy-start | bytes 6916

commit v9 on v8

--- a/solution.py
+++ b/solution.py
@@ -45,9 +45,12 @@
 STEPS = 252.0
 
 
-def spread_rows(rows_ref, across_ref, out_ref, squares_ref):
+def spread_rows(rows_ref, out_ref):
     rows = rows_ref[...].astype(f32)
     out_ref[...] = jnp.broadcast_to(rows[None], (32, 8, 576)).reshape(256, 576).astype(bf16)
+
+
+def sum_squares(across_ref, _, squares_ref):
     for q in range(8):
         wide = across_ref[:, q * 128 : (q + 1) * 128].astype(f32)
         squares_ref[q : q + 1, :] = jnp.sum(wide * wide, axis=0, keepdims=True)
@@ -183,11 +186,12 @@
 def local(residual, w_enc, b_enc, w_dec, b_dec):
     w_across = w_dec.T
     work = 2 * 512 * 576 * 1024
-    near, squares = call(spread_rows, [((256, 576), bf16), ((8, 128), f32)], residual, w_across)
+    near = call(spread_rows, [((256, 576), bf16)], residual)[0]
     half = lax.axis_index("c").astype(jnp.int32).reshape(1)
     near, half = lax.optimization_barrier((near, half))
-    near = exchange(near.reshape(32, 8, 576), CHIPS).reshape(256, 576)
-    rows_all = lax.all_gather(near, "c", axis=0, tiled=True)
+    near = exchange(near.reshape(32, 8, 576), CHIPS)
+    rows_all = lax.all_gather(near.reshape(256, 576), "c", axis=0, tiled=True)
+    squares = call(sum_squares, [((8, 128), f32)], w_across, rows_all)[0]
     sent = call(encode, [((8, 528, 128), bf16)], rows_all, w_enc, squares, flops=work)[0]
     acts, pre, norms, penalty = call(
         activate,

time: 166 us -> 164 us (0.988)
    pallas_call x9 -> x10, Pallas kernels: 8.73 us -> 8.76 us  [call(): pl.pallas_call(body, out_shape=outs, in_specs=[pl.BlockSpec(memory_space=...]
where the time goes in v9:
time: 164 us
  blocking collectives  153 us (93%)
  Pallas kernels  8.76 us (5%)
    all_to_all x7, blocking collectives, exchange(): return lax.all_to_all(blocks, axes, 0, 0, tiled=True)  139 us
    pallas_call x10, Pallas kernels, call(): pl.pallas_call(body, out_shape=outs, in_specs=[pl.BlockSpec(memory_space=...  8.76 us
    all_gather x1, blocking collectives, local(): err = lax.all_gather(packed, 'c', axis=0, tiled=True)  5.22 us
    all_gather x1, blocking collectives, local(): rows_all = lax.all_gather(near.reshape(256, 576), 'c', axis=0, tiled=True)  4.8 us
    all_gather x1, blocking collectives, local(): both = lax.all_gather(other, 'c', axis=0, tiled=True)  4.11 us

profile of v9, /device:TPU:1, one launch (start us, length us, event | category | flops | bytes accessed | tf_op | source)
XLA Modules:
  0.0 163.7 jit_solution(2541423444737302357)
XLA Ops:
  0.6 0.0 copy-start
  0.6 0.0 copy-start.2
  0.7 0.8 copy-done.2
  1.5 29.9 %all_to_all.35 = bf16[32,8,576]{2,1,0:T(8,128)(2,1)S(1)} all-to-all(bf16[32,8,576]{2,1,0:T(8,128)(2,1)S(1)} %bitcast.18), channel_id=1, replica_groups=mesh['x'=4,'yl'=2,'z'=8,'yh'=4,'c'=2] {'z','yh'}, dimensions={0} | all-to-all | bytes 589824 | tf_op jit(solution)/shard_map/all_to_all | solution.py:183
  31.4 0.0 copy-start.1
  31.4 4.8 %all_gather.9._.rows_ref = bf16[512,576]{1,0:T(8,128)(2,1)S(1)} all-gather(bf16[256,576]{1,0:T(8,128)(2,1)S(1)} %bitcast.21), channel_id=1, replica_groups=mesh['x'=4,'yl'=2,'z'=8,'yh'=4,'c'=2] {'c'}, dimensions={0}, use_global_device_ids=true | all-gather | bytes 884736 | tf_op jit(solution)/shard_map/all_gather | solution.py:193
  36.2 0.0 copy-done
  36.2 0.3 shard_map.93.squares_ref
  36.5 0.0 copy-done.1
  36.5 1.5 shard_map.94
  38.0 0.0 copy-start.4
  38.1 19.4 %all_to_all.36.got_ref = bf16[8,528,128]{2,1,0:T(8,128)(2,1)S(1)} all-to-all(bf16[8,528,128]{2,1,0:T(8,128)(2,1)S(1)} %shard_map.94), channel_id=1, replica_groups=mesh['x'=4,'yl'=2,'z'=8,'yh'=4,'c'=2] {'x','yl'}, dimensions={0} | all-to-all | bytes 2162688 | tf_op jit(solution)/shard_map/all_to_all | solution.py:183
  57.5 0.0 copy-done.4
  57.5 0.7 shard_map.95
  58.2 17.2 %all_to_all.37.acts_ref = bf16[8,512,128]{2,1,0:T(8,128)(2,1)S(1)} all-to-all(bf16[8,512,128]{2,1,0:T(8,128)(2,1)S(1)} %get-tuple-element.22), channel_id=1, replica_groups=mesh['x'=4,'yl'=2,'z'=8,'yh'=4,'c'=2] {'x','yl'}, dimensions={0} | all-to-all | bytes 2097152 | tf_op jit(solution)/shard_map/all_to_all | solution.py:183
  75.3 1.0 shard_map.96
  76.4 4.1 %all_gather.10.both_ref = bf16[512,576]{1,0:T(8,128)(2,1)S(1)} all-gather(bf16[256,576]{1,0:T(8,128)(2,1)S(1)} %get-tuple-element.24), channel_id=1, replica_groups=mesh['x'=4,'yl'=2,'z'=8,'yh'=4,'c'=2] {'c'}, dimensions={0}, use_global_device_ids=true | all-gather | bytes 884736 | tf_op jit(solution)/shard_map/all_gather | solution.py:207
  80.5 0.0 copy-start.3
  80.5 0.0 copy-start.5
  80.5 0.1 shard_map.97
  80.6 17.6 %all_to_all.38 = bf16[32,8,576]{2,1,0:T(8,128)(2,1)S(1)} all-to-all(bf16[32,8,576]{2,1,0:T(8,128)(2,1)S(1)} %bitcast.19), channel_id=1, replica_groups=mesh['x'=4,'yl'=2,'z'=8,'yh'=4,'c'=2] {'z','yh'}, dimensions={0} | all-to-all | bytes 589824 | tf_op jit(solution)/shard_map/all_to_all | solution.py:183
  98.1 0.0 copy-done.3
  98.1 0.0 copy-done.5
  98.1 0.3 shard_map.98
  98.4 18.8 %all_to_all.39 = bf16[32,8,640]{2,1,0:T(8,128)(2,1)S(1)} all-to-all(bf16[32,8,640]{2,1,0:T(8,128)(2,1)S(1)} %bitcast.17), channel_id=1, replica_groups=mesh['x'=4,'yl'=2,'z'=8,'yh'=4,'c'=2] {'z','yh'}, dimensions={0} | all-to-all | bytes 655360 | tf_op jit(solution)/shard_map/all_to_all | solution.py:183
  117.2 5.2 %all_gather.11.err_ref = bf16[512,640]{1,0:T(8,128)(2,1)S(1)} all-gather(bf16[256,640]{1,0:T(8,128)(2,1)S(1)} %bitcast.22), channel_id=1, replica_groups=mesh['x'=4,'yl'=2,'z'=8,'yh'=4,'c'=2] {'c'}, dimensions={0}, use_global_device_ids=true | all-gather | bytes 983040 | tf_op jit(solution)/shard_map/all_gather | solution.py:219
  122.4 1.0 shard_map.99
  123.4 19.2 %all_to_all.40.got_ref = bf16[8,528,128]{2,1,0:T(8,128)(2,1)S(1)} all-to-all(bf16[8,528,128]{2,1,0:T(8,128)(2,1)S(1)} %shard_map.99), channel_id=1, replica_groups=mesh['x'=4,'yl'=2,'z'=8,'yh'=4,'c'=2] {'x','yl'}, dimensions={0} | all-to-all | bytes 2162688 | tf_op jit(solution)/shard_map/all_to_all | solution.py:183
  142.6 0.8 shard_map.100
  143.4 17.2 %all_to_all.41.d_pre_ref = bf16[8,512,128]{2,1,0:T(8,128)(2,1)S(1)} all-to-all(bf16[8,512,128]{2,1,0:T(8,128)(2,1)S(1)} %get-tuple-element.31), channel_id=1, replica_groups=mesh['x'=4,'yl'=2,'z'=8,'yh'=4,'c'=2] {'x','yl'}, dimensions={0} | all-to-all | bytes 2097152 | tf_op jit(solution)/shard_map/all_to_all | solution.py:183
  160.6 3.1 %shard_map.101 = (bf16[576,1024]{1,0:T(8,128)(2,1)}, bf16[576]{0:T(1024)(128)(2,1)}, bf16[576,1024]{1,0:T(8,128)(2,1)}, bf16[8,128]{1,0:T(8,128)(2,1)}) custom-call(bf16[8,512,128]{2,1,0:T(8,128)(2,1)S(1)} %all_to_all.37.acts_ref, bf16[512,640]{1,0:T(8,128)(2,1)S(1)} %all_gather.11.err_ref, bf16[576,1024]{1,0:T(8,128)(2,1)S(1)} %bitcast.15, ...), custom_call_target="tpu_custom_call" | custom-call | flops 1207959552 | bytes 6888576 | tf_op jit(solution)/shard_map/pallas_call | solution.py:23
  (1 shorter events, 0.0 us)
Async XLA Ops:
  0.6 35.6 %copy-start = (bf16[1024,576]{0,1:T(8,128)(2,1)S(1)}, bf16[1024,576]{0,1:T(8,128)(2,1)}, u32[]{:S(2)}) copy-start(bf16[1024,576]{0,1:T(8,128)(2,1)} %param.8) | copy-start | bytes 3538948
  0.6 0.8 copy-start.2
  31.4 5.1 %copy-start.1 = (bf16[576,1024]{1,0:T(8,128)(2,1)S(1)}, bf16[576,1024]{1,0:T(8,128)(2,1)}, u32[]{:S(2)}) copy-start(bf16[576,1024]{1,0:T(8,128)(2,1)} %w_ref.1) | copy-start | bytes 3538948
  38.0 19.4 %copy-start.4 = (f32[1024]{0:T(1024)S(1)}, f32[1024]{0:T(1024)}, u32[]{:S(2)}) copy-start(f32[1024]{0:T(1024)} %param.7) | copy-start | bytes 12292
  80.5 17.6 %copy-start.3 = (bf16[8,576]{1,0:T(8,128)(2,1)S(1)}, bf16[8,576]{1,0:T(8,128)(2,1)}, u32[]{:S(2)}) copy-start(bf16[8,576]{1,0:T(8,128)(2,1)} %residual_ref.1) | copy-start | bytes 27652
  80.5 17.6 %copy-start.5 = (f32[576]{0:T(1024)S(1)}, f32[576]{0:T(1024)}, u32[]{:S(2)}) copy-start(f32[576]{0:T(1024)} %bias_ref.1) | copy-start | bytes 6916

commit v10 on v9

--- a/solution.py
+++ b/solution.py
@@ -42,7 +42,7 @@
     return jnp.concatenate(parts, axis=1)
 
 
-STEPS = 252.0
+STEPS, LEAST = 250.0, -124.0
 
 
 def spread_rows(rows_ref, out_ref):
@@ -63,7 +63,7 @@
         part = matmul(rows, w_ref[:, n * 256 : (n + 1) * 256], ((1,), (0,))).reshape(8, 64, 256)
         size = jnp.abs(part)
         top = (jnp.max(size, axis=1, keepdims=True) * (1 + 2.0**-7) + 1e-30).astype(bf16).astype(f32)
-        code = jnp.exp2(size * (STEPS / top) - 126.0)
+        code = jnp.exp2(size * (STEPS / top) + LEAST)
         code = jnp.where(part < 0, -code, code).astype(bf16)
         for h in range(2):
             at = pl.ds((2 * n + h) * 64, 64)
@@ -82,7 +82,7 @@
     for q in range(8):
         at = pl.ds(q * 64, 64)
         code = got_ref[:, at, :].astype(f32)
-        part = (jnp.log2(jnp.abs(code)) + 126.0) * (extra[:, 8 + q : 9 + q, :] / STEPS)
+        part = (jnp.log2(jnp.abs(code)) - LEAST) * (extra[:, 8 + q : 9 + q, :] / STEPS)
         pre = jnp.sum(jnp.where(code < 0, -part, part), axis=0) + bias_ref[q : q + 1, :]
         pre_ref[at, :] = pre
         acts = jnp.maximum(pre, 0.0).astype(bf16)

time: 164 us -> 164 us (level)
  no operation moved by 1% of the time
where the time goes in v10:
time: 164 us
  blocking collectives  153 us (93%)
  Pallas kernels  8.76 us (5%)
    all_to_all x7, blocking collectives, exchange(): return lax.all_to_all(blocks, axes, 0, 0, tiled=True)  139 us
    pallas_call x10, Pallas kernels, call(): pl.pallas_call(body, out_shape=outs, in_specs=[pl.BlockSpec(memory_space=...  8.76 us
    all_gather x1, blocking collectives, local(): err = lax.all_gather(packed, 'c', axis=0, tiled=True)  5.22 us
    all_gather x1, blocking collectives, local(): rows_all = lax.all_gather(near.reshape(256, 576), 'c', axis=0, tiled=True)  4.8 us
    all_gather x1, blocking collectives, local(): both = lax.all_gather(other, 'c', axis=0, tiled=True)  4.11 us

profile of v10, /device:TPU:1, one launch (start us, length us, event | category | flops | bytes accessed | tf_op | source)
XLA Modules:
  0.0 163.7 jit_solution(3044297107131438324)
XLA Ops:
  0.6 0.0 copy-start
  0.6 0.0 copy-start.2
  0.7 0.8 copy-done.2
  1.5 29.9 %all_to_all.35 = bf16[32,8,576]{2,1,0:T(8,128)(2,1)S(1)} all-to-all(bf16[32,8,576]{2,1,0:T(8,128)(2,1)S(1)} %bitcast.18), channel_id=1, replica_groups=mesh['x'=4,'yl'=2,'z'=8,'yh'=4,'c'=2] {'z','yh'}, dimensions={0} | all-to-all | bytes 589824 | tf_op jit(solution)/shard_map/all_to_all | solution.py:183
  31.4 0.0 copy-start.1
  31.4 4.8 %all_gather.9._.rows_ref = bf16[512,576]{1,0:T(8,128)(2,1)S(1)} all-gather(bf16[256,576]{1,0:T(8,128)(2,1)S(1)} %bitcast.21), channel_id=1, replica_groups=mesh['x'=4,'yl'=2,'z'=8,'yh'=4,'c'=2] {'c'}, dimensions={0}, use_global_device_ids=true | all-gather | bytes 884736 | tf_op jit(solution)/shard_map/all_gather | solution.py:193
  36.2 0.0 copy-done
  36.2 0.3 shard_map.93.squares_ref
  36.5 0.0 copy-done.1
  36.5 1.5 shard_map.94
  38.0 0.0 copy-start.4
  38.1 19.4 %all_to_all.36.got_ref = bf16[8,528,128]{2,1,0:T(8,128)(2,1)S(1)} all-to-all(bf16[8,528,128]{2,1,0:T(8,128)(2,1)S(1)} %shard_map.94), channel_id=1, replica_groups=mesh['x'=4,'yl'=2,'z'=8,'yh'=4,'c'=2] {'x','yl'}, dimensions={0} | all-to-all | bytes 2162688 | tf_op jit(solution)/shard_map/all_to_all | solution.py:183
  57.5 0.0 copy-done.4
  57.5 0.7 shard_map.95
  58.2 17.2 %all_to_all.37.acts_ref = bf16[8,512,128]{2,1,0:T(8,128)(2,1)S(1)} all-to-all(bf16[8,512,128]{2,1,0:T(8,128)(2,1)S(1)} %get-tuple-element.22), channel_id=1, replica_groups=mesh['x'=4,'yl'=2,'z'=8,'yh'=4,'c'=2] {'x','yl'}, dimensions={0} | all-to-all | bytes 2097152 | tf_op jit(solution)/shard_map/all_to_all | solution.py:183
  75.3 1.0 shard_map.96
  76.4 4.1 %all_gather.10.both_ref = bf16[512,576]{1,0:T(8,128)(2,1)S(1)} all-gather(bf16[256,576]{1,0:T(8,128)(2,1)S(1)} %get-tuple-element.24), channel_id=1, replica_groups=mesh['x'=4,'yl'=2,'z'=8,'yh'=4,'c'=2] {'c'}, dimensions={0}, use_global_device_ids=true | all-gather | bytes 884736 | tf_op jit(solution)/shard_map/all_gather | solution.py:207
  80.5 0.0 copy-start.3
  80.5 0.0 copy-start.5
  80.5 0.1 shard_map.97
  80.6 17.6 %all_to_all.38 = bf16[32,8,576]{2,1,0:T(8,128)(2,1)S(1)} all-to-all(bf16[32,8,576]{2,1,0:T(8,128)(2,1)S(1)} %bitcast.19), channel_id=1, replica_groups=mesh['x'=4,'yl'=2,'z'=8,'yh'=4,'c'=2] {'z','yh'}, dimensions={0} | all-to-all | bytes 589824 | tf_op jit(solution)/shard_map/all_to_all | solution.py:183
  98.1 0.0 copy-done.3
  98.1 0.0 copy-done.5
  98.1 0.3 shard_map.98
  98.4 18.8 %all_to_all.39 = bf16[32,8,640]{2,1,0:T(8,128)(2,1)S(1)} all-to-all(bf16[32,8,640]{2,1,0:T(8,128)(2,1)S(1)} %bitcast.17), channel_id=1, replica_groups=mesh['x'=4,'yl'=2,'z'=8,'yh'=4,'c'=2] {'z','yh'}, dimensions={0} | all-to-all | bytes 655360 | tf_op jit(solution)/shard_map/all_to_all | solution.py:183
  117.2 5.2 %all_gather.11.err_ref = bf16[512,640]{1,0:T(8,128)(2,1)S(1)} all-gather(bf16[256,640]{1,0:T(8,128)(2,1)S(1)} %bitcast.22), channel_id=1, replica_groups=mesh['x'=4,'yl'=2,'z'=8,'yh'=4,'c'=2] {'c'}, dimensions={0}, use_global_device_ids=true | all-gather | bytes 983040 | tf_op jit(solution)/shard_map/all_gather | solution.py:219
  122.4 1.0 shard_map.99
  123.4 19.2 %all_to_all.40.got_ref = bf16[8,528,128]{2,1,0:T(8,128)(2,1)S(1)} all-to-all(bf16[8,528,128]{2,1,0:T(8,128)(2,1)S(1)} %shard_map.99), channel_id=1, replica_groups=mesh['x'=4,'yl'=2,'z'=8,'yh'=4,'c'=2] {'x','yl'}, dimensions={0} | all-to-all | bytes 2162688 | tf_op jit(solution)/shard_map/all_to_all | solution.py:183
  142.6 0.8 shard_map.100
  143.4 17.2 %all_to_all.41.d_pre_ref = bf16[8,512,128]{2,1,0:T(8,128)(2,1)S(1)} all-to-all(bf16[8,512,128]{2,1,0:T(8,128)(2,1)S(1)} %get-tuple-element.31), channel_id=1, replica_groups=mesh['x'=4,'yl'=2,'z'=8,'yh'=4,'c'=2] {'x','yl'}, dimensions={0} | all-to-all | bytes 2097152 | tf_op jit(solution)/shard_map/all_to_all | solution.py:183
  160.6 3.1 %shard_map.101 = (bf16[576,1024]{1,0:T(8,128)(2,1)}, bf16[576]{0:T(1024)(128)(2,1)}, bf16[576,1024]{1,0:T(8,128)(2,1)}, bf16[8,128]{1,0:T(8,128)(2,1)}) custom-call(bf16[8,512,128]{2,1,0:T(8,128)(2,1)S(1)} %all_to_all.37.acts_ref, bf16[512,640]{1,0:T(8,128)(2,1)S(1)} %all_gather.11.err_ref, bf16[576,1024]{1,0:T(8,128)(2,1)S(1)} %bitcast.15, ...), custom_call_target="tpu_custom_call" | custom-call | flops 1207959552 | bytes 6888576 | tf_op jit(solution)/shard_map/pallas_call | solution.py:23
  (1 shorter events, 0.0 us)
Async XLA Ops:
  0.6 35.6 %copy-start = (bf16[1024,576]{0,1:T(8,128)(2,1)S(1)}, bf16[1024,576]{0,1:T(8,128)(2,1)}, u32[]{:S(2)}) copy-start(bf16[1024,576]{0,1:T(8,128)(2,1)} %param.8) | copy-start | bytes 3538948
  0.6 0.8 copy-start.2
  31.4 5.1 %copy-start.1 = (bf16[576,1024]{1,0:T(8,128)(2,1)S(1)}, bf16[576,1024]{1,0:T(8,128)(2,1)}, u32[]{:S(2)}) copy-start(bf16[576,1024]{1,0:T(8,128)(2,1)} %w_ref.1) | copy-start | bytes 3538948
  38.0 19.4 %copy-start.4 = (f32[1024]{0:T(1024)S(1)}, f32[1024]{0:T(1024)}, u32[]{:S(2)}) copy-start(f32[1024]{0:T(1024)} %param.7) | copy-start | bytes 12292
  80.5 17.6 %copy-start.3 = (bf16[8,576]{1,0:T(8,128)(2,1)S(1)}, bf16[8,576]{1,0:T(8,128)(2,1)}, u32[]{:S(2)}) copy-start(bf16[8,576]{1,0:T(8,128)(2,1)} %residual_ref.1) | copy-start | bytes 27652
  80.5 17.6 %copy-start.5 = (f32[576]{0:T(1024)S(1)}, f32[576]{0:T(1024)}, u32[]{:S(2)}) copy-start(f32[576]{0:T(1024)} %bias_ref.1) | copy-start | bytes 6916

commit v11 on v10

--- a/solution.py
+++ b/solution.py
@@ -156,7 +156,7 @@
         out_ref[:, at] = (outer + scale * w_ref[:, at].astype(f32)).astype(bf16)
 
 
-def encoder_gradient(rows_ref, d_pre_ref, out_ref, bias_ref):
+def encoder_gradient(rows_ref, d_pre_ref, out_ref, bias_ref, halves):
     rows = rows_ref[...]
     sums = []
     for n in range(4):
@@ -164,6 +164,8 @@
         sums += [jnp.sum(part.astype(f32), axis=0, keepdims=True) for part in pair]
         d_pre = jnp.concatenate(pair, axis=1)
         out_ref[:, n * 256 : (n + 1) * 256] = matmul(rows, d_pre, ((0,), (0,))).astype(bf16)
+        if n % 2:
+            halves[n // 2].start()
     bias_ref[...] = jnp.concatenate(sums, axis=0).astype(bf16)
 
 
@@ -172,11 +174,12 @@
     decoder_gradient(acts_ref, err_ref, w_ref, norms_ref, dec_ref, dec_bias)
     dec_out = pltpu.make_async_copy(dec_ref, dec_far, dec_sem)
     dec_out.start()
-    encoder_gradient(rows_ref, d_pre_ref, enc_ref, enc_bias)
-    enc_out = pltpu.make_async_copy(enc_ref, enc_far, enc_sem)
-    enc_out.start()
+    halves = [(slice(None), pl.ds(h * 512, 512)) for h in range(2)]
+    enc_out = [pltpu.make_async_copy(enc_ref.at[at], enc_far.at[at], enc_sem.at[h]) for h, at in enumerate(halves)]
+    encoder_gradient(rows_ref, d_pre_ref, enc_ref, enc_bias, enc_out)
     dec_out.wait()
-    enc_out.wait()
+    for copy in enc_out:
+        copy.wait()
 
 
 def exchange(blocks, axes):
@@ -233,7 +236,7 @@
         exchange(d_pre, LAYER),
         flops=2 * work,
         far=(0, 2),
-        scratch=(wide, wide, pltpu.SemaphoreType.DMA, pltpu.SemaphoreType.DMA),
+        scratch=(wide, wide, pltpu.SemaphoreType.DMA, pltpu.SemaphoreType.DMA((2,))),
     )
     return (
         grad_enc,

time: 164 us -> 164 us (level)
  no operation moved by 1% of the time
where the time goes in v11:
time: 164 us; the launch traced here: 163 us
  blocking collectives  153 us (93%)
  Pallas kernels  8.53 us (5%)
    all_to_all x7, blocking collectives, exchange(): return lax.all_to_all(blocks, axes, 0, 0, tiled=True)  139 us
    pallas_call x10, Pallas kernels, call(): pl.pallas_call(body, out_shape=outs, in_specs=[pl.BlockSpec(memory_space=...  8.53 us
    all_gather x1, blocking collectives, local(): err = lax.all_gather(packed, 'c', axis=0, tiled=True)  5.22 us
    all_gather x1, blocking collectives, local(): rows_all = lax.all_gather(near.reshape(256, 576), 'c', axis=0, tiled=True)  4.8 us
    all_gather x1, blocking collectives, local(): both = lax.all_gather(other, 'c', axis=0, tiled=True)  4.11 us

profile of v11, /device:TPU:1, one launch (start us, length us, event | category | flops | bytes accessed | tf_op | source)
XLA Modules:
  0.0 163.4 jit_solution(18245761705026128072)
XLA Ops:
  0.6 0.0 copy-start
  0.6 0.0 copy-start.2
  0.7 0.8 copy-done.2
  1.5 29.9 %all_to_all.35 = bf16[32,8,576]{2,1,0:T(8,128)(2,1)S(1)} all-to-all(bf16[32,8,576]{2,1,0:T(8,128)(2,1)S(1)} %bitcast.18), channel_id=1, replica_groups=mesh['x'=4,'yl'=2,'z'=8,'yh'=4,'c'=2] {'z','yh'}, dimensions={0} | all-to-all | bytes 589824 | tf_op jit(solution)/shard_map/all_to_all | solution.py:186
  31.4 0.0 copy-start.1
  31.4 4.8 %all_gather.9._.rows_ref = bf16[512,576]{1,0:T(8,128)(2,1)S(1)} all-gather(bf16[256,576]{1,0:T(8,128)(2,1)S(1)} %bitcast.21), channel_id=1, replica_groups=mesh['x'=4,'yl'=2,'z'=8,'yh'=4,'c'=2] {'c'}, dimensions={0}, use_global_device_ids=true | all-gather | bytes 884736 | tf_op jit(solution)/shard_map/all_gather | solution.py:196
  36.2 0.0 copy-done
  36.2 0.3 shard_map.93.squares_ref
  36.5 0.0 copy-done.1
  36.5 1.5 shard_map.94
  38.0 0.0 copy-start.4
  38.1 19.4 %all_to_all.36.got_ref = bf16[8,528,128]{2,1,0:T(8,128)(2,1)S(1)} all-to-all(bf16[8,528,128]{2,1,0:T(8,128)(2,1)S(1)} %shard_map.94), channel_id=1, replica_groups=mesh['x'=4,'yl'=2,'z'=8,'yh'=4,'c'=2] {'x','yl'}, dimensions={0} | all-to-all | bytes 2162688 | tf_op jit(solution)/shard_map/all_to_all | solution.py:186
  57.5 0.0 copy-done.4
  57.5 0.7 shard_map.95
  58.2 17.2 %all_to_all.37.acts_ref = bf16[8,512,128]{2,1,0:T(8,128)(2,1)S(1)} all-to-all(bf16[8,512,128]{2,1,0:T(8,128)(2,1)S(1)} %get-tuple-element.22), channel_id=1, replica_groups=mesh['x'=4,'yl'=2,'z'=8,'yh'=4,'c'=2] {'x','yl'}, dimensions={0} | all-to-all | bytes 2097152 | tf_op jit(solution)/shard_map/all_to_all | solution.py:186
  75.3 1.0 shard_map.96
  76.4 4.1 %all_gather.10.both_ref = bf16[512,576]{1,0:T(8,128)(2,1)S(1)} all-gather(bf16[256,576]{1,0:T(8,128)(2,1)S(1)} %get-tuple-element.24), channel_id=1, replica_groups=mesh['x'=4,'yl'=2,'z'=8,'yh'=4,'c'=2] {'c'}, dimensions={0}, use_global_device_ids=true | all-gather | bytes 884736 | tf_op jit(solution)/shard_map/all_gather | solution.py:210
  80.5 0.0 copy-start.3
  80.5 0.0 copy-start.5
  80.5 0.1 shard_map.97
  80.6 17.6 %all_to_all.38 = bf16[32,8,576]{2,1,0:T(8,128)(2,1)S(1)} all-to-all(bf16[32,8,576]{2,1,0:T(8,128)(2,1)S(1)} %bitcast.19), channel_id=1, replica_groups=mesh['x'=4,'yl'=2,'z'=8,'yh'=4,'c'=2] {'z','yh'}, dimensions={0} | all-to-all | bytes 589824 | tf_op jit(solution)/shard_map/all_to_all | solution.py:186
  98.1 0.0 copy-done.3
  98.1 0.0 copy-done.5
  98.1 0.3 shard_map.98
  98.4 18.8 %all_to_all.39 = bf16[32,8,640]{2,1,0:T(8,128)(2,1)S(1)} all-to-all(bf16[32,8,640]{2,1,0:T(8,128)(2,1)S(1)} %bitcast.17), channel_id=1, replica_groups=mesh['x'=4,'yl'=2,'z'=8,'yh'=4,'c'=2] {'z','yh'}, dimensions={0} | all-to-all | bytes 655360 | tf_op jit(solution)/shard_map/all_to_all | solution.py:186
  117.2 5.2 %all_gather.11.err_ref = bf16[512,640]{1,0:T(8,128)(2,1)S(1)} all-gather(bf16[256,640]{1,0:T(8,128)(2,1)S(1)} %bitcast.22), channel_id=1, replica_groups=mesh['x'=4,'yl'=2,'z'=8,'yh'=4,'c'=2] {'c'}, dimensions={0}, use_global_device_ids=true | all-gather | bytes 983040 | tf_op jit(solution)/shard_map/all_gather | solution.py:222
  122.4 1.0 shard_map.99
  123.4 19.2 %all_to_all.40.got_ref = bf16[8,528,128]{2,1,0:T(8,128)(2,1)S(1)} all-to-all(bf16[8,528,128]{2,1,0:T(8,128)(2,1)S(1)} %shard_map.99), channel_id=1, replica_groups=mesh['x'=4,'yl'=2,'z'=8,'yh'=4,'c'=2] {'x','yl'}, dimensions={0} | all-to-all | bytes 2162688 | tf_op jit(solution)/shard_map/all_to_all | solution.py:186
  142.6 0.8 shard_map.100
  143.4 17.2 %all_to_all.41.d_pre_ref = bf16[8,512,128]{2,1,0:T(8,128)(2,1)S(1)} all-to-all(bf16[8,512,128]{2,1,0:T(8,128)(2,1)S(1)} %get-tuple-element.31), channel_id=1, replica_groups=mesh['x'=4,'yl'=2,'z'=8,'yh'=4,'c'=2] {'x','yl'}, dimensions={0} | all-to-all | bytes 2097152 | tf_op jit(solution)/shard_map/all_to_all | solution.py:186
  160.6 2.9 %shard_map.101 = (bf16[576,1024]{1,0:T(8,128)(2,1)}, bf16[576]{0:T(1024)(128)(2,1)}, bf16[576,1024]{1,0:T(8,128)(2,1)}, bf16[8,128]{1,0:T(8,128)(2,1)}) custom-call(bf16[8,512,128]{2,1,0:T(8,128)(2,1)S(1)} %all_to_all.37.acts_ref, bf16[512,640]{1,0:T(8,128)(2,1)S(1)} %all_gather.11.err_ref, bf16[576,1024]{1,0:T(8,128)(2,1)S(1)} %bitcast.15, ...), custom_call_target="tpu_custom_call" | custom-call | flops 1207959552 | bytes 6888576 | tf_op jit(solution)/shard_map/pallas_call | solution.py:23
  (1 shorter events, 0.0 us)
Async XLA Ops:
  0.6 35.6 %copy-start = (bf16[1024,576]{0,1:T(8,128)(2,1)S(1)}, bf16[1024,576]{0,1:T(8,128)(2,1)}, u32[]{:S(2)}) copy-start(bf16[1024,576]{0,1:T(8,128)(2,1)} %param.8) | copy-start | bytes 3538948
  0.6 0.8 copy-start.2
  31.4 5.1 %copy-start.1 = (bf16[576,1024]{1,0:T(8,128)(2,1)S(1)}, bf16[576,1024]{1,0:T(8,128)(2,1)}, u32[]{:S(2)}) copy-start(bf16[576,1024]{1,0:T(8,128)(2,1)} %w_ref.1) | copy-start | bytes 3538948
  38.0 19.4 %copy-start.4 = (f32[1024]{0:T(1024)S(1)}, f32[1024]{0:T(1024)}, u32[]{:S(2)}) copy-start(f32[1024]{0:T(1024)} %param.7) | copy-start | bytes 12292
  80.5 17.6 %copy-start.3 = (bf16[8,576]{1,0:T(8,128)(2,1)S(1)}, bf16[8,576]{1,0:T(8,128)(2,1)}, u32[]{:S(2)}) copy-start(bf16[8,576]{1,0:T(8,128)(2,1)} %residual_ref.1) | copy-start | bytes 27652
  80.5 17.6 %copy-start.5 = (f32[576]{0:T(1024)S(1)}, f32[576]{0:T(1024)}, u32[]{:S(2)}) copy-start(f32[576]{0:T(1024)} %bias_ref.1) | copy-start | bytes 6916
